TPU v7x, 32 devices: a whole 2x2x4 slice. The times are simulated.
32 devices in a mesh: node: 8 (over z, x), head: 4 (over y, core).
Axes of the slice: x: 2, y: 2, z: 4, core: 2. Of those that a mesh axis runs over, the one named last changes fastest.
Arguments:
- queries: bfloat16 [768, 8192], P('head', 'node'), may hold values from -9 to 9
- key_rows: bfloat16 [768, 8192], P('head', 'node'), may hold values from -9 to 9
- value_rows: bfloat16 [768, 8192], P('head', 'node'), may hold values from -6 to 6
- out_weight: bfloat16 [768, 768], P('head'), may hold values from -0.21875 to 0.21875
- cotangent: bfloat16 [768, 8192], P('head', 'node'), may hold values from -12 to 12
- cluster_ids: int32 [8192], P('node'), may hold values from 0 to 15, as said below
- members: int32 [16, 1024], P('node'), may hold values from 0 to 8191, as said below
- counts: int32 [16], P('node'), may hold values from 0 to 1024, as said below
Outputs:
- output: bfloat16 [768, 8192], P('head', 'node')
- grad_queries: bfloat16 [768, 8192], P('head', 'node')
- grad_keys: bfloat16 [768, 8192], P('head', 'node')
- grad_values: bfloat16 [768, 8192], P('head', 'node')
Inputs may be any that keep to these rules, and one draw needn't show every extreme that they name: Node i is listed exactly once, in cluster cluster_ids[i]; cluster c is owned by index c // 2 of node. Each index of node has 256 of its nodes in clusters of a quarter of the owners (one of them takes 256 from every index), 128 in clusters of half of the owners, and none in the rest. Row c lists the members of cluster c in its first counts[c] entries; the other entries are arbitrary node ids. `counts`: each owner's members fill its clusters 1024 at a time: all of its clusters but at most one are full or empty.
All inputs are finite; a program needn't handle non-finite values.
Results may differ from a plain program's by a relative error of at most 0.012.
The roundings to bfloat16 on the way count: a program that leaves them out, or rounds other values in their place, can miss the bound.
Values may be sent and summed in bfloat16 or wider, within the bound.
No kernel may reach another device: no remote copies, remote signals or barrier semaphores. Data moves between devices by JAX's collectives and lax.ppermute only.
A program may use at most 128 MiB of HBM per device.

v0:
```python
import math

import jax
import jax.numpy as jnp
from jax import lax
from jax.sharding import PartitionSpec as P

HEAD_DIM = 64
CLUSTER = 1024


masked_score = -1e30


def shortened(value):

    def short(part):
        return part.astype(jnp.bfloat16) if part.dtype == jnp.float32 else part

    return jax.tree.map(short, value)


def block_weights(query_block, key_head, key_valid, row_valid, scale):
    scores = (
        lax.dot_general(
            query_block, key_head, (((1,), (1,)), ((), ())), preferred_element_type=jnp.float32
        )
        * scale
    )
    scores = jnp.where(key_valid[None, :], scores, masked_score)
    raised = jnp.exp(scores - jnp.max(scores, axis=1, keepdims=True))
    weights = raised / jnp.sum(raised, axis=1, keepdims=True)
    weights = jnp.where(row_valid[:, None], weights, 0.0)
    return lax.optimization_barrier(weights.astype(jnp.bfloat16))


def block_mix(weights, value_head):
    mixed = jnp.dot(weights, value_head, preferred_element_type=jnp.float32).astype(jnp.bfloat16)
    return lax.optimization_barrier(mixed)


def block_grads(weights, query_block, key_head, value_head, grad_block, mixed_block, scale):
    dweights = lax.dot_general(
        grad_block, value_head, (((1,), (1,)), ((), ())), preferred_element_type=jnp.float32
    )
    delta = jnp.sum(grad_block.astype(jnp.float32) * mixed_block.astype(jnp.float32), axis=1)
    dscores = (weights.astype(jnp.float32) * (dweights - delta[:, None])).astype(jnp.bfloat16)
    grad_query = (jnp.dot(dscores, key_head, preferred_element_type=jnp.float32) * scale).astype(
        jnp.bfloat16
    )
    key_term = lax.dot_general(
        dscores, query_block, (((0,), (0,)), ((), ())), preferred_element_type=jnp.float32
    )
    value_term = lax.dot_general(
        weights, grad_block, (((0,), (0,)), ((), ())), preferred_element_type=jnp.float32
    )
    return (grad_query, key_term, value_term)


def head_pass(query_head, key_head, value_head, grad_head, mixed_head, row_valid, block, scale):
    rows, depth = query_head.shape
    parts = rows // block

    def split_rows(array):
        if array is None:
            return None
        return array.reshape((parts, block) + array.shape[1:])

    zero = jnp.zeros((rows, depth), jnp.float32)

    def visit(carry, pieces):
        query_block, valid_block, grad_block, mixed_block = pieces
        weights = block_weights(query_block, key_head, row_valid, valid_block, scale)
        if mixed_block is None:
            mixed_block = block_mix(weights, value_head)
        if grad_block is None:
            return (carry, (mixed_block, None))
        grad_query, key_term, value_term = block_grads(
            weights, query_block, key_head, value_head, grad_block, mixed_block, scale
        )
        return ((carry[0] + key_term, carry[1] + value_term), (mixed_block, grad_query))

    pieces = (
        split_rows(query_head),
        split_rows(row_valid),
        split_rows(grad_head),
        split_rows(mixed_head),
    )
    carry, results = lax.scan(visit, (zero, zero), pieces)
    mixed = results[0].reshape(rows, depth)
    if grad_head is None:
        return (mixed, None, None, None)
    grad_query = results[1].reshape(rows, depth)
    return (
        mixed,
        grad_query,
        (carry[0] * scale).astype(jnp.bfloat16),
        carry[1].astype(jnp.bfloat16),
    )


def head_columns(array, head):
    if array is None:
        return None
    return array[:, head * HEAD_DIM : (head + 1) * HEAD_DIM]


def run_cluster(query_part, key_part, value_part, grad_part, mixed_part, count, keep, block, scale):

    def work():
        row_valid = jnp.arange(query_part.shape[0]) < count
        groups = [[], [], [], []]
        for head in range(query_part.shape[1] // HEAD_DIM):
            results = head_pass(
                head_columns(query_part, head),
                head_columns(key_part, head),
                head_columns(value_part, head),
                head_columns(grad_part, head),
                head_columns(mixed_part, head),
                row_valid,
                block,
                scale,
            )
            for index in range(4):
                groups[index].append(results[index])
        return jnp.concatenate([jnp.concatenate(groups[index], axis=1) for index in keep], axis=1)

    def spare():
        return jnp.zeros((query_part.shape[0], len(keep) * query_part.shape[1]), jnp.bfloat16)

    return lax.cond(count > 0, work, spare)


def inverse_index(targets, slot_total):
    hits = jnp.arange(slot_total, dtype=jnp.int32)[:, None] == targets[None, :]
    present = jnp.any(hits, axis=1)
    source = jnp.sum(
        jnp.where(hits, jnp.arange(targets.shape[0], dtype=jnp.int32)[None, :], 0), axis=1
    )
    return (source, present)


def place_rows(rows, source, present):
    return jnp.where(present[:, None], rows[source], jnp.zeros((), rows.dtype))


def dispatch_rows(rows, send_source, send_present, node_count):
    return place_rows(rows, send_source, send_present).reshape(node_count, -1)


def collect_rows(arrived, owner_slot, slot_total, clusters):
    flat = arrived.reshape(slot_total, -1)[owner_slot]
    return flat.reshape(clusters, -1, flat.shape[1])


def return_rows(results, back_source, back_present, node_count):
    flat = results.reshape(-1, results.shape[2])
    return place_rows(flat, back_source, back_present).reshape(node_count, -1)


def take_home(arrived, home_slot, slot_total):
    return arrived.reshape(slot_total, -1)[home_slot]


def body(queries, key_rows, value_rows, out_weight, cotangent, cluster_ids, members, counts):
    node_count = lax.axis_size("node")
    width, node_rows = queries.shape
    clusters = members.shape[0]
    slot_depth = 2 * node_rows // node_count
    slot_total = node_count * slot_depth
    scale = 1.0 / math.sqrt(HEAD_DIM)
    block = min(512, CLUSTER)
    query_nodes = queries.T
    key_nodes = key_rows.T
    value_nodes = value_rows.T
    owner = cluster_ids // clusters
    local = jnp.arange(node_rows, dtype=jnp.int32)
    same_owner = owner[:, None] == owner[None, :]
    before = local[None, :] < local[:, None]
    rank_home = jnp.sum(jnp.logical_and(same_owner, before), axis=1)
    home_slot = owner * slot_depth + rank_home
    send_source, send_present = inverse_index(home_slot, slot_total)
    member_ids = members.reshape(-1)
    listed = (jnp.arange(CLUSTER, dtype=jnp.int32)[None, :] < counts[:, None]).reshape(-1)
    source_dev = member_ids // node_rows
    same_source = source_dev[:, None] == source_dev[None, :]
    smaller = member_ids[None, :] < member_ids[:, None]
    counted = jnp.logical_and(jnp.logical_and(same_source, smaller), listed[None, :])
    ranking = jnp.sum(counted, axis=1)
    owner_slot = jnp.where(listed, source_dev * slot_depth + ranking, 0)
    drop_slot = jnp.where(listed, owner_slot, slot_total)
    back_source, back_present = inverse_index(drop_slot, slot_total)
    rows = jnp.concatenate([query_nodes, key_nodes, value_nodes], axis=1)
    arrived = lax.all_to_all(
        dispatch_rows(rows, send_source, send_present, node_count),
        "node",
        split_axis=0,
        concat_axis=0,
        tiled=True,
    )
    cluster_rows = collect_rows(arrived, owner_slot, slot_total, clusters)

    def forward_cluster(pair):
        held, count = pair
        return run_cluster(
            held[:, :width],
            held[:, width : 2 * width],
            held[:, 2 * width :],
            None,
            None,
            count,
            (0,),
            block,
            scale,
        )

    mixed = lax.map(forward_cluster, (cluster_rows, counts))
    back = lax.all_to_all(
        shortened(return_rows(mixed, back_source, back_present, node_count)),
        "node",
        split_axis=0,
        concat_axis=0,
        tiled=True,
    )
    attention = take_home(back, home_slot, slot_total)
    summed = lax.dot_general(
        lax.all_gather(cotangent, "head", axis=0, tiled=True),
        out_weight,
        (((0,), (1,)), ((), ())),
        preferred_element_type=jnp.float32,
    )
    grad_in = summed.astype(jnp.bfloat16)
    arrived_grad = lax.all_to_all(
        dispatch_rows(grad_in, send_source, send_present, node_count),
        "node",
        split_axis=0,
        concat_axis=0,
        tiled=True,
    )
    cluster_grads = collect_rows(arrived_grad, owner_slot, slot_total, clusters)

    def backward_cluster(group):
        held, grad_part, mixed_part, count = group
        return run_cluster(
            held[:, :width],
            held[:, width : 2 * width],
            held[:, 2 * width :],
            grad_part,
            mixed_part,
            count,
            (1, 2, 3),
            block,
            scale,
        )

    results = lax.map(backward_cluster, (cluster_rows, cluster_grads, mixed, counts))
    back_grads = lax.all_to_all(
        shortened(return_rows(results, back_source, back_present, node_count)),
        "node",
        split_axis=0,
        concat_axis=0,
        tiled=True,
    )
    grads = take_home(back_grads, home_slot, slot_total)
    full_weight = lax.all_gather(out_weight, "head", axis=0, tiled=True)
    mine = lax.dynamic_slice_in_dim(full_weight, lax.axis_index("head") * width, width, 1)
    piece = lax.all_gather(shortened(attention.T), "head", axis=0, tiled=True)
    rows_used = lax.slice_in_dim(mine, 0, piece.shape[0], axis=0)
    summed = lax.dot_general(
        rows_used, piece, (((0,), (0,)), ((), ())), preferred_element_type=jnp.float32
    )
    output = summed.astype(jnp.bfloat16)
    return (output, grads[:, :width].T, grads[:, width : 2 * width].T, grads[:, 2 * width :].T)


def solution(mesh):
    placed = (
        P("head", "node"),
        P("head", "node"),
        P("head", "node"),
        P("head", None),
        P("head", "node"),
        P("node"),
        P("node", None),
        P("node"),
    )
    return jax.shard_map(
        body,
        mesh=mesh,
        in_specs=placed,
        out_specs=(P("head", "node"), P("head", "node"), P("head", "node"), P("head", "node")),
        check_vma=False,
    )
```

profile of v0, /device:TPU:0, one launch (start us, length us, event | category | flops | bytes accessed | tf_op | source)
XLA Modules:
  0.0 541.9 jit_solution(2734272637832812277)
XLA Ops:
  13.1 9.5 %gather_fusion = bf16[2048,576]{1,0:T(8,128)(2,1)} fusion(bf16[1024,576]{1,0:T(8,128)(2,1)S(1)} %pad_maximum_fusion, s32[2048]{0:T(1024)S(1)} %broadcast_clamp_fusion.2), kind=kCustom, calls=%fused_computation | custom fusion | bytes 4726784 | tf_op jit(solution)/shard_map/gather | solution.py:144
  22.6 4.7 reshape.609
  31.4 2.7 reshape.607
  40.1 7.9 %gather_fusion.4 = bf16[2048,192]{1,0:T(8,128)(2,1)S(1)} fusion(bf16[1024,192]{1,0:T(8,128)(2,1)S(1)} %copy.71, s32[2048]{0:T(1024)S(1)} %broadcast_clamp_fusion.2), kind=kCustom, calls=%fused_computation.4 | custom fusion | bytes 1581056 | tf_op jit(solution)/shard_map/gather | solution.py:144
  50.7 3.1 reduce.18
  53.8 2.7 reshape.623
  56.5 7.3 %all-to-all-start.2 = ((bf16[8,2,24576]{2,1,0:T(2,128)(2,1)}), bf16[8,2,24576]{2,1,0:T(2,128)(2,1)}, u32[]{:S(2)}, u32[]{:S(2)}) async-start(bf16[8,2,24576]{2,1,0:T(2,128)(2,1)} %reshape.623), calls=%async_computation.2 | async-start | bytes 1572864 | tf_op jit(solution)/shard_map/all_to_all | solution.py:233
  63.7 2.6 broadcast_select_fusion.1
  66.3 3.1 reduce.16
  69.4 3.5 reshape.619
  72.9 11.1 %all-to-all-done.2 = bf16[8,2,24576]{2,1,0:T(2,128)(2,1)} async-done(((bf16[8,2,24576]{2,1,0:T(2,128)(2,1)}), bf16[8,2,24576]{2,1,0:T(2,128)(2,1)}, u32[]{:S(2)}, u32[]{:S(2)}) %all-to-all-start.2) | async-done | bytes 786464 | tf_op jit(solution)/shard_map/all_to_all | solution.py:233
  84.0 4.4 all-to-all-start
  89.4 4.3 convert_reduce_fusion
  96.3 2.7 reshape.613
  106.1 4.3 reshape.624
  110.4 4.8 reduce.8
  116.4 9.0 %gather_fusion.5 = bf16[2048,192]{1,0:T(8,128)(2,1)} fusion(bf16[2048,192]{1,0:T(8,128)(2,1)S(1)} %reshape.521, s32[2048]{0:T(1024)S(1)} %broadcast_clamp_fusion.1), kind=kCustom, calls=%fused_computation.5 | custom fusion | bytes 1581056 | tf_op jit(solution)/shard_map/gather | solution.py:152
  125.4 16.4 %all-to-all-done = bf16[8,2,73728]{2,1,0:T(2,128)(2,1)} async-done(((bf16[8,2,73728]{2,1,0:T(2,128)(2,1)}), bf16[8,2,73728]{2,1,0:T(2,128)(2,1)}, u32[]{:S(2)}, u32[]{:S(2)}) %all-to-all-start) | async-done | bytes 2359328 | tf_op jit(solution)/shard_map/all_to_all | solution.py:194
  141.8 7.0 %reshape.620 = bf16[8,1,147456]{2,1,0:T(2,128)(2,1)} reshape(bf16[8,2,73728]{2,1,0:T(2,128)(2,1)} %all-to-all-done) | data formatting | bytes 4718592
  148.8 14.8 %reduce.6 = bf16[8,147456]{1,0:T(8,128)(2,1)S(1)} reduce(bf16[8,1,147456]{2,1,0:T(2,128)(2,1)} %reshape.620, bf16[]{:T(256)} %constant.249), dimensions={1}, to_apply=%all_to_all.16.reduce_sub_computation | reduce | bytes 4718594 | tf_op jit(solution)/shard_map/all_to_all | solution.py:194
  166.1 4.3 reshape.516
  170.4 9.3 %gather_fusion.1 = bf16[2048,576]{1,0:T(8,128)(2,1)} fusion(bf16[2048,576]{1,0:T(8,128)(2,1)S(1)} %reshape.516, s32[2048]{0:T(1024)S(1)} %broadcast_clamp_fusion.1), kind=kCustom, calls=%fused_computation.1 | custom fusion | bytes 4726784 | tf_op jit(solution)/shard_map/gather | solution.py:152
  179.7 46.6 %while.176 = (s32[]{:T(128)}, bf16[2,1024,192]{2,1,0:T(8,128)(2,1)}, s32[2]{0:T(128)S(1)}, bf16[2,1024,576]{2,1,0:T(8,128)(2,1)}, s32[]{:T(128)}, /*index=5*/s32[]{:T(128)}) while((s32[]{:T(128)}, bf16[2,1024,192]{2,1,0:T(8,128)(2,1)}, s32[2]{0:T(128)S(1)}, bf16[2,1024,576]{2,1,0:T(8,128)(2,1)}, s32[]{:T(128)}, /*index=5*/s32[]{:T(128)}) %tuple.266), condition=%wide.region_20.21_spmd, body=%wide.region_5.20_spmd.sunk | while | flops 424381440 | bytes 41402576 | solution.py:217
  181.2 20.8 %conditional.4 = (bf16[1,1024,192]{2,1,0:T(8,128)(2,1)S(1)}) conditional(s32[]{:T(128)} %convert_element_type.244, () %tuple.198, (bf16[2,1024,576]{2,1,0:T(8,128)(2,1)}, s32[]{:T(128)}, s32[]{:T(128)}) %tuple.199), branch_computations={%region_6.6_spmd, %region_7.19_spmd} | conditional | flops 424381440 | bytes 34062364 | solution.py:131
  183.9 5.7 %while.170 = (s32[]{:T(128)}, bf16[2,512,64]{1,2,0:T(8,128)(2,1)S(1)}, pred[2,512]{1,0:T(4,128)(4,1)S(1)}, bf16[2,512,64]{2,1,0:T(8,128)(2,1)S(1)}, bf16[1024,64...) while((s32[]{:T(128)}, bf16[2,512,64]{1,2,0:T(8,128)(2,1)S(1)}, ...), condition=%wide.region_11.10_spmd.clone, body=%wide.region_8.9_spmd.clone.sunk | while | flops 141066240 | bytes 9125477 | solution.py:89
  189.9 5.7 %while.171 = (s32[]{:T(128)}, bf16[2,512,64]{1,2,0:T(8,128)(2,1)S(1)}, pred[2,512]{1,0:T(4,128)(4,1)S(1)}, bf16[2,512,64]{2,1,0:T(8,128)(2,1)S(1)}, bf16[1024,64...) while((s32[]{:T(128)}, bf16[2,512,64]{1,2,0:T(8,128)(2,1)S(1)}, ...), condition=%wide.region_15.14_spmd.clone, body=%wide.region_12.13_spmd.clone.sunk | while | flops 141066240 | bytes 9125477 | solution.py:89
  195.8 5.7 %while.172 = (s32[]{:T(128)}, bf16[2,512,64]{1,2,0:T(8,128)(2,1)S(1)}, pred[2,512]{1,0:T(4,128)(4,1)S(1)}, bf16[2,512,64]{2,1,0:T(8,128)(2,1)S(1)}, bf16[1024,64...) while((s32[]{:T(128)}, bf16[2,512,64]{1,2,0:T(8,128)(2,1)S(1)}, ...), condition=%wide.region_19.18_spmd.clone, body=%wide.region_16.17_spmd.clone.sunk | while | flops 141066240 | bytes 9125477 | solution.py:89
  204.4 20.8 %conditional.4 = (bf16[1,1024,192]{2,1,0:T(8,128)(2,1)S(1)}) conditional(s32[]{:T(128)} %convert_element_type.244, () %tuple.198, (bf16[2,1024,576]{2,1,0:T(8,128)(2,1)}, s32[]{:T(128)}, s32[]{:T(128)}) %tuple.199), branch_computations={%region_6.6_spmd, %region_7.19_spmd} | conditional | flops 424381440 | bytes 34062364 | solution.py:131
  207.1 5.7 %while.170 = (s32[]{:T(128)}, bf16[2,512,64]{1,2,0:T(8,128)(2,1)S(1)}, pred[2,512]{1,0:T(4,128)(4,1)S(1)}, bf16[2,512,64]{2,1,0:T(8,128)(2,1)S(1)}, bf16[1024,64...) while((s32[]{:T(128)}, bf16[2,512,64]{1,2,0:T(8,128)(2,1)S(1)}, ...), condition=%wide.region_11.10_spmd.clone, body=%wide.region_8.9_spmd.clone.sunk | while | flops 141066240 | bytes 9125477 | solution.py:89
  213.1 5.7 %while.171 = (s32[]{:T(128)}, bf16[2,512,64]{1,2,0:T(8,128)(2,1)S(1)}, pred[2,512]{1,0:T(4,128)(4,1)S(1)}, bf16[2,512,64]{2,1,0:T(8,128)(2,1)S(1)}, bf16[1024,64...) while((s32[]{:T(128)}, bf16[2,512,64]{1,2,0:T(8,128)(2,1)S(1)}, ...), condition=%wide.region_15.14_spmd.clone, body=%wide.region_12.13_spmd.clone.sunk | while | flops 141066240 | bytes 9125477 | solution.py:89
  219.0 5.7 %while.172 = (s32[]{:T(128)}, bf16[2,512,64]{1,2,0:T(8,128)(2,1)S(1)}, pred[2,512]{1,0:T(4,128)(4,1)S(1)}, bf16[2,512,64]{2,1,0:T(8,128)(2,1)S(1)}, bf16[1024,64...) while((s32[]{:T(128)}, bf16[2,512,64]{1,2,0:T(8,128)(2,1)S(1)}, ...), condition=%wide.region_19.18_spmd.clone, body=%wide.region_16.17_spmd.clone.sunk | while | flops 141066240 | bytes 9125477 | solution.py:89
  226.3 150.7 %while.177 = (s32[]{:T(128)}, bf16[2,1024,576]{1,2,0:T(8,128)(2,1)}, s32[2]{0:T(128)S(1)}, bf16[2,1024,576]{2,1,0:T(8,128)(2,1)}, bf16[2,1024,192]{2,1,0:T(8,128...) while((s32[]{:T(128)}, bf16[2,1024,576]{1,2,0:T(8,128)(2,1)}, s32[2]{0:T(128)S(1)}, ...), condition=%wide.region_40.41_spmd, body=%wide.region_22.40_spmd.sunk | while | flops 1035339264 | bytes 69338328 | solution.py:256
  228.1 71.4 %conditional.5 = (bf16[1,1024,576]{1,2,0:T(8,128)(2,1)}) conditional(s32[]{:T(128)} %convert_element_type.245, () %tuple.201, (bf16[2,1024,576]{2,1,0:T(8,128)(2,1)}, s32[]{:T(128)}, s32[]{:T(128)}, bf16[2,1024,192]{2,1,0:T(8,128)(2,1)}, bf16[2,1024,192]{2,1,0:T(8,128)(2,1)}) %tuple.202), branch_computations={%region_23.23_spmd, %region_24.39_spmd} | conditional | flops 1035339264 | bytes 66978368 | solution.py:131
  233.8 20.6 %while.174 = (s32[]{:T(128)}, f32[1024,64]{0,1:T(8,128)}, f32[1024,64]{0,1:T(8,128)}, bf16[2,512,64]{1,2,0:T(8,128)(2,1)S(1)}, pred[2,512]{1,0:T(4,128)(4,1)S(1)...) while((s32[]{:T(128)}, f32[1024,64]{0,1:T(8,128)}, ...), condition=%wide.region_34.33_spmd.clone, body=%wide.region_30.32_spmd.clone.sunk | while | flops 344915456 | bytes 15423156 | solution.py:89
  256.7 17.8 %while.173 = (s32[]{:T(128)}, f32[1024,64]{0,1:T(8,128)}, f32[1024,64]{0,1:T(8,128)}, bf16[2,512,64]{1,2,0:T(8,128)(2,1)}, pred[2,512]{1,0:T(4,128)(4,1)S(1)}, /...) while((s32[]{:T(128)}, f32[1024,64]{0,1:T(8,128)}, ...), condition=%wide.region_29.28_spmd.clone, body=%wide.region_25.27_spmd.clone.sunk | while | flops 344915456 | bytes 15946964 | solution.py:89
  276.8 13.3 %while.175 = (s32[]{:T(128)}, f32[1024,64]{0,1:T(8,128)S(1)}, f32[1024,64]{0,1:T(8,128)}, bf16[2,512,64]{1,2,0:T(8,128)(2,1)S(1)}, pred[2,512]{1,0:T(4,128)(4,1)...) while((s32[]{:T(128)}, f32[1024,64]{0,1:T(8,128)S(1)}, ...), condition=%wide.region_39.38_spmd.clone, body=%wide.region_35.37_spmd.clone.sunk | while | flops 344915456 | bytes 16077020 | solution.py:89
  303.2 71.4 %conditional.5 = (bf16[1,1024,576]{1,2,0:T(8,128)(2,1)}) conditional(s32[]{:T(128)} %convert_element_type.245, () %tuple.201, (bf16[2,1024,576]{2,1,0:T(8,128)(2,1)}, s32[]{:T(128)}, s32[]{:T(128)}, bf16[2,1024,192]{2,1,0:T(8,128)(2,1)}, bf16[2,1024,192]{2,1,0:T(8,128)(2,1)}) %tuple.202), branch_computations={%region_23.23_spmd, %region_24.39_spmd} | conditional | flops 1035339264 | bytes 66978368 | solution.py:131
  309.0 20.6 %while.174 = (s32[]{:T(128)}, f32[1024,64]{0,1:T(8,128)}, f32[1024,64]{0,1:T(8,128)}, bf16[2,512,64]{1,2,0:T(8,128)(2,1)S(1)}, pred[2,512]{1,0:T(4,128)(4,1)S(1)...) while((s32[]{:T(128)}, f32[1024,64]{0,1:T(8,128)}, ...), condition=%wide.region_34.33_spmd.clone, body=%wide.region_30.32_spmd.clone.sunk | while | flops 344915456 | bytes 15423156 | solution.py:89
  331.9 17.8 %while.173 = (s32[]{:T(128)}, f32[1024,64]{0,1:T(8,128)}, f32[1024,64]{0,1:T(8,128)}, bf16[2,512,64]{1,2,0:T(8,128)(2,1)}, pred[2,512]{1,0:T(4,128)(4,1)S(1)}, /...) while((s32[]{:T(128)}, f32[1024,64]{0,1:T(8,128)}, ...), condition=%wide.region_29.28_spmd.clone, body=%wide.region_25.27_spmd.clone.sunk | while | flops 344915456 | bytes 15946964 | solution.py:89
  351.9 13.3 %while.175 = (s32[]{:T(128)}, f32[1024,64]{0,1:T(8,128)S(1)}, f32[1024,64]{0,1:T(8,128)}, bf16[2,512,64]{1,2,0:T(8,128)(2,1)S(1)}, pred[2,512]{1,0:T(4,128)(4,1)...) while((s32[]{:T(128)}, f32[1024,64]{0,1:T(8,128)S(1)}, ...), condition=%wide.region_39.38_spmd.clone, body=%wide.region_35.37_spmd.clone.sunk | while | flops 344915456 | bytes 16077020 | solution.py:89
  377.0 3.1 copy.73
  380.1 9.3 %gather_fusion.6 = bf16[2048,576]{1,0:T(8,128)(2,1)} fusion(bf16[2048,576]{1,0:T(8,128)(2,1)S(1)} %bitcast.306, s32[2048]{0:T(1024)S(1)} %copy-done.18), kind=kCustom, calls=%fused_computation.6 | custom fusion | bytes 4726784 | tf_op jit(solution)/shard_map/gather | solution.py:144
  389.5 6.0 %reshape.615 = bf16[1179648]{0:T(1024)(128)(2,1)} reshape(bf16[2048,576]{1,0:T(8,128)(2,1)} %gather_fusion.6) | data formatting | bytes 4718592
  395.5 4.2 reshape.616
  399.6 7.5 %gather_fusion.2 = bf16[2048,192]{1,0:T(8,128)(2,1)S(1)} fusion(bf16[2048,192]{1,0:T(8,128)(2,1)S(1)} %bitcast.307, s32[2048]{0:T(1024)S(1)} %copy-done.18), kind=kCustom, calls=%fused_computation.2 | custom fusion | bytes 1581056 | tf_op jit(solution)/shard_map/gather | solution.py:144
  409.2 3.2 reduce.17
  412.4 2.6 reshape.621
  415.0 4.2 all-to-all-start.1
  419.3 2.6 broadcast_select_fusion
  421.9 3.1 reduce.19
  424.9 3.5 reshape.625
  428.4 10.7 %all-to-all-done.1 = bf16[8,2,24576]{2,1,0:T(2,128)(2,1)} async-done(((bf16[8,2,24576]{2,1,0:T(2,128)(2,1)}), bf16[8,2,24576]{2,1,0:T(2,128)(2,1)}, u32[]{:S(2)}, u32[]{:S(2)}) %all-to-all-start.1) | async-done | bytes 786464 | tf_op jit(solution)/shard_map/all_to_all | solution.py:218
  439.1 4.4 all-to-all-start.3
  443.5 4.3 reshape.622
  447.9 4.8 reduce.7
  453.8 3.9 gather_fusion.3
  458.8 21.0 %all-gather.6.cloned.1.call-done = bf16[768,1024]{1,0:T(8,128)(2,1)} async-done(((bf16[192,1024]{1,0:T(8,128)(2,1)}), bf16[768,1024]{1,0:T(8,128)(2,1)}) %all-gather.6.cloned.1.call-update) | async-done | bytes 1572880 | tf_op jit(solution)/shard_map/all_gather | solution.py:267
  479.8 2.9 convolution_convert_fusion.4
  482.8 14.0 %all-to-all-done.3 = bf16[8,2,73728]{2,1,0:T(2,128)(2,1)} async-done(((bf16[8,2,73728]{2,1,0:T(2,128)(2,1)}), bf16[8,2,73728]{2,1,0:T(2,128)(2,1)}, u32[]{:S(2)}, u32[]{:S(2)}) %all-to-all-start.3) | async-done | bytes 2359328 | tf_op jit(solution)/shard_map/all_to_all | solution.py:257
  496.8 7.0 %reshape.626 = bf16[8,1,147456]{2,1,0:T(2,128)(2,1)} reshape(bf16[8,2,73728]{2,1,0:T(2,128)(2,1)} %all-to-all-done.3) | data formatting | bytes 4718592
  503.7 14.8 %reduce.9 = bf16[8,147456]{1,0:T(8,128)(2,1)S(1)} reduce(bf16[8,1,147456]{2,1,0:T(2,128)(2,1)} %reshape.626, bf16[]{:T(256)} %constant.249), dimensions={1}, to_apply=%all_to_all.19.reduce_sub_computation | reduce | bytes 4718594 | tf_op jit(solution)/shard_map/all_to_all | solution.py:257
  518.6 2.5 reshape.617
  521.1 4.3 reshape.524
  525.4 5.1 gather_fusion.7
  (432 shorter events, 234.0 us)
Async XLA Ops:
  7.2 3.2 copy-start.16
  7.2 30.8 %all-gather.8.cloned.1.call-start = ((), (), s32[]{:S(2)}) async-start(), calls=%async_computation.6 | async-start | bytes 1966080 | tf_op jit(solution)/shard_map/all_gather | solution.py:227
  10.3 0.7 copy-start.20
  34.1 3.9 copy-start.15
  50.7 13.1 %copy-start.12 = (bf16[1,8,147456]{2,1,0:T(8,128)(2,1)S(1)}, bf16[1,8,147456]{2,1,0:T(8,128)(2,1)}, u32[]{:S(2)}) copy-start(bf16[1,8,147456]{2,1,0:T(8,128)(2,1)} %reshape.610) | copy-start | bytes 7077892
  56.5 27.6 %all-to-all-start.2 = ((bf16[8,2,24576]{2,1,0:T(2,128)(2,1)}), bf16[8,2,24576]{2,1,0:T(2,128)(2,1)}, u32[]{:S(2)}, u32[]{:S(2)}) async-start(bf16[8,2,24576]{2,1,0:T(2,128)(2,1)} %reshape.623), calls=%async_computation.2 | async-start | bytes 1572864 | tf_op jit(solution)/shard_map/all_to_all | solution.py:233
  72.9 16.3 %copy-start.21 = (s32[2]{0:T(128)S(1)}, s32[2]{0:T(128)}, u32[]{:S(2)}) copy-start(s32[2]{0:T(128)} %param.35) | copy-start | bytes 28
  72.9 16.4 %copy-start.17 = (s32[2,1024]{1,0:T(2,128)S(1)}, s32[2,1024]{1,0:T(2,128)}, u32[]{:S(2)}) copy-start(s32[2,1024]{1,0:T(2,128)} %param.34) | copy-start | bytes 24580
  84.0 57.7 %all-to-all-start = ((bf16[8,2,73728]{2,1,0:T(2,128)(2,1)}), bf16[8,2,73728]{2,1,0:T(2,128)(2,1)}, u32[]{:S(2)}, u32[]{:S(2)}) async-start(bf16[8,2,73728]{2,1,0:T(2,128)(2,1)} %reshape.619), calls=%async_computation | async-start | bytes 4718592 | tf_op jit(solution)/shard_map/all_to_all | solution.py:194
  88.4 370.3 %all-gather.4.cloned.1.call-start = ((), (), s32[]{:S(2)}) async-start(), calls=%async_computation.4 | async-start | bytes 1474560 | tf_op jit(solution)/shard_map/all_gather | solution.py:265
  181.2 20.9 %copy-start.4 = (bf16[2,1024,192]{2,1,0:T(8,128)(2,1)S(1)}, bf16[2,1024,192]{2,1,0:T(8,128)(2,1)}, u32[]{:S(2)}) copy-start(bf16[2,1024,192]{2,1,0:T(8,128)(2,1)} %get-tuple-element.1442) | copy-start | bytes 2359300 | tf_op jit(solution)/shard_map/while
  202.1 1.0 copy-start.5
  204.4 20.9 %copy-start.4 = (bf16[2,1024,192]{2,1,0:T(8,128)(2,1)S(1)}, bf16[2,1024,192]{2,1,0:T(8,128)(2,1)}, u32[]{:S(2)}) copy-start(bf16[2,1024,192]{2,1,0:T(8,128)(2,1)} %get-tuple-element.1442) | copy-start | bytes 2359300 | tf_op jit(solution)/shard_map/while
  225.3 1.0 copy-start.5
  229.5 2.2 copy-start.6
  229.5 2.2 copy-start.11
  236.5 1.8 copy-start.3
  246.7 1.8 copy-start.3
  254.4 0.7 copy-start.10
  256.7 20.1 %copy-start = (bf16[1024,64]{1,0:T(8,128)(2,1)S(1)}, bf16[1024,64]{1,0:T(8,128)(2,1)}, u32[]{:S(2)}) copy-start(bf16[1024,64]{1,0:T(8,128)(2,1)} %get-tuple-element.1332) | copy-start | bytes 393220 | tf_op jit(solution)/shard_map/while/body/eval_jaxpr/cond
  259.4 1.0 copy-start.9
  259.4 1.1 copy-start.2
  267.8 1.0 copy-start.9
  267.8 1.1 copy-start.2
  279.5 1.0 copy-start.8
  280.1 1.0 copy-start.1
  285.7 1.0 copy-start.8
  286.3 1.0 copy-start.1
  304.7 2.2 copy-start.6
  304.7 2.2 copy-start.11
  311.7 1.8 copy-start.3
  321.9 1.8 copy-start.3
  329.6 0.7 copy-start.10
  331.8 20.1 %copy-start = (bf16[1024,64]{1,0:T(8,128)(2,1)S(1)}, bf16[1024,64]{1,0:T(8,128)(2,1)}, u32[]{:S(2)}) copy-start(bf16[1024,64]{1,0:T(8,128)(2,1)} %get-tuple-element.1332) | copy-start | bytes 393220 | tf_op jit(solution)/shard_map/while/body/eval_jaxpr/cond
  334.6 1.0 copy-start.9
  334.6 1.1 copy-start.2
  343.0 1.0 copy-start.9
  343.0 1.1 copy-start.2
  354.6 1.0 copy-start.8
  355.3 1.0 copy-start.1
  360.8 1.0 copy-start.8
  361.4 1.0 copy-start.1
  377.0 3.1 copy-start.18
  395.5 4.2 copy-start.7
  407.1 1.2 copy-start.14
  409.2 10.0 %copy-start.13 = (bf16[1,8,147456]{2,1,0:T(8,128)(2,1)S(1)}, bf16[1,8,147456]{2,1,0:T(8,128)(2,1)}, u32[]{:S(2)}) copy-start(bf16[1,8,147456]{2,1,0:T(8,128)(2,1)} %reshape.616) | copy-start | bytes 7077892
  415.0 24.1 %all-to-all-start.1 = ((bf16[8,2,24576]{2,1,0:T(2,128)(2,1)}), bf16[8,2,24576]{2,1,0:T(2,128)(2,1)}, u32[]{:S(2)}, u32[]{:S(2)}) async-start(bf16[8,2,24576]{2,1,0:T(2,128)(2,1)} %reshape.621), calls=%async_computation.1 | async-start | bytes 1572864 | tf_op jit(solution)/shard_map/all_to_all | solution.py:218
  439.1 57.7 %all-to-all-start.3 = ((bf16[8,2,73728]{2,1,0:T(2,128)(2,1)}), bf16[8,2,73728]{2,1,0:T(2,128)(2,1)}, u32[]{:S(2)}, u32[]{:S(2)}) async-start(bf16[8,2,73728]{2,1,0:T(2,128)(2,1)} %reshape.625), calls=%async_computation.3 | async-start | bytes 4718592 | tf_op jit(solution)/shard_map/all_to_all | solution.py:257
  443.5 36.4 %all-gather.6.cloned.1.call-start = ((), (), s32[]{:S(2)}) async-start(), calls=%async_computation.5 | async-start | bytes 1966080 | tf_op jit(solution)/shard_map/all_gather | solution.py:267
  447.8 6.0 %copy-start.19 = (s32[1024]{0:T(1024)S(1)}, s32[1024]{0:T(1024)}, u32[]{:S(2)}) copy-start(s32[1024]{0:T(1024)} %get-tuple-element.785) | copy-start | bytes 12292
Sparse Core Ops, SparseCore 0:
  9.6 22.3 all-gather.7
  90.8 18.7 all-gather.3
  458.9 20.9 all-gather.5
where the time goes:
time: 547 us; the launch traced here: 542 us
  local copies, waits for them, and re-layouts  197 us (36%)
  other arithmetic  142 us (26%)
  matrix products  88.3 us (16%)
  waiting for transfers between devices  74.6 us (14%)
  starting transfers between devices  20.3 us (4%)
  between operations  14.5 us (3%)
    unnamed x49, local copies, waits for them, and re-layouts  72.5 us
    gather x6, local copies, waits for them, and re-layouts, place_rows(): return jnp.where(present[:, None], rows[source], jnp.zeros((), rows.dtype))  36.5 us
    dot_general x24, matrix products, block_weights(): lax.dot_general(query_block, key_head, (((1,), (1,)), ((), ())), preferre...  23.5 us
    all_gather x1, waiting for transfers between devices, body(): piece = lax.all_gather(shortened(attention.T), 'head', axis=0, tiled=True)  21 us
    dot_general x12, matrix products, block_grads(): lax.dot_general(weights, grad_block, (((0,), (0,)), ((), ())), preferred_...  20.3 us
    select_n x10, other arithmetic, place_rows(): return jnp.where(present[:, None], rows[source], jnp.zeros((), rows.dtype))  19.6 us
    lt x28, other arithmetic, work(): row_valid = jnp.arange(query_part.shape[0]) < count  18.8 us
    gather x2, local copies, waits for them, and re-layouts, collect_rows(): flat = arrived.reshape(slot_total, -1)[owner_slot]  18.3 us
  transfers between devices with their start and end apart: 7, of which 5 were waited for; matrix products, arithmetic and copies ran while one was open for 67% of the time, Pallas kernels for 0%

commit v1 on v0

v1 whole, which is shorter than its diff:
```python
import functools
import math

import jax
import jax.numpy as jnp
from jax import lax
from jax.experimental import pallas as pl
from jax.experimental.pallas import tpu as pltpu
from jax.sharding import PartitionSpec as P

HEAD_DIM = 64
CLUSTER = 1024
PAIR = 2 * HEAD_DIM
TILE = 256
SPARE = 32
VMEM_LIMIT = 56 * 1024 * 1024
masked_score = -1e30

NT = (((1,), (1,)), ((), ()))
NN = (((1,), (0,)), ((), ()))


def dot(left, right, dims=NN):
    return lax.dot_general(left, right, dims, preferred_element_type=jnp.float32)


class Plan:
    def __init__(self, nodes, rows, width, clusters):
        self.nodes = nodes
        self.rows = rows
        self.width = width
        self.heads = width // HEAD_DIM
        self.clusters = clusters
        self.total = nodes * clusters
        self.depth = 2 * rows // nodes
        self.half = self.depth // 2
        large = min(self.heads, nodes // 4)
        self.cap = large * self.depth + (self.heads - large) * self.half
        self.shift = tuple(3 * head % nodes for head in range(self.heads))
        self.units = self.heads * clusters
        self.tiles = self.units * (CLUSTER // TILE)


def owner_rows(plan, hist, owner):
    return sum(hist[owner * plan.clusters + index] for index in range(plan.clusters))


def each_chunk(plan, hist, starts, visit):
    def begin(owner, at):
        starts[owner] = at
        return at + owner_rows(plan, hist, owner) // plan.half

    lax.fori_loop(0, plan.nodes, begin, jnp.int32(0))

    def block(dest, carry):
        slot = jnp.int32(0)
        for head in range(plan.heads):
            owner = lax.rem(dest + plan.shift[head], plan.nodes)
            row = starts[owner]
            count = owner_rows(plan, hist, owner) // plan.half
            for index in range(2):

                @pl.when(index < count)
                def _(slot=slot, head=head, row=row, index=index):
                    visit(dest, slot + index, head, row + index)

            slot = slot + count
        return carry

    lax.fori_loop(0, plan.nodes, block, 0)


def chunk_rows(plan, index):
    return pl.ds(pl.multiple_of(index * plan.half, plan.half), plan.half)


def spread(plan, pos, first, second, hist, starts, ordered, wire):
    parts = []
    for head in range(plan.heads):
        span = slice(head * HEAD_DIM, (head + 1) * HEAD_DIM)
        parts += [first[span, :], second[span, :]]
    source = jnp.concatenate(parts, axis=0)
    for at in range(0, plan.rows, TILE):
        row = lax.broadcasted_iota(jnp.int32, (TILE, plan.rows), 0) + at
        pick = (row == pos).astype(jnp.bfloat16)
        ordered[at : at + TILE, :] = dot(pick, source, NT).astype(jnp.bfloat16)
    wire[...] = jnp.zeros_like(wire)

    def visit(dest, slot, head, row):
        wire[dest, chunk_rows(plan, slot), :] = ordered[
            chunk_rows(plan, row), head * PAIR : (head + 1) * PAIR
        ]

    each_chunk(plan, hist, starts, visit)


def pack_first_kernel(plan, hist, ids, queries, keys, wire, pos_out, starts, ordered):
    rows = plan.rows
    rank = ids[...] * rows + lax.broadcasted_iota(jnp.int32, (1, rows), 1)
    rank = rank.astype(jnp.float32)
    column = jnp.broadcast_to(rank, (128, rows)).T
    parts = []
    for at in range(0, rows, 128):
        below = (column < rank[:, at : at + 128]).astype(jnp.float32)
        parts.append(jnp.sum(below, axis=0, keepdims=True))
    pos = jnp.concatenate(parts, axis=1).astype(jnp.int32)
    pos_out[...] = pos
    spread(plan, pos, queries[...], keys[...], hist, starts, ordered, wire)


def pack_second_kernel(plan, hist, pos, values, weight, cotangent, wire, starts, ordered):
    grad_in = dot(weight[...], cotangent[...]).astype(jnp.bfloat16)
    spread(plan, pos[...], values[...], grad_in, hist, starts, ordered, wire)


def unpack_kernel(plan, hist, pos, wire, first, second, starts, ordered):
    def visit(dest, slot, head, row):
        ordered[head, chunk_rows(plan, row), :] = wire[dest, chunk_rows(plan, slot), :]

    each_chunk(plan, hist, starts, visit)
    source = jnp.concatenate(
        [ordered[head].astype(jnp.float32).T.astype(jnp.bfloat16) for head in range(plan.heads)],
        axis=0,
    )
    for at in range(0, plan.rows, TILE):
        row = lax.broadcasted_iota(jnp.int32, (plan.rows, TILE), 0)
        pick = (row == pos[:, at : at + TILE]).astype(jnp.bfloat16)
        out = dot(source, pick).astype(jnp.bfloat16)
        for head in range(plan.heads):
            span = slice(head * HEAD_DIM, (head + 1) * HEAD_DIM)
            first[span, at : at + TILE] = out[head * PAIR : head * PAIR + HEAD_DIM, :]
            second[span, at : at + TILE] = out[head * PAIR + HEAD_DIM : (head + 1) * PAIR, :]


def each_group(plan, hist, me, visit):
    def source(index, places):
        at = index * plan.cap
        after = []
        for head in range(plan.heads):
            owner = lax.rem(me + plan.shift[head], plan.nodes)
            for cluster in range(plan.clusters):
                unit = head * plan.clusters + cluster
                count = hist[index * plan.total + owner * plan.clusters + cluster]
                visit(unit, places[unit], at, count)
                at = at + count
                after.append(places[unit] + count)
        return tuple(after)

    return lax.fori_loop(0, plan.nodes, source, (jnp.int32(0),) * plan.units)


def gather_units(plan, hist, me, wire, stage, held, counts):
    flat = plan.nodes * plan.cap
    for index in range(plan.nodes):
        stage[index * plan.cap : (index + 1) * plan.cap, :] = wire[index].astype(jnp.float32)
    stage[flat : flat + SPARE, :] = jnp.zeros((SPARE, PAIR), jnp.float32)

    def visit(unit, place, at, count):
        def step(index, carry):
            held[unit, pl.ds(place + index * SPARE, SPARE), :] = stage[
                pl.ds(at + index * SPARE, SPARE), :
            ]
            return carry

        lax.fori_loop(0, pl.cdiv(count, SPARE), step, 0)

    totals = each_group(plan, hist, me, visit)
    for unit in range(plan.units):
        counts[unit] = totals[unit]


def scatter_units(plan, hist, me, held, stage, wire):
    def visit(unit, place, at, count):
        def step(index, carry):
            stage[pl.ds(at + index * SPARE, SPARE), :] = held[
                unit, pl.ds(place + index * SPARE, SPARE), :
            ]
            return carry

        lax.fori_loop(0, pl.cdiv(count, SPARE), step, 0)

    each_group(plan, hist, me, visit)
    for index in range(plan.nodes):
        wire[index] = stage[index * plan.cap : (index + 1) * plan.cap, :].astype(jnp.bfloat16)


def unit_rows(held, unit, count):
    row = lax.broadcasted_iota(jnp.int32, (CLUSTER, PAIR), 0)
    return jnp.where(row < count, held[unit, 0:CLUSTER, :], 0.0)


def weights_kernel(plan, hist, me, wire, queries, keys_t, weights, stage, held, counts, query_aug,
                   key_aug, out, sems):
    gather_units(plan, hist, me[0], wire, stage, held, counts)
    factor = math.log2(math.e) / math.sqrt(HEAD_DIM)
    lane = lax.broadcasted_iota(jnp.int32, (CLUSTER, PAIR), 1)
    row = lax.broadcasted_iota(jnp.int32, (CLUSTER, PAIR), 0)

    def copy_out(step):
        slot = lax.rem(step, 2)
        return pltpu.make_async_copy(out.at[slot], weights.at[step], sems.at[slot])

    def one_unit(unit, step):
        count = counts[unit]
        both = unit_rows(held, unit, count)
        turned = pltpu.roll(both, HEAD_DIM, 1)
        queries[unit] = jnp.where(lane < HEAD_DIM, both, 0.0).astype(jnp.bfloat16)
        keys_t[unit] = turned.T[0:HEAD_DIM, :].astype(jnp.bfloat16)
        one = jnp.where(lane == HEAD_DIM, 1.0, 0.0)
        query_aug[...] = jnp.where(lane < HEAD_DIM, both, one).astype(jnp.bfloat16)
        outside = jnp.where(jnp.logical_and(lane == HEAD_DIM, row >= count), masked_score, 0.0)
        key_aug[...] = jnp.where(lane < HEAD_DIM, turned, outside).astype(jnp.bfloat16)

        def one_tile(tile, step):
            slot = lax.rem(step, 2)
            part = query_aug[pl.ds(pl.multiple_of(tile * TILE, TILE), TILE), :]
            scores = dot(key_aug[...], part, NT)
            raised = jnp.exp2((scores - jnp.max(scores, axis=0, keepdims=True)) * factor)
            share = 1.0 / jnp.sum(raised, axis=0, keepdims=True)

            @pl.when(step >= 2)
            def _():
                copy_out(step - 2).wait()

            out[slot] = (raised * share).astype(jnp.bfloat16)
            copy_out(step).start()
            return step + 1

        return lax.fori_loop(0, pl.cdiv(count, TILE), one_tile, step)

    steps = lax.fori_loop(0, plan.units, one_unit, jnp.int32(0))
    for back in (2, 1):

        @pl.when(steps >= back)
        def _(back=back):
            copy_out(steps - back).wait()


def grads_kernel(plan, hist, me, wire, queries, keys_t, weights, wire_first, wire_second, stage,
                 held, counts, value_turned, grad_rows, both_t, held_first, held_second, total,
                 tiles, sems):
    gather_units(plan, hist, me[0], wire, stage, held, counts)
    scale = 1.0 / math.sqrt(HEAD_DIM)
    lane = lax.broadcasted_iota(jnp.int32, (CLUSTER, PAIR), 1)
    steps = sum(pl.cdiv(counts[unit], TILE) for unit in range(plan.units))

    def copy_in(step):
        slot = lax.rem(step, 2)
        return pltpu.make_async_copy(weights.at[step], tiles.at[slot], sems.at[slot])

    @pl.when(steps > 0)
    def _():
        copy_in(0).start()

    def one_unit(unit, step):
        count = counts[unit]
        both = unit_rows(held, unit, count)
        turned = pltpu.roll(both, HEAD_DIM, 1)
        value_turned[...] = jnp.where(lane >= HEAD_DIM, turned, 0.0).astype(jnp.bfloat16)
        grad_rows[...] = jnp.where(lane >= HEAD_DIM, both, 0.0).astype(jnp.bfloat16)
        both_t[...] = both.T.astype(jnp.bfloat16)
        total[...] = jnp.zeros_like(total)

        def one_tile(tile, step):
            slot = lax.rem(step, 2)
            span = pl.ds(pl.multiple_of(tile * TILE, TILE), TILE)

            @pl.when(step + 1 < steps)
            def _():
                copy_in(step + 1).start()

            copy_in(step).wait()
            held_weights = tiles[slot]
            mixed = dot(both_t[0:HEAD_DIM, :], held_weights).astype(jnp.bfloat16)
            mixed = mixed.astype(jnp.float32)
            grad_t = both_t[HEAD_DIM:PAIR, span].astype(jnp.float32)
            delta = jnp.sum(grad_t * mixed, axis=0, keepdims=True)
            grad_part = grad_rows[span, :]
            dweights = dot(value_turned[...], grad_part, NT)
            dscores = (held_weights.astype(jnp.float32) * (dweights - delta)).astype(jnp.bfloat16)
            grad_query = dot(keys_t[unit], dscores) * scale
            held_first[unit, span, :] = jnp.concatenate([mixed, grad_query], axis=0).T
            total[...] += dot(
                jnp.concatenate([dscores, held_weights], axis=1),
                jnp.concatenate([queries[unit, span, :], grad_part], axis=0),
            )
            return step + 1

        step = lax.fori_loop(0, pl.cdiv(count, TILE), one_tile, step)
        factor = jnp.where(lane < HEAD_DIM, scale, 1.0)
        held_second[unit, 0:CLUSTER, :] = total[...] * factor
        return step

    lax.fori_loop(0, plan.units, one_unit, jnp.int32(0))
    scatter_units(plan, hist, me[0], held_first, stage, wire_first)
    scatter_units(plan, hist, me[0], held_second, stage, wire_second)


SCALARS = pl.BlockSpec(memory_space=pltpu.SMEM)
WHOLE = pl.BlockSpec(memory_space=pltpu.VMEM)
APART = pl.BlockSpec(memory_space=pl.ANY)


def call(kernel, plan, name, outs, out_specs, in_specs, scratch, flops, args):
    shapes = [jax.ShapeDtypeStruct(shape, dtype) for shape, dtype in outs]
    moved = sum(math.prod(shape) * jnp.dtype(dtype).itemsize for shape, dtype in outs)
    return pl.pallas_call(
        functools.partial(kernel, plan),
        out_shape=shapes,
        in_specs=in_specs,
        out_specs=out_specs,
        scratch_shapes=scratch,
        compiler_params=pltpu.CompilerParams(vmem_limit_bytes=VMEM_LIMIT),
        cost_estimate=pl.CostEstimate(flops=flops, bytes_accessed=2 * moved, transcendentals=0),
        name=name,
    )(*args)


def body(queries, key_rows, value_rows, out_weight, cotangent, cluster_ids, members, counts):
    nodes = lax.axis_size("node")
    width, rows = queries.shape
    plan = Plan(nodes, rows, width, members.shape[0])
    me = lax.axis_index("node").astype(jnp.int32).reshape(1)
    narrow = jnp.bfloat16
    wire_shape = ((plan.nodes, plan.cap, PAIR), narrow)
    home_shape = ((width, rows), narrow)
    starts = pltpu.SMEM((plan.nodes,), jnp.int32)
    ordered = pltpu.VMEM((rows, plan.heads * PAIR), narrow)
    stage = pltpu.VMEM((plan.nodes * plan.cap + SPARE, PAIR), jnp.float32)
    held = pltpu.VMEM((plan.units, CLUSTER + SPARE, PAIR), jnp.float32)
    unit_counts = pltpu.SMEM((plan.units,), jnp.int32)
    unit_block = pltpu.VMEM((CLUSTER, PAIR), narrow)
    tiles = pltpu.VMEM((2, CLUSTER, TILE), narrow)
    sems = pltpu.SemaphoreType.DMA((2,))

    def swap(wire):
        return lax.all_to_all(wire, "node", split_axis=0, concat_axis=0, tiled=True)

    named = jnp.arange(plan.total, dtype=jnp.int32)[:, None] == cluster_ids[None, :]
    hist = jnp.sum(named, axis=1, dtype=jnp.int32)
    all_hist = lax.all_gather(hist, "node", axis=0, tiled=True)
    all_cotangent = lax.all_gather(cotangent, "head", axis=0, tiled=True)
    all_weight = lax.all_gather(out_weight, "head", axis=0, tiled=True)

    wire, pos = call(
        pack_first_kernel, plan, "pack_queries_keys", [wire_shape, ((1, rows), jnp.int32)],
        [WHOLE, WHOLE], [SCALARS, WHOLE, WHOLE, WHOLE], [starts, ordered], 2 * 10**9,
        (hist, cluster_ids.reshape(1, rows), queries, key_rows),
    )
    query_wire = swap(wire)
    (wire,) = call(
        pack_second_kernel, plan, "pack_values_grads", [wire_shape],
        [WHOLE], [SCALARS, WHOLE, WHOLE, WHOLE, WHOLE], [starts, ordered], 2 * 10**9,
        (hist, pos, value_rows, out_weight, all_cotangent),
    )
    value_wire = swap(wire)

    unit_queries = ((plan.units, CLUSTER, PAIR), narrow)
    unit_keys = ((plan.units, HEAD_DIM, CLUSTER), narrow)
    unit_weights = ((plan.tiles, CLUSTER, TILE), narrow)
    kept_queries, kept_keys, weights = call(
        weights_kernel, plan, "weights", [unit_queries, unit_keys, unit_weights],
        [WHOLE, WHOLE, APART], [SCALARS, SCALARS, WHOLE],
        [stage, held, unit_counts, unit_block, unit_block, tiles, sems], 10 * 10**9,
        (all_hist, me, query_wire),
    )
    wire_first, wire_second = call(
        grads_kernel, plan, "attention_and_grads", [wire_shape, wire_shape],
        [WHOLE, WHOLE], [SCALARS, SCALARS, WHOLE, WHOLE, WHOLE, APART],
        [stage, held, unit_counts, unit_block, unit_block, pltpu.VMEM((PAIR, CLUSTER), narrow),
         held, held, pltpu.VMEM((CLUSTER, PAIR), jnp.float32), tiles, sems], 10 * 10**9,
        (all_hist, me, value_wire, kept_queries, kept_keys, weights),
    )

    def unpack(wire, name):
        return call(
            unpack_kernel, plan, name, [home_shape, home_shape], [WHOLE, WHOLE],
            [SCALARS, WHOLE, WHOLE],
            [starts, pltpu.VMEM((plan.heads, rows, PAIR), narrow)], 2 * 10**9,
            (hist, pos, wire),
        )

    attention, grad_queries = unpack(swap(wire_first), "unpack_attention_grad_queries")
    grad_keys, grad_values = unpack(swap(wire_second), "unpack_grad_keys_grad_values")
    all_attention = lax.all_gather(attention, "head", axis=0, tiled=True)
    mine = lax.dynamic_slice_in_dim(all_weight, lax.axis_index("head") * width, width, 1)
    output = lax.dot_general(
        mine, all_attention, (((0,), (0,)), ((), ())), preferred_element_type=jnp.float32
    ).astype(narrow)
    return (output, grad_queries, grad_keys, grad_values)


def solution(mesh):
    placed = (
        P("head", "node"),
        P("head", "node"),
        P("head", "node"),
        P("head", None),
        P("head", "node"),
        P("node"),
        P("node", None),
        P("node"),
    )
    return jax.shard_map(
        body,
        mesh=mesh,
        in_specs=placed,
        out_specs=(P("head", "node"), P("head", "node"), P("head", "node"), P("head", "node")),
        check_vma=False,
    )
```

time: 547 us -> 219 us (0.40)
  local copies, waits for them, and re-layouts: 197 us -> 5.11 us
  other arithmetic: 142 us -> 1.4 us
  matrix products: 88.3 us -> 2.92 us
  Pallas kernels: 0 us -> 59.4 us
  blocking collectives: 0 us -> 30.7 us
  waiting for transfers between devices: 74.6 us -> 84.8 us
    dot_general x86 -> x1, matrix products: 88.3 us -> 2.92 us  [body(): lax.dot_general(mine, all_attention, (((0,), (0,)), ((), ())), preferred_...]
    unnamed x49 -> x15, local copies, waits for them, and re-layouts: 72.5 us -> 5.11 us
    gather x10 -> x0, local copies, waits for them, and re-layouts: 63.9 us -> none  [the longest x6 36.5 us: place_rows(): return jnp.where(present[:, None], rows[source], jnp.zeros((), rows.dtype))]
    pallas_call x0 -> x6, Pallas kernels: none -> 59.4 us  [call(): pl.pallas_call(functools.partial(kernel, plan), out_shape=shapes, in_spec...]
    all_to_all x4 -> x0, other arithmetic: 39.2 us -> none  [the longest x1 14.8 us: body(): lax.all_to_all(dispatch_rows(rows, send_source, send_present, node_count)...]
    unnamed x0 -> x1, blocking collectives: none -> 30.7 us
    reduce_sum x40 -> x1, other arithmetic: 27.1 us -> 1.4 us  [body(): hist = jnp.sum(named, axis=1, dtype=jnp.int32)]
    all_to_all x4, waiting for transfers between devices: 52.2 us -> 72.9 us  [swap(): return lax.all_to_all(wire, 'node', split_axis=0, concat_axis=0, tiled=True)]
  transfers between devices with their start and end apart: 7 -> 7, of which waited for: 5 -> 4; matrix products, arithmetic and copies ran while one was open for 67% -> 1% of each run, Pallas kernels for 0% -> 16%
where the time goes in v1:
time: 219 us; the launch traced here: 217 us
  waiting for transfers between devices  84.8 us (39%)
  Pallas kernels  59.4 us (27%)
  blocking collectives  30.7 us (14%)
  starting transfers between devices  18.3 us (8%)
  between operations  14.5 us (7%)
  local copies, waits for them, and re-layouts  5.11 us (2%)
  matrix products  2.92 us (1%)
    all_to_all x4, waiting for transfers between devices, swap(): return lax.all_to_all(wire, 'node', split_axis=0, concat_axis=0, tiled=True)  72.9 us
    pallas_call x6, Pallas kernels, call(): pl.pallas_call(functools.partial(kernel, plan), out_shape=shapes, in_spec...  59.4 us
    unnamed x1, blocking collectives  30.7 us
    all_to_all x4, starting transfers between devices, swap(): return lax.all_to_all(wire, 'node', split_axis=0, concat_axis=0, tiled=True)  18.2 us
    all_gather x1, waiting for transfers between devices, body(): all_cotangent = lax.all_gather(cotangent, 'head', axis=0, tiled=True)  10.4 us
    unnamed x15, local copies, waits for them, and re-layouts  5.11 us
  transfers between devices with their start and end apart: 7, of which 4 were waited for; matrix products, arithmetic and copies ran while one was open for 1% of the time, Pallas kernels for 16%

profile of v1, /device:TPU:0, one launch (start us, length us, event | category | flops | bytes accessed | tf_op | source)
XLA Modules:
  0.0 217.1 jit_solution(5851459183358063302)
XLA Ops:
  7.2 0.0 all-gather.6.cloned.1.call-start
  7.2 0.7 all-gather.6.cloned.1.call-update
  7.9 1.4 convert_reduce_fusion.hist
  9.3 5.0 %pack_queries_keys.1 = (bf16[8,640,128]{2,1,0:T(8,128)(2,1)}, s32[1,1024]{1,0:T(1,128)}) custom-call(s32[16]{0:T(128)} %convert_reduce_fusion.hist, s32[1,1024]{1,0:T(1,128)} %bitcast.4, bf16[192,1024]{1,0:T(8,128)(2,1)} %queries.1, bf16[192,1024]{1,0:T(8,128)(2,1)} %keys.1), custom_call_target="tpu_custom_call" | custom-call | flops 2000000000 | bytes 2629632 | tf_op jit(solution)/shard_map/pack_queries_keys/pallas_call | solution.py:307
  14.3 7.3 %all-to-all-start.1 = ((bf16[8,640,128]{2,1,0:T(8,128)(2,1)}), bf16[8,640,128]{2,1,0:T(8,128)(2,1)S(1)}, u32[]{:S(2)}, u32[]{:S(2)}) async-start(bf16[8,640,128]{2,1,0:T(8,128)(2,1)} %get-tuple-element.16), calls=%async_computation.1 | async-start | bytes 2621440 | tf_op jit(solution)/shard_map/all_to_all | solution.py:337
  21.5 10.4 %all-gather.6.cloned.1.call-done.cotangent = bf16[768,1024]{1,0:T(8,128)(2,1)} async-done(((bf16[192,1024]{1,0:T(8,128)(2,1)}), bf16[768,1024]{1,0:T(8,128)(2,1)}) %all-gather.6.cloned.1.call-update) | async-done | bytes 1572880 | tf_op jit(solution)/shard_map/all_gather | solution.py:342
  32.0 5.2 %pack_values_grads.1 = bf16[8,640,128]{2,1,0:T(8,128)(2,1)} custom-call(s32[16]{0:T(128)} %convert_reduce_fusion.hist, s32[1,1024]{1,0:T(1,128)} %get-tuple-element.15.pos, bf16[192,1024]{1,0:T(8,128)(2,1)} %values.1, bf16[192,768]{1,0:T(8,128)(2,1)} %weight.1, bf16[768,1024]{1,0:T(8,128)(2,1)} %all-gather.6.cloned.1.call-done.cotangent), custom_call_target="tpu_custom_call" | custom-call | flops 2000000000 | bytes 2621440 | tf_op jit(solution)/shard_map/pack_values_grads/pallas_call | solution.py:307
  37.1 0.0 copy-start.5
  37.1 0.0 copy-start.4
  37.1 15.8 %all-to-all-done.1.wire = bf16[8,640,128]{2,1,0:T(8,128)(2,1)S(1)} async-done(((bf16[8,640,128]{2,1,0:T(8,128)(2,1)}), bf16[8,640,128]{2,1,0:T(8,128)(2,1)S(1)}, u32[]{:S(2)}, u32[]{:S(2)}) %all-to-all-start.1) | async-done | bytes 1310752 | tf_op jit(solution)/shard_map/all_to_all | solution.py:337
  52.9 0.0 copy-start
  52.9 1.1 copy-done
  54.0 3.6 %all-to-all-start = ((bf16[8,640,128]{2,1,0:T(8,128)(2,1)}), bf16[8,640,128]{2,1,0:T(8,128)(2,1)S(1)}, u32[]{:S(2)}, u32[]{:S(2)}) async-start(bf16[8,640,128]{2,1,0:T(8,128)(2,1)} %pack_values_grads.1), calls=%async_computation | async-start | bytes 2621440 | tf_op jit(solution)/shard_map/all_to_all | solution.py:337
  57.6 0.0 copy-done.5
  57.6 0.6 dynamic-slice
  58.9 0.0 copy-done.4
  58.9 0.2 dynamic-update-slice
  59.1 30.7 %all-reduce.hist = s32[128]{0:T(128)} all-reduce(s32[128]{0:T(128)S(1)} %dynamic-update-slice), channel_id=1, replica_groups=mesh['node'=8,'head'=4] {'node'}, use_global_device_ids=true, to_apply=%add | all-reduce | flops 128 | bytes 1024
  89.9 15.7 %weights.1 = (bf16[6,1024,128]{2,1,0:T(8,128)(2,1)}, bf16[6,64,1024]{2,1,0:T(8,128)(2,1)}, bf16[24,1024,256]{2,1,0:T(8,128)(2,1)}) custom-call(s32[128]{0:T(128)} %all-reduce.hist, s32[1]{0:T(128)} %bitcast.2.me, bf16[8,640,128]{2,1,0:T(8,128)(2,1)} %copy-done), custom_call_target="tpu_custom_call" | custom-call | flops 10000000000 | bytes 29884416 | tf_op jit(solution)/shard_map/weights/pallas_call | solution.py:307
  105.5 0.0 all-to-all-done.wire
  105.6 0.0 copy-start.1
  105.6 1.1 copy-done.1
  106.6 25.3 %attention_and_grads.1 = (bf16[8,640,128]{2,1,0:T(8,128)(2,1)}, bf16[8,640,128]{2,1,0:T(8,128)(2,1)}) custom-call(s32[128]{0:T(128)} %all-reduce.hist, s32[1]{0:T(128)} %bitcast.2.me, bf16[8,640,128]{2,1,0:T(8,128)(2,1)} %copy-done.1, bf16[6,1024,128]{2,1,0:T(8,128)(2,1)} %get-tuple-element.17.queries, bf16[6,64,1024]{2,1,0:T(8,128)(2,1)} %get-tuple-element.18.keys_t, ...), custom_call_target="tpu_custom_call" | custom-call | flops 10000000000 | bytes 5242880 | tf_op jit(solution)/shard_map/attention_and_grads/pallas_call | solution.py:307
  131.9 3.7 %all-to-all-start.2 = ((bf16[8,640,128]{2,1,0:T(8,128)(2,1)}), bf16[8,640,128]{2,1,0:T(8,128)(2,1)S(1)}, u32[]{:S(2)}, u32[]{:S(2)}) async-start(bf16[8,640,128]{2,1,0:T(8,128)(2,1)} %get-tuple-element.20), calls=%async_computation.2 | async-start | bytes 2621440 | tf_op jit(solution)/shard_map/all_to_all | solution.py:337
  135.7 0.0 all-gather.4.cloned.1.call-start
  135.7 0.7 all-gather.4.cloned.1.call-update
  136.4 30.0 %all-to-all-done.2.wire = bf16[8,640,128]{2,1,0:T(8,128)(2,1)S(1)} async-done(((bf16[8,640,128]{2,1,0:T(8,128)(2,1)}), bf16[8,640,128]{2,1,0:T(8,128)(2,1)S(1)}, u32[]{:S(2)}, u32[]{:S(2)}) %all-to-all-start.2) | async-done | bytes 1310752 | tf_op jit(solution)/shard_map/all_to_all | solution.py:337
  166.4 0.0 copy-start.3
  166.4 1.1 copy-done.3
  167.5 3.6 %all-to-all-start.3 = ((bf16[8,640,128]{2,1,0:T(8,128)(2,1)}), bf16[8,640,128]{2,1,0:T(8,128)(2,1)S(1)}, u32[]{:S(2)}, u32[]{:S(2)}) async-start(bf16[8,640,128]{2,1,0:T(8,128)(2,1)} %get-tuple-element.23), calls=%async_computation.3 | async-start | bytes 2621440 | tf_op jit(solution)/shard_map/all_to_all | solution.py:337
  171.1 0.0 all-gather.8.cloned.1.call-start
  171.1 4.1 %unpack_attention_grad_queries.1 = (bf16[192,1024]{1,0:T(8,128)(2,1)}, bf16[192,1024]{1,0:T(8,128)(2,1)}) custom-call(s32[16]{0:T(128)} %convert_reduce_fusion.hist, s32[1,1024]{1,0:T(1,128)} %get-tuple-element.15.pos, bf16[8,640,128]{2,1,0:T(8,128)(2,1)} %copy-done.3), custom_call_target="tpu_custom_call" | custom-call | flops 2000000000 | bytes 1572864 | tf_op jit(solution)/shard_map/unpack_attention_grad_queries/pallas_call | solution.py:307
  175.3 0.0 all-gather.8.cloned.1.call-update
  175.3 27.1 %all-to-all-done.3.wire = bf16[8,640,128]{2,1,0:T(8,128)(2,1)S(1)} async-done(((bf16[8,640,128]{2,1,0:T(8,128)(2,1)}), bf16[8,640,128]{2,1,0:T(8,128)(2,1)S(1)}, u32[]{:S(2)}, u32[]{:S(2)}) %all-to-all-start.3) | async-done | bytes 1310752 | tf_op jit(solution)/shard_map/all_to_all | solution.py:337
  202.4 0.0 copy-start.2
  202.4 1.1 copy-done.2
  203.5 4.1 %unpack_grad_keys_grad_values.1 = (bf16[192,1024]{1,0:T(8,128)(2,1)}, bf16[192,1024]{1,0:T(8,128)(2,1)}) custom-call(s32[16]{0:T(128)} %convert_reduce_fusion.hist, s32[1,1024]{1,0:T(1,128)} %get-tuple-element.15.pos, bf16[8,640,128]{2,1,0:T(8,128)(2,1)} %copy-done.2), custom_call_target="tpu_custom_call" | custom-call | flops 2000000000 | bytes 1572864 | tf_op jit(solution)/shard_map/unpack_grad_keys_grad_values/pallas_call | solution.py:307
  207.7 0.0 all-gather.4.cloned.1.call-done
  207.7 0.0 all-gather.8.cloned.1.call-done
  207.7 2.9 %convolution_convert_fusion = bf16[192,1024]{1,0:T(8,128)(2,1)} fusion(bf16[768,1024]{1,0:T(8,128)(2,1)} %all-gather.8.cloned.1.call-done, bf16[768,768]{1,0:T(8,128)(2,1)} %all-gather.4.cloned.1.call-done, s32[]{:T(128)S(6)} %select_n.3), kind=kOutput, calls=%fused_computation | convolution fusion | flops 302186496 | bytes 2359300 | tf_op jit(solution)/shard_map/dot_general | solution.py:387
  (1 shorter events, 0.0 us)
Async XLA Ops:
  7.2 24.8 %all-gather.6.cloned.1.call-start = ((), (), s32[]{:S(2)}) async-start(), calls=%async_computation.5 | async-start | bytes 1966080 | tf_op jit(solution)/shard_map/all_gather | solution.py:342
  14.3 38.6 %all-to-all-start.1 = ((bf16[8,640,128]{2,1,0:T(8,128)(2,1)}), bf16[8,640,128]{2,1,0:T(8,128)(2,1)S(1)}, u32[]{:S(2)}, u32[]{:S(2)}) async-start(bf16[8,640,128]{2,1,0:T(8,128)(2,1)} %get-tuple-element.16), calls=%async_computation.1 | async-start | bytes 2621440 | tf_op jit(solution)/shard_map/all_to_all | solution.py:337
  37.1 20.5 %copy-start.5 = (u32[32]{0:T(128)S(1)}, u32[32]{0:T(128)}, u32[]{:S(2)}) copy-start(u32[32]{0:T(128)} %constant.17) | copy-start | bytes 388
  37.1 21.7 %copy-start.4 = (s32[16]{0:T(128)S(1)}, s32[16]{0:T(128)}, u32[]{:S(2)}) copy-start(s32[16]{0:T(128)} %convert_reduce_fusion.hist) | copy-start | bytes 196
  52.9 1.1 copy-start
  54.0 51.6 %all-to-all-start = ((bf16[8,640,128]{2,1,0:T(8,128)(2,1)}), bf16[8,640,128]{2,1,0:T(8,128)(2,1)S(1)}, u32[]{:S(2)}, u32[]{:S(2)}) async-start(bf16[8,640,128]{2,1,0:T(8,128)(2,1)} %pack_values_grads.1), calls=%async_computation | async-start | bytes 2621440 | tf_op jit(solution)/shard_map/all_to_all | solution.py:337
  105.6 1.1 copy-start.1
  131.9 34.5 %all-to-all-start.2 = ((bf16[8,640,128]{2,1,0:T(8,128)(2,1)}), bf16[8,640,128]{2,1,0:T(8,128)(2,1)S(1)}, u32[]{:S(2)}, u32[]{:S(2)}) async-start(bf16[8,640,128]{2,1,0:T(8,128)(2,1)} %get-tuple-element.20), calls=%async_computation.2 | async-start | bytes 2621440 | tf_op jit(solution)/shard_map/all_to_all | solution.py:337
  135.7 72.0 %all-gather.4.cloned.1.call-start = ((), (), s32[]{:S(2)}) async-start(), calls=%async_computation.4 | async-start | bytes 1474560 | tf_op jit(solution)/shard_map/all_gather | solution.py:343
  166.4 1.1 copy-start.3
  167.5 34.9 %all-to-all-start.3 = ((bf16[8,640,128]{2,1,0:T(8,128)(2,1)}), bf16[8,640,128]{2,1,0:T(8,128)(2,1)S(1)}, u32[]{:S(2)}, u32[]{:S(2)}) async-start(bf16[8,640,128]{2,1,0:T(8,128)(2,1)} %get-tuple-element.23), calls=%async_computation.3 | async-start | bytes 2621440 | tf_op jit(solution)/shard_map/all_to_all | solution.py:337
  171.1 36.6 %all-gather.8.cloned.1.call-start = ((), (), s32[]{:S(2)}) async-start(), calls=%async_computation.6 | async-start | bytes 1966080 | tf_op jit(solution)/shard_map/all_gather | solution.py:385
  202.4 1.1 copy-start.2
Sparse Core Ops, SparseCore 0:
  9.6 22.3 all-gather.5
  138.1 18.8 all-gather.3
  175.4 21.0 all-gather.7

commit v2 on v1

v2 whole, which is shorter than its diff:
```python
import functools
import math

import jax
import jax.numpy as jnp
from jax import lax
from jax.experimental import pallas as pl
from jax.experimental.pallas import tpu as pltpu
from jax.sharding import PartitionSpec as P

HEAD_DIM = 64
CLUSTER = 1024
PAIR = 2 * HEAD_DIM
TILE = 256
SPARE = 32
NOTE = 16
VMEM_LIMIT = 56 * 1024 * 1024
masked_score = -1e30

NT = (((1,), (1,)), ((), ()))
NN = (((1,), (0,)), ((), ()))


def dot(left, right, dims=NN):
    return lax.dot_general(left, right, dims, preferred_element_type=jnp.float32)


class Plan:
    def __init__(self, nodes, rows, width, clusters):
        self.nodes = nodes
        self.rows = rows
        self.width = width
        self.heads = width // HEAD_DIM
        self.clusters = clusters
        self.total = nodes * clusters
        self.depth = 2 * rows // nodes
        self.half = self.depth // 2
        large = min(self.heads, nodes // 4)
        self.cap = large * self.depth + (self.heads - large) * self.half
        self.shift = tuple(3 * head % nodes for head in range(self.heads))
        self.units = self.heads * clusters
        self.tiles = self.units * (CLUSTER // TILE)
        self.split = nodes <= 16 and nodes & (nodes - 1) == 0
        self.blocks = nodes if self.split else 1


def owner_rows(plan, hist, owner):
    return sum(hist[owner * plan.clusters + index] for index in range(plan.clusters))


def each_block(plan, visit):
    if plan.split:
        for index in range(plan.nodes):
            visit(index)
    else:
        lax.fori_loop(0, plan.nodes, lambda index, carry: visit(index) or carry, 0)


def block_of(plan, blocks, index):
    return blocks[index] if plan.split else blocks[0].at[index]


def partner(plan, me, index):
    return jnp.bitwise_xor(me, index) if plan.split else index


def each_chunk(plan, hist, me, starts, visit):
    def begin(owner, at):
        starts[owner] = at
        return at + owner_rows(plan, hist, owner) // plan.half

    lax.fori_loop(0, plan.nodes, begin, jnp.int32(0))

    def block(number):
        dest = partner(plan, me, number)
        slot = jnp.int32(0)
        for head in range(plan.heads):
            owner = lax.rem(dest + plan.shift[head], plan.nodes)
            row = starts[owner]
            count = owner_rows(plan, hist, owner) // plan.half
            for index in range(2):

                @pl.when(index < count)
                def _(slot=slot, head=head, row=row, index=index):
                    visit(number, slot + index, head, row + index)

            slot = slot + count

    each_block(plan, block)


def chunk_rows(plan, index):
    return pl.ds(pl.multiple_of(index * plan.half, plan.half), plan.half)


def spread(plan, pos, first, second, hist, me, starts, ordered, wires):
    parts = []
    for head in range(plan.heads):
        span = slice(head * HEAD_DIM, (head + 1) * HEAD_DIM)
        parts += [first[span, :], second[span, :]]
    source = jnp.concatenate(parts, axis=0)
    for at in range(0, plan.rows, TILE):
        row = lax.broadcasted_iota(jnp.int32, (TILE, plan.rows), 0) + at
        pick = (row == pos).astype(jnp.bfloat16)
        ordered[at : at + TILE, :] = dot(pick, source, NT).astype(jnp.bfloat16)

    def clear(number):
        block = block_of(plan, wires, number)
        block[...] = jnp.zeros(block.shape, block.dtype)

    each_block(plan, clear)

    def visit(number, slot, head, row):
        block_of(plan, wires, number)[chunk_rows(plan, slot), :] = ordered[
            chunk_rows(plan, row), head * PAIR : (head + 1) * PAIR
        ]

    each_chunk(plan, hist, me, starts, visit)


def pack_first_kernel(plan, hist, me, ids, queries, keys, *refs):
    wires, (pos_out, starts, ordered) = refs[: plan.blocks], refs[plan.blocks :]
    rows = plan.rows
    rank = ids[...] * rows + lax.broadcasted_iota(jnp.int32, (1, rows), 1)
    rank = rank.astype(jnp.float32)
    column = jnp.broadcast_to(rank, (128, rows)).T
    parts = []
    for at in range(0, rows, 128):
        below = (column < rank[:, at : at + 128]).astype(jnp.float32)
        parts.append(jnp.sum(below, axis=0, keepdims=True))
    pos = jnp.concatenate(parts, axis=1).astype(jnp.int32)
    pos_out[...] = pos
    spread(plan, pos, queries[...], keys[...], hist, me[0], starts, ordered, wires)
    lane = lax.broadcasted_iota(jnp.int32, (NOTE, PAIR), 1)

    def note(number):
        dest = partner(plan, me[0], number)
        counts = jnp.zeros((NOTE, PAIR), jnp.int32)
        for head in range(plan.heads):
            owner = lax.rem(dest + plan.shift[head], plan.nodes)
            for cluster in range(plan.clusters):
                unit = head * plan.clusters + cluster
                count = hist[owner * plan.clusters + cluster]
                counts = jnp.where(lane == unit, count, counts)
        block_of(plan, wires, number)[plan.cap :, :] = counts.astype(jnp.float32).astype(
            jnp.bfloat16
        )

    each_block(plan, note)


def pack_second_kernel(plan, hist, me, pos, values, weight, cotangent, *refs):
    wires, (starts, ordered) = refs[: plan.blocks], refs[plan.blocks :]
    grad_in = dot(weight[...], cotangent[...]).astype(jnp.bfloat16)
    spread(plan, pos[...], values[...], grad_in, hist, me[0], starts, ordered, wires)


def unpack_kernel(plan, hist, me, pos, *refs):
    wires, (first, second, starts, ordered) = refs[: plan.blocks], refs[plan.blocks :]

    def visit(number, slot, head, row):
        ordered[head, chunk_rows(plan, row), :] = block_of(plan, wires, number)[
            chunk_rows(plan, slot), :
        ]

    each_chunk(plan, hist, me[0], starts, visit)
    source = jnp.concatenate(
        [ordered[head].astype(jnp.float32).T.astype(jnp.bfloat16) for head in range(plan.heads)],
        axis=0,
    )
    for at in range(0, plan.rows, TILE):
        row = lax.broadcasted_iota(jnp.int32, (plan.rows, TILE), 0)
        pick = (row == pos[:, at : at + TILE]).astype(jnp.bfloat16)
        out = dot(source, pick).astype(jnp.bfloat16)
        for head in range(plan.heads):
            span = slice(head * HEAD_DIM, (head + 1) * HEAD_DIM)
            first[span, at : at + TILE] = out[head * PAIR : head * PAIR + HEAD_DIM, :]
            second[span, at : at + TILE] = out[head * PAIR + HEAD_DIM : (head + 1) * PAIR, :]


def each_group(plan, table, visit):
    def source(index, places):
        at = index * plan.cap
        after = []
        for unit in range(plan.units):
            count = table[index, unit]
            visit(unit, places[unit], at, count)
            at = at + count
            after.append(places[unit] + count)
        return tuple(after)

    return lax.fori_loop(0, plan.nodes, source, (jnp.int32(0),) * plan.units)


def stage_rows(plan, index):
    start = index * plan.cap
    return pl.ds(start if plan.split else pl.multiple_of(start, plan.half), plan.cap)


def gather_units(plan, table, wires, stage, held, counts):
    flat = plan.nodes * plan.cap

    def widen(index):
        block = block_of(plan, wires, index)
        stage[stage_rows(plan, index), :] = block[0 : plan.cap, :].astype(jnp.float32)

    each_block(plan, widen)
    stage[flat : flat + SPARE, :] = jnp.zeros((SPARE, PAIR), jnp.float32)

    def visit(unit, place, at, count):
        def step(index, carry):
            held[unit, pl.ds(place + index * SPARE, SPARE), :] = stage[
                pl.ds(at + index * SPARE, SPARE), :
            ]
            return carry

        lax.fori_loop(0, pl.cdiv(count, SPARE), step, 0)

    totals = each_group(plan, table, visit)
    for unit in range(plan.units):
        counts[unit] = totals[unit]


def scatter_units(plan, table, held, stage, wires):
    def visit(unit, place, at, count):
        def step(index, carry):
            stage[pl.ds(at + index * SPARE, SPARE), :] = held[
                unit, pl.ds(place + index * SPARE, SPARE), :
            ]
            return carry

        lax.fori_loop(0, pl.cdiv(count, SPARE), step, 0)

    each_group(plan, table, visit)

    def narrow(index):
        block = block_of(plan, wires, index)
        block[...] = stage[stage_rows(plan, index), :].astype(jnp.bfloat16)

    each_block(plan, narrow)


def unit_rows(held, unit, count):
    row = lax.broadcasted_iota(jnp.int32, (CLUSTER, PAIR), 0)
    return jnp.where(row < count, held[unit, 0:CLUSTER, :], 0.0)


def weights_kernel(plan, *refs):
    wires, refs = refs[: plan.blocks], refs[plan.blocks :]
    (table, queries, keys_t, weights, noted, stage, held, counts, query_aug, key_aug, out, sems,
     table_sem) = refs

    def note(index):
        row = block_of(plan, wires, index)[plan.cap :, :].astype(jnp.float32)
        noted[pl.ds(index, 1), :] = row[0:1, :].astype(jnp.int32)

    each_block(plan, note)
    table_copy = pltpu.make_async_copy(noted, table, table_sem)
    table_copy.start()
    table_copy.wait()
    gather_units(plan, table, wires, stage, held, counts)
    factor = math.log2(math.e) / math.sqrt(HEAD_DIM)
    lane = lax.broadcasted_iota(jnp.int32, (CLUSTER, PAIR), 1)
    row = lax.broadcasted_iota(jnp.int32, (CLUSTER, PAIR), 0)

    def copy_out(step):
        slot = lax.rem(step, 2)
        return pltpu.make_async_copy(out.at[slot], weights.at[step], sems.at[slot])

    def one_unit(unit, step):
        count = counts[unit]
        both = unit_rows(held, unit, count)
        turned = pltpu.roll(both, HEAD_DIM, 1)
        queries[unit] = jnp.where(lane < HEAD_DIM, both, 0.0).astype(jnp.bfloat16)
        keys_t[unit] = turned.T[0:HEAD_DIM, :].astype(jnp.bfloat16)
        one = jnp.where(lane == HEAD_DIM, 1.0, 0.0)
        query_aug[...] = jnp.where(lane < HEAD_DIM, both, one).astype(jnp.bfloat16)
        outside = jnp.where(jnp.logical_and(lane == HEAD_DIM, row >= count), masked_score, 0.0)
        key_aug[...] = jnp.where(lane < HEAD_DIM, turned, outside).astype(jnp.bfloat16)

        def one_tile(tile, step):
            slot = lax.rem(step, 2)
            part = query_aug[pl.ds(pl.multiple_of(tile * TILE, TILE), TILE), :]
            scores = dot(key_aug[...], part, NT)
            raised = jnp.exp2((scores - jnp.max(scores, axis=0, keepdims=True)) * factor)
            share = 1.0 / jnp.sum(raised, axis=0, keepdims=True)

            @pl.when(step >= 2)
            def _():
                copy_out(step - 2).wait()

            out[slot] = (raised * share).astype(jnp.bfloat16)
            copy_out(step).start()
            return step + 1

        return lax.fori_loop(0, pl.cdiv(count, TILE), one_tile, step)

    steps = lax.fori_loop(0, plan.units, one_unit, jnp.int32(0))
    for back in (2, 1):

        @pl.when(steps >= back)
        def _(back=back):
            copy_out(steps - back).wait()


def queries_kernel(plan, table, *refs):
    wires, refs = refs[: plan.blocks], refs[plan.blocks :]
    keys_t, weights = refs[:2]
    wires_out, refs = refs[2 : 2 + plan.blocks], refs[2 + plan.blocks :]
    (dscores_out, grads, counts_out, stage, held, counts, value_turned, both_t, held_out, tiles,
     out, sems, out_sems) = refs
    gather_units(plan, table, wires, stage, held, counts)
    scale = 1.0 / math.sqrt(HEAD_DIM)
    lane = lax.broadcasted_iota(jnp.int32, (CLUSTER, PAIR), 1)
    steps = jnp.int32(0)
    for unit in range(plan.units):
        steps = steps + pl.cdiv(counts[unit], TILE)
        counts_out[unit] = counts[unit]

    def copy_in(step):
        slot = lax.rem(step, 2)
        return pltpu.make_async_copy(weights.at[step], tiles.at[slot], sems.at[slot])

    def copy_out(step):
        slot = lax.rem(step, 2)
        return pltpu.make_async_copy(out.at[slot], dscores_out.at[step], out_sems.at[slot])

    @pl.when(steps > 0)
    def _():
        copy_in(0).start()

    def one_unit(unit, step):
        count = counts[unit]
        both = unit_rows(held, unit, count)
        turned = pltpu.roll(both, HEAD_DIM, 1)
        value_turned[...] = jnp.where(lane >= HEAD_DIM, turned, 0.0).astype(jnp.bfloat16)
        grads[unit] = jnp.where(lane >= HEAD_DIM, both, 0.0).astype(jnp.bfloat16)
        both_t[...] = both.T.astype(jnp.bfloat16)

        def one_tile(tile, step):
            slot = lax.rem(step, 2)
            span = pl.ds(pl.multiple_of(tile * TILE, TILE), TILE)

            @pl.when(step + 1 < steps)
            def _():
                copy_in(step + 1).start()

            copy_in(step).wait()
            held_weights = tiles[slot]
            mixed = dot(both_t[0:HEAD_DIM, :], held_weights).astype(jnp.bfloat16)
            mixed = mixed.astype(jnp.float32)
            grad_t = both_t[HEAD_DIM:PAIR, span].astype(jnp.float32)
            delta = jnp.sum(grad_t * mixed, axis=0, keepdims=True)
            dweights = dot(value_turned[...], grads[unit, span, :], NT)
            dscores = (held_weights.astype(jnp.float32) * (dweights - delta)).astype(jnp.bfloat16)

            @pl.when(step >= 2)
            def _():
                copy_out(step - 2).wait()

            out[slot] = dscores
            copy_out(step).start()
            grad_query = dot(keys_t[unit], dscores) * scale
            held_out[unit, span, :] = jnp.concatenate([mixed, grad_query], axis=0).T
            return step + 1

        return lax.fori_loop(0, pl.cdiv(count, TILE), one_tile, step)

    lax.fori_loop(0, plan.units, one_unit, jnp.int32(0))
    scatter_units(plan, table, held_out, stage, wires_out)
    for back in (2, 1):

        @pl.when(steps >= back)
        def _(back=back):
            copy_out(steps - back).wait()


def keys_kernel(plan, table, counts, queries, grads, weights, dscores, *refs):
    wires_out, refs = refs[: plan.blocks], refs[plan.blocks :]
    stage, held_out, total, tiles, sems = refs
    scale = 1.0 / math.sqrt(HEAD_DIM)
    lane = lax.broadcasted_iota(jnp.int32, (CLUSTER, PAIR), 1)
    steps = jnp.int32(0)
    for unit in range(plan.units):
        steps = steps + pl.cdiv(counts[unit], TILE)

    def copies_in(step):
        slot = lax.rem(step, 2)
        return [
            pltpu.make_async_copy(
                source.at[step],
                tiles.at[slot, :, pl.ds(index * TILE, TILE)],
                sems.at[slot, index],
            )
            for index, source in enumerate((dscores, weights))
        ]

    @pl.when(steps > 0)
    def _():
        for copy in copies_in(0):
            copy.start()

    def one_unit(unit, step):
        total[...] = jnp.zeros_like(total)

        def one_tile(tile, step):
            slot = lax.rem(step, 2)
            span = pl.ds(pl.multiple_of(tile * TILE, TILE), TILE)

            @pl.when(step + 1 < steps)
            def _():
                for copy in copies_in(step + 1):
                    copy.start()

            for copy in copies_in(step):
                copy.wait()
            total[...] += dot(
                tiles[slot],
                jnp.concatenate([queries[unit, span, :], grads[unit, span, :]], axis=0),
            )
            return step + 1

        step = lax.fori_loop(0, pl.cdiv(counts[unit], TILE), one_tile, step)
        factor = jnp.where(lane < HEAD_DIM, scale, 1.0)
        held_out[unit, 0:CLUSTER, :] = total[...] * factor
        return step

    lax.fori_loop(0, plan.units, one_unit, jnp.int32(0))
    scatter_units(plan, table, held_out, stage, wires_out)


SCALARS = pl.BlockSpec(memory_space=pltpu.SMEM)
WHOLE = pl.BlockSpec(memory_space=pltpu.VMEM)
APART = pl.BlockSpec(memory_space=pl.ANY)


def call(kernel, plan, name, outs, out_specs, in_specs, scratch, flops, args):
    shapes = [jax.ShapeDtypeStruct(shape, dtype) for shape, dtype in outs]
    moved = sum(math.prod(shape) * jnp.dtype(dtype).itemsize for shape, dtype in outs)
    return pl.pallas_call(
        functools.partial(kernel, plan),
        out_shape=shapes,
        in_specs=in_specs,
        out_specs=out_specs,
        scratch_shapes=scratch,
        compiler_params=pltpu.CompilerParams(vmem_limit_bytes=VMEM_LIMIT),
        cost_estimate=pl.CostEstimate(flops=flops, bytes_accessed=2 * moved, transcendentals=0),
        name=name,
    )(*args)


def body(queries, key_rows, value_rows, out_weight, cotangent, cluster_ids, members, counts):
    nodes = lax.axis_size("node")
    width, rows = queries.shape
    plan = Plan(nodes, rows, width, members.shape[0])
    me = lax.axis_index("node").astype(jnp.int32).reshape(1)
    narrow = jnp.bfloat16
    home_shape = ((width, rows), narrow)
    starts = pltpu.SMEM((plan.nodes,), jnp.int32)
    ordered = pltpu.VMEM((rows, plan.heads * PAIR), narrow)
    stage = pltpu.VMEM((plan.nodes * plan.cap + SPARE, PAIR), jnp.float32)
    held = pltpu.VMEM((plan.units, CLUSTER + SPARE, PAIR), jnp.float32)
    unit_counts = pltpu.SMEM((plan.units,), jnp.int32)
    unit_block = pltpu.VMEM((CLUSTER, PAIR), narrow)
    tiles = pltpu.VMEM((2, CLUSTER, TILE), narrow)
    sems = pltpu.SemaphoreType.DMA((2,))
    lead = () if plan.split else (plan.nodes,)
    wire_shapes = [(lead + (plan.cap, PAIR), narrow)] * plan.blocks
    noted_shapes = [(lead + (plan.cap + NOTE, PAIR), narrow)] * plan.blocks
    wire_specs = [WHOLE] * plan.blocks

    def swap(wires):
        if not plan.split:
            return [lax.all_to_all(wires[0], "node", split_axis=0, concat_axis=0, tiled=True)]
        arrived = list(wires)
        for index in range(plan.nodes - 1, 0, -1):
            pairs = [(node, node ^ index) for node in range(plan.nodes)]
            arrived[index] = lax.ppermute(wires[index], "node", pairs)
        return arrived

    named = jnp.arange(plan.total, dtype=jnp.int32)[:, None] == cluster_ids[None, :]
    hist = jnp.sum(named, axis=1, dtype=jnp.int32)
    all_cotangent = lax.all_gather(cotangent, "head", axis=0, tiled=True)
    all_weight = lax.all_gather(out_weight, "head", axis=0, tiled=True)

    *wires, pos = call(
        pack_first_kernel, plan, "pack_queries_keys",
        noted_shapes + [((1, rows), jnp.int32)], wire_specs + [WHOLE],
        [SCALARS, SCALARS, WHOLE, WHOLE, WHOLE], [starts, ordered], 2 * 10**9,
        (hist, me, cluster_ids.reshape(1, rows), queries, key_rows),
    )
    query_wires = swap(wires)
    wires = call(
        pack_second_kernel, plan, "pack_values_grads", wire_shapes, wire_specs,
        [SCALARS, SCALARS, WHOLE, WHOLE, WHOLE, WHOLE], [starts, ordered], 2 * 10**9,
        (hist, me, pos, value_rows, out_weight, all_cotangent),
    )
    value_wires = swap(wires)

    unit_rows_shape = ((plan.units, CLUSTER, PAIR), narrow)
    unit_keys_shape = ((plan.units, HEAD_DIM, CLUSTER), narrow)
    tiles_shape = ((plan.tiles, CLUSTER, TILE), narrow)
    table_shape = (plan.nodes, PAIR)
    table, kept_queries, kept_keys, weights = call(
        weights_kernel, plan, "weights",
        [(table_shape, jnp.int32), unit_rows_shape, unit_keys_shape, tiles_shape],
        [SCALARS, WHOLE, WHOLE, APART], wire_specs,
        [pltpu.VMEM(table_shape, jnp.int32), stage, held, unit_counts, unit_block, unit_block,
         tiles, sems, pltpu.SemaphoreType.DMA], 10 * 10**9,
        query_wires,
    )
    *first_wires, dscores, kept_grads, counted = call(
        queries_kernel, plan, "attention_and_grad_queries",
        wire_shapes + [tiles_shape, unit_rows_shape, ((plan.units,), jnp.int32)],
        wire_specs + [APART, WHOLE, SCALARS], [SCALARS] + wire_specs + [WHOLE, APART],
        [stage, held, unit_counts, unit_block, pltpu.VMEM((PAIR, CLUSTER), narrow), held, tiles,
         tiles, sems, sems], 10 * 10**9,
        [table] + value_wires + [kept_keys, weights],
    )
    second_wires = call(
        keys_kernel, plan, "grad_keys_and_grad_values", wire_shapes, wire_specs,
        [SCALARS, SCALARS, WHOLE, WHOLE, APART, APART],
        [stage, held, pltpu.VMEM((CLUSTER, PAIR), jnp.float32),
         pltpu.VMEM((2, CLUSTER, 2 * TILE), narrow), pltpu.SemaphoreType.DMA((2, 2))], 10 * 10**9,
        [table, counted, kept_queries, kept_grads, weights, dscores],
    )

    def unpack(wires, name):
        return call(
            unpack_kernel, plan, name, [home_shape, home_shape], [WHOLE, WHOLE],
            [SCALARS, SCALARS, WHOLE] + wire_specs,
            [starts, pltpu.VMEM((plan.heads, rows, PAIR), narrow)], 2 * 10**9,
            [hist, me, pos] + wires,
        )

    attention, grad_queries = unpack(swap(first_wires), "unpack_attention_grad_queries")
    grad_keys, grad_values = unpack(swap(second_wires), "unpack_grad_keys_grad_values")
    all_attention = lax.all_gather(attention, "head", axis=0, tiled=True)
    mine = lax.dynamic_slice_in_dim(all_weight, lax.axis_index("head") * width, width, 1)
    output = lax.dot_general(
        mine, all_attention, (((0,), (0,)), ((), ())), preferred_element_type=jnp.float32
    ).astype(narrow)
    return (output, grad_queries, grad_keys, grad_values)


def solution(mesh):
    placed = (
        P("head", "node"),
        P("head", "node"),
        P("head", "node"),
        P("head", None),
        P("head", "node"),
        P("node"),
        P("node", None),
        P("node"),
    )
    return jax.shard_map(
        body,
        mesh=mesh,
        in_specs=placed,
        out_specs=(P("head", "node"), P("head", "node"), P("head", "node"), P("head", "node")),
        check_vma=False,
    )
```

time: 219 us -> 217 us (level)
  the two profiles are of different devices: /device:TPU:0 before, /device:TPU:12 now
where the time goes in v2:
time: 217 us; the launch traced here: 214 us
  Pallas kernels  75.7 us (35%)
  waiting for transfers between devices  73.8 us (34%)
  starting transfers between devices  44 us (20%)
  between operations  14.1 us (6%)
  matrix products  2.94 us (1%)
    pallas_call x7, Pallas kernels, call(): pl.pallas_call(functools.partial(kernel, plan), out_shape=shapes, in_spec...  75.7 us
    ppermute x28, waiting for transfers between devices, swap(): arrived[index] = lax.ppermute(wires[index], 'node', pairs)  71 us
    ppermute x28, starting transfers between devices, swap(): arrived[index] = lax.ppermute(wires[index], 'node', pairs)  43.9 us
  transfers between devices with their start and end apart: 31, of which 17 were waited for; matrix products, arithmetic and copies ran while one was open for 1% of the time, Pallas kernels for 35%

profile of v2, /device:TPU:12, one launch (start us, length us, event | category | flops | bytes accessed | tf_op | source)
XLA Modules:
  0.0 213.9 jit_solution(11417693537493506057)
XLA Ops:
  7.2 0.7 all-gather.6.cloned.1.call-update
  7.9 0.0 all-gather.4.cloned.1.call-start
  8.0 1.4 convert_reduce_fusion.hist
  9.3 5.0 %pack_queries_keys.1 = (bf16[656,128]{1,0:T(8,128)(2,1)}, bf16[656,128]{1,0:T(8,128)(2,1)}, bf16[656,128]{1,0:T(8,128)(2,1)}, bf16[656,128]{1,0:T(8,128)(2,1)}, ...) custom-call(s32[16]{0:T(128)} %convert_reduce_fusion.hist, ...), custom_call_target="tpu_custom_call" | custom-call | flops 2000000000 | bytes 2695168 | tf_op jit(solution)/shard_map/pack_queries_keys/pallas_call | solution.py:440
  14.3 1.5 collective-permute-start
  15.8 0.4 collective-permute-start.1
  16.2 1.5 collective-permute-start.2
  17.8 2.6 %collective-permute-start.3 = (bf16[656,128]{1,0:T(8,128)(2,1)}, bf16[656,128]{1,0:T(8,128)(2,1)S(1)}, u32[]{:S(2)}, u32[]{:S(2)}) collective-permute-start(bf16[656,128]{1,0:T(8,128)(2,1)} %get-tuple-element.53), channel_id=1, source_target_pairs={{0,16},{4,20},{8,24},{12,28},{16,0},{20,4},{24,8},{28,12},{1,17},{... | collective-permute-start | bytes 503816 | tf_op jit(solution)/shard_map/ppermute | solution.py:478
  20.4 1.3 collective-permute-start.4
  21.7 1.6 collective-permute-start.5
  23.2 4.1 %collective-permute-done.1.refs_2_ = bf16[656,128]{1,0:T(8,128)(2,1)S(1)} collective-permute-done((bf16[656,128]{1,0:T(8,128)(2,1)}, bf16[656,128]{1,0:T(8,128)(2,1)S(1)}, u32[]{:S(2)}, u32[]{:S(2)}) %collective-permute-start.1) | collective-permute-done | bytes 167968 | tf_op jit(solution)/shard_map/ppermute | solution.py:478
  27.3 0.1 collective-permute-start.6
  27.4 2.1 all-gather.6.cloned.1.call-done.cotangent
  29.4 5.2 %pack_values_grads.1 = (bf16[640,128]{1,0:T(8,128)(2,1)}, bf16[640,128]{1,0:T(8,128)(2,1)}, bf16[640,128]{1,0:T(8,128)(2,1)}, bf16[640,128]{1,0:T(8,128)(2,1)}, ...) custom-call(s32[16]{0:T(128)} %convert_reduce_fusion.hist, ...), custom_call_target="tpu_custom_call" | custom-call | flops 2000000000 | bytes 2621440 | tf_op jit(solution)/shard_map/pack_values_grads/pallas_call | solution.py:440
  34.6 2.5 %collective-permute-start.10 = (bf16[640,128]{1,0:T(8,128)(2,1)}, bf16[640,128]{1,0:T(8,128)(2,1)S(1)}, u32[]{:S(2)}, u32[]{:S(2)}) collective-permute-start(bf16[640,128]{1,0:T(8,128)(2,1)} %get-tuple-element.62), channel_id=1, source_target_pairs={{0,16},{4,20},{8,24},{12,28},{16,0},{20,4},{24,8},{28,12},{1,17},{... | collective-permute-start | bytes 491528 | tf_op jit(solution)/shard_map/ppermute | solution.py:478
  37.1 9.8 %collective-permute-done.3.refs_4_ = bf16[656,128]{1,0:T(8,128)(2,1)S(1)} collective-permute-done((bf16[656,128]{1,0:T(8,128)(2,1)}, bf16[656,128]{1,0:T(8,128)(2,1)S(1)}, u32[]{:S(2)}, u32[]{:S(2)}) %collective-permute-start.3) | collective-permute-done | bytes 167968 | tf_op jit(solution)/shard_map/ppermute | solution.py:478
  46.9 4.2 %collective-permute-start.11 = (bf16[640,128]{1,0:T(8,128)(2,1)}, bf16[640,128]{1,0:T(8,128)(2,1)S(1)}, u32[]{:S(2)}, u32[]{:S(2)}) collective-permute-start(bf16[640,128]{1,0:T(8,128)(2,1)} %get-tuple-element.63), channel_id=1, source_target_pairs={{0,20},{4,16},{8,28},{12,24},{16,4},{20,0},{24,12},{28,8},{1,21},{... | collective-permute-start | bytes 491528 | tf_op jit(solution)/shard_map/ppermute | solution.py:478
  51.1 0.0 all-gather.8.cloned.1.call-start
  51.2 0.1 collective-permute-start.12
  51.2 9.7 %collective-permute-done.5.refs_6_ = bf16[656,128]{1,0:T(8,128)(2,1)S(1)} collective-permute-done((bf16[656,128]{1,0:T(8,128)(2,1)}, bf16[656,128]{1,0:T(8,128)(2,1)S(1)}, u32[]{:S(2)}, u32[]{:S(2)}) %collective-permute-start.5) | collective-permute-done | bytes 167968 | tf_op jit(solution)/shard_map/ppermute | solution.py:478
  60.9 3.4 %collective-permute-start.13 = (bf16[640,128]{1,0:T(8,128)(2,1)}, bf16[640,128]{1,0:T(8,128)(2,1)S(1)}, u32[]{:S(2)}, u32[]{:S(2)}) collective-permute-start(bf16[640,128]{1,0:T(8,128)(2,1)} %get-tuple-element.65), channel_id=1, source_target_pairs={{0,28},{4,24},{8,20},{12,16},{16,12},{20,8},{24,4},{28,0},{1,29},{... | collective-permute-start | bytes 491528 | tf_op jit(solution)/shard_map/ppermute | solution.py:478
  64.4 0.5 collective-permute-done.6.refs_7_
  64.9 1.3 collective-permute-start.7
  66.2 2.0 collective-permute-done.10.refs_4_
  68.2 1.1 collective-permute-start.8
  69.3 2.4 %collective-permute-done.11.refs_5_ = bf16[640,128]{1,0:T(8,128)(2,1)S(1)} collective-permute-done((bf16[640,128]{1,0:T(8,128)(2,1)}, bf16[640,128]{1,0:T(8,128)(2,1)S(1)}, u32[]{:S(2)}, u32[]{:S(2)}) %collective-permute-start.11) | collective-permute-done | bytes 163872 | tf_op jit(solution)/shard_map/ppermute | solution.py:478
  71.7 1.9 collective-permute-start.9
  73.6 16.4 %weights.1 = (s32[8,128]{1,0:T(8,128)}, bf16[6,1024,128]{2,1,0:T(8,128)(2,1)}, bf16[6,64,1024]{2,1,0:T(8,128)(2,1)}, bf16[24,1024,256]{2,1,0:T(8,128)(2,1)}) custom-call(bf16[656,128]{1,0:T(8,128)(2,1)} %get-tuple-element.49.refs_0_, bf16[656,128]{1,0:T(8,128)(2,1)} %copy-done, bf16[656,128]{1,0:T(8,128)(2,1)} %copy-done.1, bf16[656,128]{1,0:T(8,128)(2,1)} %copy-done.2, ...), custom_call_target="tpu_custom_call" | custom-call | flops 10000000000 | bytes 29892608 | tf_op jit(solution)/shard_map/weights/pallas_call | solution.py:440
  90.2 0.6 copy-done.9
  90.8 0.0 copy-done.11
  90.8 0.1 copy-done.14
  90.9 0.1 copy-done.17
  90.9 0.1 copy-done.20
  91.0 22.7 %attention_and_grad_queries.1 = (bf16[640,128]{1,0:T(8,128)(2,1)}, bf16[640,128]{1,0:T(8,128)(2,1)}, bf16[640,128]{1,0:T(8,128)(2,1)}, bf16[640,128]{1,0:T(8,128...) custom-call(s32[8,128]{1,0:T(8,128)} %get-tuple-element.57.table, ...), custom_call_target="tpu_custom_call" | custom-call | flops 10000000000 | bytes 30933040 | tf_op jit(solution)/shard_map/attention_and_grad_queries/pallas_call | solution.py:440
  113.7 0.1 collective-permute-start.14
  113.8 0.1 collective-permute-start.15
  113.8 3.4 %collective-permute-start.16 = (bf16[640,128]{1,0:T(8,128)(2,1)}, bf16[640,128]{1,0:T(8,128)(2,1)S(1)}, u32[]{:S(2)}, u32[]{:S(2)}) collective-permute-start(bf16[640,128]{1,0:T(8,128)(2,1)} %get-tuple-element.71), channel_id=1, source_target_pairs={{0,12},{4,8},{8,4},{12,0},{16,28},{20,24},{24,20},{28,16},{1,13},{... | collective-permute-start | bytes 491528 | tf_op jit(solution)/shard_map/ppermute | solution.py:478
  117.2 2.8 %collective-permute-start.17 = (bf16[640,128]{1,0:T(8,128)(2,1)}, bf16[640,128]{1,0:T(8,128)(2,1)S(1)}, u32[]{:S(2)}, u32[]{:S(2)}) collective-permute-start(bf16[640,128]{1,0:T(8,128)(2,1)} %get-tuple-element.72), channel_id=1, source_target_pairs={{0,16},{4,20},{8,24},{12,28},{16,0},{20,4},{24,8},{28,12},{1,17},{... | collective-permute-start | bytes 491528 | tf_op jit(solution)/shard_map/ppermute | solution.py:478
  120.0 1.4 collective-permute-start.18
  121.4 2.3 %collective-permute-start.19 = (bf16[640,128]{1,0:T(8,128)(2,1)}, bf16[640,128]{1,0:T(8,128)(2,1)S(1)}, u32[]{:S(2)}, u32[]{:S(2)}) collective-permute-start(bf16[640,128]{1,0:T(8,128)(2,1)} %get-tuple-element.74), channel_id=1, source_target_pairs={{0,24},{4,28},{8,16},{12,20},{16,8},{20,12},{24,0},{28,4},{1,25},{... | collective-permute-start | bytes 491528 | tf_op jit(solution)/shard_map/ppermute | solution.py:478
  123.7 1.0 collective-permute-start.20
  124.7 1.3 collective-permute-done.16.refs_3_
  126.0 9.8 %collective-permute-done.17.refs_4_ = bf16[640,128]{1,0:T(8,128)(2,1)S(1)} collective-permute-done((bf16[640,128]{1,0:T(8,128)(2,1)}, bf16[640,128]{1,0:T(8,128)(2,1)S(1)}, u32[]{:S(2)}, u32[]{:S(2)}) %collective-permute-start.17) | collective-permute-done | bytes 163872 | tf_op jit(solution)/shard_map/ppermute | solution.py:478
  135.9 3.5 %collective-permute-done.18.refs_5_ = bf16[640,128]{1,0:T(8,128)(2,1)S(1)} collective-permute-done((bf16[640,128]{1,0:T(8,128)(2,1)}, bf16[640,128]{1,0:T(8,128)(2,1)S(1)}, u32[]{:S(2)}, u32[]{:S(2)}) %collective-permute-start.18) | collective-permute-done | bytes 163872 | tf_op jit(solution)/shard_map/ppermute | solution.py:478
  139.4 4.2 %collective-permute-done.19.refs_6_ = bf16[640,128]{1,0:T(8,128)(2,1)S(1)} collective-permute-done((bf16[640,128]{1,0:T(8,128)(2,1)}, bf16[640,128]{1,0:T(8,128)(2,1)S(1)}, u32[]{:S(2)}, u32[]{:S(2)}) %collective-permute-start.19) | collective-permute-done | bytes 163872 | tf_op jit(solution)/shard_map/ppermute | solution.py:478
  143.6 1.6 collective-permute-done.20.refs_7_
  145.2 0.6 copy-done.27
  145.8 4.4 %unpack_attention_grad_queries.1 = (bf16[192,1024]{1,0:T(8,128)(2,1)}, bf16[192,1024]{1,0:T(8,128)(2,1)}) custom-call(s32[16]{0:T(128)} %convert_reduce_fusion.hist, s32[1]{0:T(128)} %bitcast.me, s32[1,1024]{1,0:T(1,128)} %get-tuple-element.48.pos, bf16[640,128]{1,0:T(8,128)(2,1)} %get-tuple-element.68.refs_0_, bf16[640,128]{1,0:T(8,128)(2,1)} %copy-done.19, ...), custom_call_target="tpu_custom_call" | custom-call | flops 2000000000 | bytes 1572864 | tf_op jit(solution)/shard_map/unpack_attention_grad_queries/pallas_call | solution.py:440
  150.2 17.9 %grad_keys_and_grad_values.1 = (bf16[640,128]{1,0:T(8,128)(2,1)}, bf16[640,128]{1,0:T(8,128)(2,1)}, bf16[640,128]{1,0:T(8,128)(2,1)}, bf16[640,128]{1,0:T(8,128)...) custom-call(s32[8,128]{1,0:T(8,128)} %get-tuple-element.57.table, ...), custom_call_target="tpu_custom_call" | custom-call | flops 10000000000 | bytes 2621440 | tf_op jit(solution)/shard_map/grad_keys_and_grad_values/pallas_call | solution.py:440
  168.2 0.1 collective-permute-start.21
  168.2 0.1 collective-permute-start.22
  168.3 3.4 %collective-permute-start.23 = (bf16[640,128]{1,0:T(8,128)(2,1)}, bf16[640,128]{1,0:T(8,128)(2,1)S(1)}, u32[]{:S(2)}, u32[]{:S(2)}) collective-permute-start(bf16[640,128]{1,0:T(8,128)(2,1)} %get-tuple-element.85), channel_id=1, source_target_pairs={{0,12},{4,8},{8,4},{12,0},{16,28},{20,24},{24,20},{28,16},{1,13},{... | collective-permute-start | bytes 491528 | tf_op jit(solution)/shard_map/ppermute | solution.py:478
  171.7 0.5 collective-permute-start.24
  172.2 2.0 collective-permute-start.25
  174.2 2.4 %collective-permute-start.26 = (bf16[640,128]{1,0:T(8,128)(2,1)}, bf16[640,128]{1,0:T(8,128)(2,1)S(1)}, u32[]{:S(2)}, u32[]{:S(2)}) collective-permute-start(bf16[640,128]{1,0:T(8,128)(2,1)} %get-tuple-element.88), channel_id=1, source_target_pairs={{0,24},{4,28},{8,16},{12,20},{16,8},{20,12},{24,0},{28,4},{1,25},{... | collective-permute-start | bytes 491528 | tf_op jit(solution)/shard_map/ppermute | solution.py:478
  176.6 1.0 collective-permute-start.27
  177.6 2.9 %collective-permute-done.23.refs_3_ = bf16[640,128]{1,0:T(8,128)(2,1)S(1)} collective-permute-done((bf16[640,128]{1,0:T(8,128)(2,1)}, bf16[640,128]{1,0:T(8,128)(2,1)S(1)}, u32[]{:S(2)}, u32[]{:S(2)}) %collective-permute-start.23) | collective-permute-done | bytes 163872 | tf_op jit(solution)/shard_map/ppermute | solution.py:478
  180.5 8.7 %collective-permute-done.24.refs_4_ = bf16[640,128]{1,0:T(8,128)(2,1)S(1)} collective-permute-done((bf16[640,128]{1,0:T(8,128)(2,1)}, bf16[640,128]{1,0:T(8,128)(2,1)S(1)}, u32[]{:S(2)}, u32[]{:S(2)}) %collective-permute-start.24) | collective-permute-done | bytes 163872 | tf_op jit(solution)/shard_map/ppermute | solution.py:478
  189.2 3.5 %collective-permute-done.25.refs_5_ = bf16[640,128]{1,0:T(8,128)(2,1)S(1)} collective-permute-done((bf16[640,128]{1,0:T(8,128)(2,1)}, bf16[640,128]{1,0:T(8,128)(2,1)S(1)}, u32[]{:S(2)}, u32[]{:S(2)}) %collective-permute-start.25) | collective-permute-done | bytes 163872 | tf_op jit(solution)/shard_map/ppermute | solution.py:478
  192.7 5.3 %collective-permute-done.26.refs_6_ = bf16[640,128]{1,0:T(8,128)(2,1)S(1)} collective-permute-done((bf16[640,128]{1,0:T(8,128)(2,1)}, bf16[640,128]{1,0:T(8,128)(2,1)S(1)}, u32[]{:S(2)}, u32[]{:S(2)}) %collective-permute-start.26) | collective-permute-done | bytes 163872 | tf_op jit(solution)/shard_map/ppermute | solution.py:478
  198.1 1.5 collective-permute-done.27.refs_7_
  199.7 0.6 copy-done.23
  200.3 4.2 %unpack_grad_keys_grad_values.1 = (bf16[192,1024]{1,0:T(8,128)(2,1)}, bf16[192,1024]{1,0:T(8,128)(2,1)}) custom-call(s32[16]{0:T(128)} %convert_reduce_fusion.hist, s32[1]{0:T(128)} %bitcast.me, s32[1,1024]{1,0:T(1,128)} %get-tuple-element.48.pos, bf16[640,128]{1,0:T(8,128)(2,1)} %get-tuple-element.82.refs_0_, bf16[640,128]{1,0:T(8,128)(2,1)} %copy-done.10, ...), custom_call_target="tpu_custom_call" | custom-call | flops 2000000000 | bytes 1572864 | tf_op jit(solution)/shard_map/unpack_grad_keys_grad_values/pallas_call | solution.py:440
  204.5 2.9 %convolution_convert_fusion = bf16[192,1024]{1,0:T(8,128)(2,1)} fusion(bf16[768,1024]{1,0:T(8,128)(2,1)} %all-gather.8.cloned.1.call-done, bf16[768,768]{1,0:T(8,128)(2,1)} %all-gather.4.cloned.1.call-done, s32[]{:T(128)S(6)} %select_n.3), kind=kOutput, calls=%fused_computation | convolution fusion | flops 302186496 | bytes 2359300 | tf_op jit(solution)/shard_map/dot_general | solution.py:540
  (66 shorter events, 0.2 us)
Async XLA Ops:
  7.2 22.3 %all-gather.6.cloned.1.call-start = ((), (), s32[]{:S(2)}) async-start(), calls=%async_computation.1 | async-start | bytes 1966080 | tf_op jit(solution)/shard_map/all_gather | solution.py:483
  7.9 196.6 %all-gather.4.cloned.1.call-start = ((), (), s32[]{:S(2)}) async-start(), calls=%async_computation | async-start | bytes 1474560 | tf_op jit(solution)/shard_map/all_gather | solution.py:484
  14.3 7.3 %collective-permute-start = (bf16[656,128]{1,0:T(8,128)(2,1)}, bf16[656,128]{1,0:T(8,128)(2,1)S(1)}, u32[]{:S(2)}, u32[]{:S(2)}) collective-permute-start(bf16[656,128]{1,0:T(8,128)(2,1)} %get-tuple-element.50), channel_id=1, source_target_pairs={{0,4},{4,0},{8,12},{12,8},{16,20},{20,16},{24,28},{28,24},{1,5},{5... | collective-permute-start | bytes 503816 | tf_op jit(solution)/shard_map/ppermute | solution.py:478
  15.8 11.5 %collective-permute-start.1 = (bf16[656,128]{1,0:T(8,128)(2,1)}, bf16[656,128]{1,0:T(8,128)(2,1)S(1)}, u32[]{:S(2)}, u32[]{:S(2)}) collective-permute-start(bf16[656,128]{1,0:T(8,128)(2,1)} %get-tuple-element.51), channel_id=1, source_target_pairs={{0,8},{4,12},{8,0},{12,4},{16,24},{20,28},{24,16},{28,20},{1,9},{5... | collective-permute-start | bytes 503816 | tf_op jit(solution)/shard_map/ppermute | solution.py:478
  16.2 18.4 %collective-permute-start.2 = (bf16[656,128]{1,0:T(8,128)(2,1)}, bf16[656,128]{1,0:T(8,128)(2,1)S(1)}, u32[]{:S(2)}, u32[]{:S(2)}) collective-permute-start(bf16[656,128]{1,0:T(8,128)(2,1)} %get-tuple-element.52), channel_id=1, source_target_pairs={{0,12},{4,8},{8,4},{12,0},{16,28},{20,24},{24,20},{28,16},{1,13},{... | collective-permute-start | bytes 503816 | tf_op jit(solution)/shard_map/ppermute | solution.py:478
  17.8 29.1 %collective-permute-start.3 = (bf16[656,128]{1,0:T(8,128)(2,1)}, bf16[656,128]{1,0:T(8,128)(2,1)S(1)}, u32[]{:S(2)}, u32[]{:S(2)}) collective-permute-start(bf16[656,128]{1,0:T(8,128)(2,1)} %get-tuple-element.53), channel_id=1, source_target_pairs={{0,16},{4,20},{8,24},{12,28},{16,0},{20,4},{24,8},{28,12},{1,17},{... | collective-permute-start | bytes 503816 | tf_op jit(solution)/shard_map/ppermute | solution.py:478
  20.4 30.8 %collective-permute-start.4 = (bf16[656,128]{1,0:T(8,128)(2,1)}, bf16[656,128]{1,0:T(8,128)(2,1)S(1)}, u32[]{:S(2)}, u32[]{:S(2)}) collective-permute-start(bf16[656,128]{1,0:T(8,128)(2,1)} %get-tuple-element.54), channel_id=1, source_target_pairs={{0,20},{4,16},{8,28},{12,24},{16,4},{20,0},{24,12},{28,8},{1,21},{... | collective-permute-start | bytes 503816 | tf_op jit(solution)/shard_map/ppermute | solution.py:478
  21.7 13.0 %copy-start = (bf16[656,128]{1,0:T(8,128)(2,1)}, bf16[656,128]{1,0:T(8,128)(2,1)S(1)}, u32[]{:S(2)}) copy-start(bf16[656,128]{1,0:T(8,128)(2,1)S(1)} %collective-permute-done.refs_1_) | copy-start | bytes 503812
  21.7 39.3 %collective-permute-start.5 = (bf16[656,128]{1,0:T(8,128)(2,1)}, bf16[656,128]{1,0:T(8,128)(2,1)S(1)}, u32[]{:S(2)}, u32[]{:S(2)}) collective-permute-start(bf16[656,128]{1,0:T(8,128)(2,1)} %get-tuple-element.55), channel_id=1, source_target_pairs={{0,24},{4,28},{8,16},{12,20},{16,8},{20,12},{24,0},{28,4},{1,25},{... | collective-permute-start | bytes 503816 | tf_op jit(solution)/shard_map/ppermute | solution.py:478
  27.3 7.3 %copy-start.1 = (bf16[656,128]{1,0:T(8,128)(2,1)}, bf16[656,128]{1,0:T(8,128)(2,1)S(1)}, u32[]{:S(2)}) copy-start(bf16[656,128]{1,0:T(8,128)(2,1)S(1)} %collective-permute-done.1.refs_2_) | copy-start | bytes 503812
  27.3 37.6 %collective-permute-start.6 = (bf16[656,128]{1,0:T(8,128)(2,1)}, bf16[656,128]{1,0:T(8,128)(2,1)S(1)}, u32[]{:S(2)}, u32[]{:S(2)}) collective-permute-start(bf16[656,128]{1,0:T(8,128)(2,1)} %get-tuple-element.56), channel_id=1, source_target_pairs={{0,28},{4,24},{8,20},{12,16},{16,12},{20,8},{24,4},{28,0},{1,29},{... | collective-permute-start | bytes 503816 | tf_op jit(solution)/shard_map/ppermute | solution.py:478
  34.6 39.0 %copy-start.2 = (bf16[656,128]{1,0:T(8,128)(2,1)}, bf16[656,128]{1,0:T(8,128)(2,1)S(1)}, u32[]{:S(2)}) copy-start(bf16[656,128]{1,0:T(8,128)(2,1)S(1)} %collective-permute-done.2.refs_3_) | copy-start | bytes 503812
  34.6 33.6 %collective-permute-start.10 = (bf16[640,128]{1,0:T(8,128)(2,1)}, bf16[640,128]{1,0:T(8,128)(2,1)S(1)}, u32[]{:S(2)}, u32[]{:S(2)}) collective-permute-start(bf16[640,128]{1,0:T(8,128)(2,1)} %get-tuple-element.62), channel_id=1, source_target_pairs={{0,16},{4,20},{8,24},{12,28},{16,0},{20,4},{24,8},{28,12},{1,17},{... | collective-permute-start | bytes 491528 | tf_op jit(solution)/shard_map/ppermute | solution.py:478
  46.9 26.8 %copy-start.3 = (bf16[656,128]{1,0:T(8,128)(2,1)}, bf16[656,128]{1,0:T(8,128)(2,1)S(1)}, u32[]{:S(2)}) copy-start(bf16[656,128]{1,0:T(8,128)(2,1)S(1)} %collective-permute-done.3.refs_4_) | copy-start | bytes 503812
  46.9 24.8 %collective-permute-start.11 = (bf16[640,128]{1,0:T(8,128)(2,1)}, bf16[640,128]{1,0:T(8,128)(2,1)S(1)}, u32[]{:S(2)}, u32[]{:S(2)}) collective-permute-start(bf16[640,128]{1,0:T(8,128)(2,1)} %get-tuple-element.63), channel_id=1, source_target_pairs={{0,20},{4,16},{8,28},{12,24},{16,4},{20,0},{24,12},{28,8},{1,21},{... | collective-permute-start | bytes 491528 | tf_op jit(solution)/shard_map/ppermute | solution.py:478
  51.1 153.4 %all-gather.8.cloned.1.call-start = ((), (), s32[]{:S(2)}) async-start(), calls=%async_computation.2 | async-start | bytes 1966080 | tf_op jit(solution)/shard_map/all_gather | solution.py:538
  51.2 22.5 %copy-start.4 = (bf16[656,128]{1,0:T(8,128)(2,1)}, bf16[656,128]{1,0:T(8,128)(2,1)S(1)}, u32[]{:S(2)}) copy-start(bf16[656,128]{1,0:T(8,128)(2,1)S(1)} %collective-permute-done.4.refs_5_) | copy-start | bytes 503812
  51.2 38.9 %collective-permute-start.12 = (bf16[640,128]{1,0:T(8,128)(2,1)}, bf16[640,128]{1,0:T(8,128)(2,1)S(1)}, u32[]{:S(2)}, u32[]{:S(2)}) collective-permute-start(bf16[640,128]{1,0:T(8,128)(2,1)} %get-tuple-element.64), channel_id=1, source_target_pairs={{0,24},{4,28},{8,16},{12,20},{16,8},{20,12},{24,0},{28,4},{1,25},{... | collective-permute-start | bytes 491528 | tf_op jit(solution)/shard_map/ppermute | solution.py:478
  60.9 12.7 %copy-start.5 = (bf16[656,128]{1,0:T(8,128)(2,1)}, bf16[656,128]{1,0:T(8,128)(2,1)S(1)}, u32[]{:S(2)}) copy-start(bf16[656,128]{1,0:T(8,128)(2,1)S(1)} %collective-permute-done.5.refs_6_) | copy-start | bytes 503812
  60.9 29.2 %collective-permute-start.13 = (bf16[640,128]{1,0:T(8,128)(2,1)}, bf16[640,128]{1,0:T(8,128)(2,1)S(1)}, u32[]{:S(2)}, u32[]{:S(2)}) collective-permute-start(bf16[640,128]{1,0:T(8,128)(2,1)} %get-tuple-element.65), channel_id=1, source_target_pairs={{0,28},{4,24},{8,20},{12,16},{16,12},{20,8},{24,4},{28,0},{1,29},{... | collective-permute-start | bytes 491528 | tf_op jit(solution)/shard_map/ppermute | solution.py:478
  64.9 8.7 %copy-start.6 = (bf16[656,128]{1,0:T(8,128)(2,1)}, bf16[656,128]{1,0:T(8,128)(2,1)S(1)}, u32[]{:S(2)}) copy-start(bf16[656,128]{1,0:T(8,128)(2,1)S(1)} %collective-permute-done.6.refs_7_) | copy-start | bytes 503812
  64.9 25.2 %collective-permute-start.7 = (bf16[640,128]{1,0:T(8,128)(2,1)}, bf16[640,128]{1,0:T(8,128)(2,1)S(1)}, u32[]{:S(2)}, u32[]{:S(2)}) collective-permute-start(bf16[640,128]{1,0:T(8,128)(2,1)} %get-tuple-element.59), channel_id=1, source_target_pairs={{0,4},{4,0},{8,12},{12,8},{16,20},{20,16},{24,28},{28,24},{1,5},{5... | collective-permute-start | bytes 491528 | tf_op jit(solution)/shard_map/ppermute | solution.py:478
  68.2 21.9 %copy-start.7 = (bf16[640,128]{1,0:T(8,128)(2,1)}, bf16[640,128]{1,0:T(8,128)(2,1)S(1)}, u32[]{:S(2)}) copy-start(bf16[640,128]{1,0:T(8,128)(2,1)S(1)} %collective-permute-done.10.refs_4_) | copy-start | bytes 491524
  68.2 21.9 %collective-permute-start.8 = (bf16[640,128]{1,0:T(8,128)(2,1)}, bf16[640,128]{1,0:T(8,128)(2,1)S(1)}, u32[]{:S(2)}, u32[]{:S(2)}) collective-permute-start(bf16[640,128]{1,0:T(8,128)(2,1)} %get-tuple-element.60), channel_id=1, source_target_pairs={{0,8},{4,12},{8,0},{12,4},{16,24},{20,28},{24,16},{28,20},{1,9},{5... | collective-permute-start | bytes 491528 | tf_op jit(solution)/shard_map/ppermute | solution.py:478
  71.7 18.4 %copy-start.8 = (bf16[640,128]{1,0:T(8,128)(2,1)}, bf16[640,128]{1,0:T(8,128)(2,1)S(1)}, u32[]{:S(2)}) copy-start(bf16[640,128]{1,0:T(8,128)(2,1)S(1)} %collective-permute-done.11.refs_5_) | copy-start | bytes 491524
  71.7 18.5 %collective-permute-start.9 = (bf16[640,128]{1,0:T(8,128)(2,1)}, bf16[640,128]{1,0:T(8,128)(2,1)S(1)}, u32[]{:S(2)}, u32[]{:S(2)}) collective-permute-start(bf16[640,128]{1,0:T(8,128)(2,1)} %get-tuple-element.61), channel_id=1, source_target_pairs={{0,12},{4,8},{8,4},{12,0},{16,28},{20,24},{24,20},{28,16},{1,13},{... | collective-permute-start | bytes 491528 | tf_op jit(solution)/shard_map/ppermute | solution.py:478
  90.1 0.7 copy-start.9
  90.1 0.7 copy-start.11
  90.1 0.7 copy-start.14
  90.2 0.8 copy-start.17
  90.2 0.8 copy-start.20
  113.7 7.7 %collective-permute-start.14 = (bf16[640,128]{1,0:T(8,128)(2,1)}, bf16[640,128]{1,0:T(8,128)(2,1)S(1)}, u32[]{:S(2)}, u32[]{:S(2)}) collective-permute-start(bf16[640,128]{1,0:T(8,128)(2,1)} %get-tuple-element.69), channel_id=1, source_target_pairs={{0,4},{4,0},{8,12},{12,8},{16,20},{20,16},{24,28},{28,24},{1,5},{5... | collective-permute-start | bytes 491528 | tf_op jit(solution)/shard_map/ppermute | solution.py:478
  113.8 10.0 %collective-permute-start.15 = (bf16[640,128]{1,0:T(8,128)(2,1)}, bf16[640,128]{1,0:T(8,128)(2,1)S(1)}, u32[]{:S(2)}, u32[]{:S(2)}) collective-permute-start(bf16[640,128]{1,0:T(8,128)(2,1)} %get-tuple-element.70), channel_id=1, source_target_pairs={{0,8},{4,12},{8,0},{12,4},{16,24},{20,28},{24,16},{28,20},{1,9},{5... | collective-permute-start | bytes 491528 | tf_op jit(solution)/shard_map/ppermute | solution.py:478
  113.8 12.2 %collective-permute-start.16 = (bf16[640,128]{1,0:T(8,128)(2,1)}, bf16[640,128]{1,0:T(8,128)(2,1)S(1)}, u32[]{:S(2)}, u32[]{:S(2)}) collective-permute-start(bf16[640,128]{1,0:T(8,128)(2,1)} %get-tuple-element.71), channel_id=1, source_target_pairs={{0,12},{4,8},{8,4},{12,0},{16,28},{20,24},{24,20},{28,16},{1,13},{... | collective-permute-start | bytes 491528 | tf_op jit(solution)/shard_map/ppermute | solution.py:478
  117.2 18.6 %collective-permute-start.17 = (bf16[640,128]{1,0:T(8,128)(2,1)}, bf16[640,128]{1,0:T(8,128)(2,1)S(1)}, u32[]{:S(2)}, u32[]{:S(2)}) collective-permute-start(bf16[640,128]{1,0:T(8,128)(2,1)} %get-tuple-element.72), channel_id=1, source_target_pairs={{0,16},{4,20},{8,24},{12,28},{16,0},{20,4},{24,8},{28,12},{1,17},{... | collective-permute-start | bytes 491528 | tf_op jit(solution)/shard_map/ppermute | solution.py:478
  120.0 19.4 %collective-permute-start.18 = (bf16[640,128]{1,0:T(8,128)(2,1)}, bf16[640,128]{1,0:T(8,128)(2,1)S(1)}, u32[]{:S(2)}, u32[]{:S(2)}) collective-permute-start(bf16[640,128]{1,0:T(8,128)(2,1)} %get-tuple-element.73), channel_id=1, source_target_pairs={{0,20},{4,16},{8,28},{12,24},{16,4},{20,0},{24,12},{28,8},{1,21},{... | collective-permute-start | bytes 491528 | tf_op jit(solution)/shard_map/ppermute | solution.py:478
  121.4 23.8 %copy-start.19 = (bf16[640,128]{1,0:T(8,128)(2,1)}, bf16[640,128]{1,0:T(8,128)(2,1)S(1)}, u32[]{:S(2)}) copy-start(bf16[640,128]{1,0:T(8,128)(2,1)S(1)} %collective-permute-done.14.refs_1_) | copy-start | bytes 491524
  121.4 22.2 %collective-permute-start.19 = (bf16[640,128]{1,0:T(8,128)(2,1)}, bf16[640,128]{1,0:T(8,128)(2,1)S(1)}, u32[]{:S(2)}, u32[]{:S(2)}) collective-permute-start(bf16[640,128]{1,0:T(8,128)(2,1)} %get-tuple-element.74), channel_id=1, source_target_pairs={{0,24},{4,28},{8,16},{12,20},{16,8},{20,12},{24,0},{28,4},{1,25},{... | collective-permute-start | bytes 491528 | tf_op jit(solution)/shard_map/ppermute | solution.py:478
  123.7 21.4 %copy-start.21 = (bf16[640,128]{1,0:T(8,128)(2,1)}, bf16[640,128]{1,0:T(8,128)(2,1)S(1)}, u32[]{:S(2)}) copy-start(bf16[640,128]{1,0:T(8,128)(2,1)S(1)} %collective-permute-done.15.refs_2_) | copy-start | bytes 491524
  123.7 21.4 %collective-permute-start.20 = (bf16[640,128]{1,0:T(8,128)(2,1)}, bf16[640,128]{1,0:T(8,128)(2,1)S(1)}, u32[]{:S(2)}, u32[]{:S(2)}) collective-permute-start(bf16[640,128]{1,0:T(8,128)(2,1)} %get-tuple-element.75), channel_id=1, source_target_pairs={{0,28},{4,24},{8,20},{12,16},{16,12},{20,8},{24,4},{28,0},{1,29},{... | collective-permute-start | bytes 491528 | tf_op jit(solution)/shard_map/ppermute | solution.py:478
  126.0 19.2 %copy-start.22 = (bf16[640,128]{1,0:T(8,128)(2,1)}, bf16[640,128]{1,0:T(8,128)(2,1)S(1)}, u32[]{:S(2)}) copy-start(bf16[640,128]{1,0:T(8,128)(2,1)S(1)} %collective-permute-done.16.refs_3_) | copy-start | bytes 491524
  135.9 9.3 %copy-start.24 = (bf16[640,128]{1,0:T(8,128)(2,1)}, bf16[640,128]{1,0:T(8,128)(2,1)S(1)}, u32[]{:S(2)}) copy-start(bf16[640,128]{1,0:T(8,128)(2,1)S(1)} %collective-permute-done.17.refs_4_) | copy-start | bytes 491524
  139.4 5.8 %copy-start.25 = (bf16[640,128]{1,0:T(8,128)(2,1)}, bf16[640,128]{1,0:T(8,128)(2,1)S(1)}, u32[]{:S(2)}) copy-start(bf16[640,128]{1,0:T(8,128)(2,1)S(1)} %collective-permute-done.18.refs_5_) | copy-start | bytes 491524
  143.6 1.6 copy-start.26
  145.2 0.7 copy-start.27
  168.2 6.0 %collective-permute-start.21 = (bf16[640,128]{1,0:T(8,128)(2,1)}, bf16[640,128]{1,0:T(8,128)(2,1)S(1)}, u32[]{:S(2)}, u32[]{:S(2)}) collective-permute-start(bf16[640,128]{1,0:T(8,128)(2,1)} %get-tuple-element.83), channel_id=1, source_target_pairs={{0,4},{4,0},{8,12},{12,8},{16,20},{20,16},{24,28},{28,24},{1,5},{5... | collective-permute-start | bytes 491528 | tf_op jit(solution)/shard_map/ppermute | solution.py:478
  168.2 8.3 %collective-permute-start.22 = (bf16[640,128]{1,0:T(8,128)(2,1)}, bf16[640,128]{1,0:T(8,128)(2,1)S(1)}, u32[]{:S(2)}, u32[]{:S(2)}) collective-permute-start(bf16[640,128]{1,0:T(8,128)(2,1)} %get-tuple-element.84), channel_id=1, source_target_pairs={{0,8},{4,12},{8,0},{12,4},{16,24},{20,28},{24,16},{28,20},{1,9},{5... | collective-permute-start | bytes 491528 | tf_op jit(solution)/shard_map/ppermute | solution.py:478
  168.3 12.2 %collective-permute-start.23 = (bf16[640,128]{1,0:T(8,128)(2,1)}, bf16[640,128]{1,0:T(8,128)(2,1)S(1)}, u32[]{:S(2)}, u32[]{:S(2)}) collective-permute-start(bf16[640,128]{1,0:T(8,128)(2,1)} %get-tuple-element.85), channel_id=1, source_target_pairs={{0,12},{4,8},{8,4},{12,0},{16,28},{20,24},{24,20},{28,16},{1,13},{... | collective-permute-start | bytes 491528 | tf_op jit(solution)/shard_map/ppermute | solution.py:478
  171.7 17.5 %collective-permute-start.24 = (bf16[640,128]{1,0:T(8,128)(2,1)}, bf16[640,128]{1,0:T(8,128)(2,1)S(1)}, u32[]{:S(2)}, u32[]{:S(2)}) collective-permute-start(bf16[640,128]{1,0:T(8,128)(2,1)} %get-tuple-element.86), channel_id=1, source_target_pairs={{0,16},{4,20},{8,24},{12,28},{16,0},{20,4},{24,8},{28,12},{1,17},{... | collective-permute-start | bytes 491528 | tf_op jit(solution)/shard_map/ppermute | solution.py:478
  172.2 20.6 %collective-permute-start.25 = (bf16[640,128]{1,0:T(8,128)(2,1)}, bf16[640,128]{1,0:T(8,128)(2,1)S(1)}, u32[]{:S(2)}, u32[]{:S(2)}) collective-permute-start(bf16[640,128]{1,0:T(8,128)(2,1)} %get-tuple-element.87), channel_id=1, source_target_pairs={{0,20},{4,16},{8,28},{12,24},{16,4},{20,0},{24,12},{28,8},{1,21},{... | collective-permute-start | bytes 491528 | tf_op jit(solution)/shard_map/ppermute | solution.py:478
  174.1 25.5 %copy-start.10 = (bf16[640,128]{1,0:T(8,128)(2,1)}, bf16[640,128]{1,0:T(8,128)(2,1)S(1)}, u32[]{:S(2)}) copy-start(bf16[640,128]{1,0:T(8,128)(2,1)S(1)} %collective-permute-done.21.refs_1_) | copy-start | bytes 491524
  174.2 23.9 %collective-permute-start.26 = (bf16[640,128]{1,0:T(8,128)(2,1)}, bf16[640,128]{1,0:T(8,128)(2,1)S(1)}, u32[]{:S(2)}, u32[]{:S(2)}) collective-permute-start(bf16[640,128]{1,0:T(8,128)(2,1)} %get-tuple-element.88), channel_id=1, source_target_pairs={{0,24},{4,28},{8,16},{12,20},{16,8},{20,12},{24,0},{28,4},{1,25},{... | collective-permute-start | bytes 491528 | tf_op jit(solution)/shard_map/ppermute | solution.py:478
  176.6 23.1 %copy-start.12 = (bf16[640,128]{1,0:T(8,128)(2,1)}, bf16[640,128]{1,0:T(8,128)(2,1)S(1)}, u32[]{:S(2)}) copy-start(bf16[640,128]{1,0:T(8,128)(2,1)S(1)} %collective-permute-done.22.refs_2_) | copy-start | bytes 491524
  176.6 23.1 %collective-permute-start.27 = (bf16[640,128]{1,0:T(8,128)(2,1)}, bf16[640,128]{1,0:T(8,128)(2,1)S(1)}, u32[]{:S(2)}, u32[]{:S(2)}) collective-permute-start(bf16[640,128]{1,0:T(8,128)(2,1)} %get-tuple-element.89), channel_id=1, source_target_pairs={{0,28},{4,24},{8,20},{12,16},{16,12},{20,8},{24,4},{28,0},{1,29},{... | collective-permute-start | bytes 491528 | tf_op jit(solution)/shard_map/ppermute | solution.py:478
  180.5 19.2 %copy-start.13 = (bf16[640,128]{1,0:T(8,128)(2,1)}, bf16[640,128]{1,0:T(8,128)(2,1)S(1)}, u32[]{:S(2)}) copy-start(bf16[640,128]{1,0:T(8,128)(2,1)S(1)} %collective-permute-done.23.refs_3_) | copy-start | bytes 491524
  189.2 10.4 %copy-start.15 = (bf16[640,128]{1,0:T(8,128)(2,1)}, bf16[640,128]{1,0:T(8,128)(2,1)S(1)}, u32[]{:S(2)}) copy-start(bf16[640,128]{1,0:T(8,128)(2,1)S(1)} %collective-permute-done.24.refs_4_) | copy-start | bytes 491524
  192.7 6.9 %copy-start.16 = (bf16[640,128]{1,0:T(8,128)(2,1)}, bf16[640,128]{1,0:T(8,128)(2,1)S(1)}, u32[]{:S(2)}) copy-start(bf16[640,128]{1,0:T(8,128)(2,1)S(1)} %collective-permute-done.25.refs_5_) | copy-start | bytes 491524
  198.1 1.6 copy-start.18
  199.6 0.7 copy-start.23
Sparse Core Ops, SparseCore 0:
  9.6 19.8 all-gather.5
  51.2 14.6 all-gather.3
  150.3 18.5 all-gather.7

commit v3 on v2

--- a/solution.py
+++ b/solution.py
@@ -14,6 +14,12 @@
 TILE = 256
 SPARE = 32
 NOTE = 16
+MASKS = (
+    (7, 6, 5, 4, 3, 2, 1),
+    (5, 4, 3, 2, 1, 7, 6),
+    (2, 1, 7, 6, 5, 4, 3),
+    (1, 7, 6, 5, 4, 3, 2),
+)
 VMEM_LIMIT = 56 * 1024 * 1024
 masked_score = -1e30
 
@@ -26,7 +32,7 @@
 
 
 class Plan:
-    def __init__(self, nodes, rows, width, clusters):
+    def __init__(self, nodes, rows, width, clusters, masks):
         self.nodes = nodes
         self.rows = rows
         self.width = width
@@ -40,7 +46,8 @@
         self.shift = tuple(3 * head % nodes for head in range(self.heads))
         self.units = self.heads * clusters
         self.tiles = self.units * (CLUSTER // TILE)
-        self.split = nodes <= 16 and nodes & (nodes - 1) == 0
+        self.split = nodes == len(masks) + 1
+        self.masks = (0,) + masks
         self.blocks = nodes if self.split else 1
 
 
@@ -61,7 +68,7 @@
 
 
 def partner(plan, me, index):
-    return jnp.bitwise_xor(me, index) if plan.split else index
+    return jnp.bitwise_xor(me, plan.masks[index]) if plan.split else index
 
 
 def each_chunk(plan, hist, me, starts, visit):
@@ -179,33 +186,35 @@
 
 
 def each_group(plan, table, visit):
-    def source(index, places):
-        at = index * plan.cap
+    def source(line, block, places):
+        at = block * (plan.cap + SPARE)
         after = []
         for unit in range(plan.units):
-            count = table[index, unit]
+            count = table[line, unit]
             visit(unit, places[unit], at, count)
             at = at + count
             after.append(places[unit] + count)
         return tuple(after)
 
-    return lax.fori_loop(0, plan.nodes, source, (jnp.int32(0),) * plan.units)
+    places = (jnp.int32(0),) * plan.units
+    if not plan.split:
+        return lax.fori_loop(0, plan.nodes, lambda at, places: source(at, at, places), places)
+    for mask in range(plan.nodes):
+        places = source(mask, plan.masks.index(mask), places)
+    return places
 
 
 def stage_rows(plan, index):
-    start = index * plan.cap
+    start = index * (plan.cap + SPARE)
     return pl.ds(start if plan.split else pl.multiple_of(start, plan.half), plan.cap)
 
 
 def gather_units(plan, table, wires, stage, held, counts):
-    flat = plan.nodes * plan.cap
-
     def widen(index):
         block = block_of(plan, wires, index)
         stage[stage_rows(plan, index), :] = block[0 : plan.cap, :].astype(jnp.float32)
 
     each_block(plan, widen)
-    stage[flat : flat + SPARE, :] = jnp.zeros((SPARE, PAIR), jnp.float32)
 
     def visit(unit, place, at, count):
         def step(index, carry):
@@ -252,7 +261,8 @@
 
     def note(index):
         row = block_of(plan, wires, index)[plan.cap :, :].astype(jnp.float32)
-        noted[pl.ds(index, 1), :] = row[0:1, :].astype(jnp.int32)
+        line = plan.masks[index] if plan.split else index
+        noted[pl.ds(line, 1), :] = row[0:1, :].astype(jnp.int32)
 
     each_block(plan, note)
     table_copy = pltpu.make_async_copy(noted, table, table_sem)
@@ -303,7 +313,8 @@
             copy_out(steps - back).wait()
 
 
-def queries_kernel(plan, table, *refs):
+def queries_kernel(plans, table, *refs):
+    plan, plan_out = plans
     wires, refs = refs[: plan.blocks], refs[plan.blocks :]
     keys_t, weights = refs[:2]
     wires_out, refs = refs[2 : 2 + plan.blocks], refs[2 + plan.blocks :]
@@ -367,7 +378,7 @@
         return lax.fori_loop(0, pl.cdiv(count, TILE), one_tile, step)
 
     lax.fori_loop(0, plan.units, one_unit, jnp.int32(0))
-    scatter_units(plan, table, held_out, stage, wires_out)
+    scatter_units(plan_out, table, held_out, stage, wires_out)
     for back in (2, 1):
 
         @pl.when(steps >= back)
@@ -452,29 +463,38 @@
 def body(queries, key_rows, value_rows, out_weight, cotangent, cluster_ids, members, counts):
     nodes = lax.axis_size("node")
     width, rows = queries.shape
-    plan = Plan(nodes, rows, width, members.shape[0])
+    query_plan, value_plan, first_plan, second_plan = [
+        Plan(nodes, rows, width, members.shape[0], masks) for masks in MASKS
+    ]
+    plan = query_plan
     me = lax.axis_index("node").astype(jnp.int32).reshape(1)
     narrow = jnp.bfloat16
     home_shape = ((width, rows), narrow)
     starts = pltpu.SMEM((plan.nodes,), jnp.int32)
     ordered = pltpu.VMEM((rows, plan.heads * PAIR), narrow)
-    stage = pltpu.VMEM((plan.nodes * plan.cap + SPARE, PAIR), jnp.float32)
+    stage = pltpu.VMEM((plan.nodes * (plan.cap + SPARE), PAIR), jnp.float32)
     held = pltpu.VMEM((plan.units, CLUSTER + SPARE, PAIR), jnp.float32)
     unit_counts = pltpu.SMEM((plan.units,), jnp.int32)
     unit_block = pltpu.VMEM((CLUSTER, PAIR), narrow)
     tiles = pltpu.VMEM((2, CLUSTER, TILE), narrow)
     sems = pltpu.SemaphoreType.DMA((2,))
-    lead = () if plan.split else (plan.nodes,)
-    wire_shapes = [(lead + (plan.cap, PAIR), narrow)] * plan.blocks
-    noted_shapes = [(lead + (plan.cap + NOTE, PAIR), narrow)] * plan.blocks
-    wire_specs = [WHOLE] * plan.blocks
-
-    def swap(wires):
+
+    def blocks(plan, extra=0):
+        lead = () if plan.split else (plan.nodes,)
+        return [(lead + (plan.cap + extra, PAIR), narrow)] * plan.blocks
+
+    def specs(plan):
+        return [WHOLE] * plan.blocks
+
+    def after(value, *others):
+        return lax.optimization_barrier((value,) + others)[0]
+
+    def swap(plan, wires):
         if not plan.split:
             return [lax.all_to_all(wires[0], "node", split_axis=0, concat_axis=0, tiled=True)]
         arrived = list(wires)
-        for index in range(plan.nodes - 1, 0, -1):
-            pairs = [(node, node ^ index) for node in range(plan.nodes)]
+        for index in range(1, plan.nodes):
+            pairs = [(node, node ^ plan.masks[index]) for node in range(plan.nodes)]
             arrived[index] = lax.ppermute(wires[index], "node", pairs)
         return arrived
 
@@ -485,17 +505,18 @@
 
     *wires, pos = call(
         pack_first_kernel, plan, "pack_queries_keys",
-        noted_shapes + [((1, rows), jnp.int32)], wire_specs + [WHOLE],
+        blocks(plan, NOTE) + [((1, rows), jnp.int32)], specs(plan) + [WHOLE],
         [SCALARS, SCALARS, WHOLE, WHOLE, WHOLE], [starts, ordered], 2 * 10**9,
         (hist, me, cluster_ids.reshape(1, rows), queries, key_rows),
     )
-    query_wires = swap(wires)
+    query_wires = swap(plan, wires)
     wires = call(
-        pack_second_kernel, plan, "pack_values_grads", wire_shapes, wire_specs,
+        pack_second_kernel, value_plan, "pack_values_grads", blocks(plan), specs(plan),
         [SCALARS, SCALARS, WHOLE, WHOLE, WHOLE, WHOLE], [starts, ordered], 2 * 10**9,
         (hist, me, pos, value_rows, out_weight, all_cotangent),
     )
-    value_wires = swap(wires)
+    value_wires = swap(value_plan, wires)
+    query_wires = [after(query_wires[0], wires[0])] + query_wires[1:]
 
     unit_rows_shape = ((plan.units, CLUSTER, PAIR), narrow)
     unit_keys_shape = ((plan.units, HEAD_DIM, CLUSTER), narrow)
@@ -504,37 +525,40 @@
     table, kept_queries, kept_keys, weights = call(
         weights_kernel, plan, "weights",
         [(table_shape, jnp.int32), unit_rows_shape, unit_keys_shape, tiles_shape],
-        [SCALARS, WHOLE, WHOLE, APART], wire_specs,
+        [SCALARS, WHOLE, WHOLE, APART], specs(plan),
         [pltpu.VMEM(table_shape, jnp.int32), stage, held, unit_counts, unit_block, unit_block,
          tiles, sems, pltpu.SemaphoreType.DMA], 10 * 10**9,
         query_wires,
     )
     *first_wires, dscores, kept_grads, counted = call(
-        queries_kernel, plan, "attention_and_grad_queries",
-        wire_shapes + [tiles_shape, unit_rows_shape, ((plan.units,), jnp.int32)],
-        wire_specs + [APART, WHOLE, SCALARS], [SCALARS] + wire_specs + [WHOLE, APART],
+        queries_kernel, (value_plan, first_plan), "attention_and_grad_queries",
+        blocks(plan) + [tiles_shape, unit_rows_shape, ((plan.units,), jnp.int32)],
+        specs(plan) + [APART, WHOLE, SCALARS], [SCALARS] + specs(plan) + [WHOLE, APART],
         [stage, held, unit_counts, unit_block, pltpu.VMEM((PAIR, CLUSTER), narrow), held, tiles,
          tiles, sems, sems], 10 * 10**9,
         [table] + value_wires + [kept_keys, weights],
     )
     second_wires = call(
-        keys_kernel, plan, "grad_keys_and_grad_values", wire_shapes, wire_specs,
+        keys_kernel, second_plan, "grad_keys_and_grad_values", blocks(plan), specs(plan),
         [SCALARS, SCALARS, WHOLE, WHOLE, APART, APART],
         [stage, held, pltpu.VMEM((CLUSTER, PAIR), jnp.float32),
          pltpu.VMEM((2, CLUSTER, 2 * TILE), narrow), pltpu.SemaphoreType.DMA((2, 2))], 10 * 10**9,
         [table, counted, kept_queries, kept_grads, weights, dscores],
     )
 
-    def unpack(wires, name):
+    def unpack(plan, wires, name):
         return call(
             unpack_kernel, plan, name, [home_shape, home_shape], [WHOLE, WHOLE],
-            [SCALARS, SCALARS, WHOLE] + wire_specs,
+            [SCALARS, SCALARS, WHOLE] + specs(plan),
             [starts, pltpu.VMEM((plan.heads, rows, PAIR), narrow)], 2 * 10**9,
             [hist, me, pos] + wires,
         )
 
-    attention, grad_queries = unpack(swap(first_wires), "unpack_attention_grad_queries")
-    grad_keys, grad_values = unpack(swap(second_wires), "unpack_grad_keys_grad_values")
+    first_back = swap(first_plan, first_wires)
+    second_back = swap(second_plan, second_wires)
+    first_back = [after(first_back[0], second_wires[0])] + first_back[1:]
+    attention, grad_queries = unpack(first_plan, first_back, "unpack_attention_grad_queries")
+    grad_keys, grad_values = unpack(second_plan, second_back, "unpack_grad_keys_grad_values")
     all_attention = lax.all_gather(attention, "head", axis=0, tiled=True)
     mine = lax.dynamic_slice_in_dim(all_weight, lax.axis_index("head") * width, width, 1)
     output = lax.dot_general(

time: 217 us -> 186 us (0.86)
  the two profiles are of different devices: /device:TPU:12 before, /device:TPU:0 now
where the time goes in v3:
time: 186 us
  Pallas kernels  78.1 us (42%)
  starting transfers between devices  66.3 us (36%)
  waiting for transfers between devices  20.2 us (11%)
  between operations  14.1 us (8%)
  matrix products  2.94 us (2%)
  local copies, waits for them, and re-layouts  2.79 us (2%)
    pallas_call x7, Pallas kernels, call(): pl.pallas_call(functools.partial(kernel, plan), out_shape=shapes, in_spec...  78.1 us
    ppermute x28, starting transfers between devices, swap(): arrived[index] = lax.ppermute(wires[index], 'node', pairs)  66.2 us
    ppermute x28, waiting for transfers between devices, swap(): arrived[index] = lax.ppermute(wires[index], 'node', pairs)  19.5 us
  transfers between devices with their start and end apart: 31, of which 8 were waited for; matrix products, arithmetic and copies ran while one was open for 1% of the time, Pallas kernels for 42%

profile of v3, /device:TPU:0, one launch (start us, length us, event | category | flops | bytes accessed | tf_op | source)
XLA Modules:
  0.0 185.8 jit_solution(2549283173616516757)
XLA Ops:
  7.2 0.0 all-gather.6.cloned.1.call-start
  7.2 0.7 all-gather.6.cloned.1.call-update
  7.9 0.0 all-gather.4.cloned.1.call-start
  8.0 1.3 convert_reduce_fusion.hist
  9.3 5.0 %pack_queries_keys.1 = (bf16[656,128]{1,0:T(8,128)(2,1)}, bf16[656,128]{1,0:T(8,128)(2,1)}, bf16[656,128]{1,0:T(8,128)(2,1)}, bf16[656,128]{1,0:T(8,128)(2,1)}, ...) custom-call(s32[16]{0:T(128)} %convert_reduce_fusion.hist, ...), custom_call_target="tpu_custom_call" | custom-call | flops 2000000000 | bytes 2695168 | tf_op jit(solution)/shard_map/pack_queries_keys/pallas_call | solution.py:451
  14.3 6.0 %collective-permute-start = (bf16[656,128]{1,0:T(8,128)(2,1)}, bf16[656,128]{1,0:T(8,128)(2,1)S(1)}, u32[]{:S(2)}, u32[]{:S(2)}) collective-permute-start(bf16[656,128]{1,0:T(8,128)(2,1)} %get-tuple-element.54), channel_id=1, source_target_pairs={{0,28},{4,24},{8,20},{12,16},{16,12},{20,8},{24,4},{28,0},{1,29},{... | collective-permute-start | bytes 503816 | tf_op jit(solution)/shard_map/ppermute | solution.py:498
  20.2 0.2 collective-permute-start.1
  20.5 0.8 collective-permute-start.2
  21.2 2.0 %collective-permute-start.3 = (bf16[656,128]{1,0:T(8,128)(2,1)}, bf16[656,128]{1,0:T(8,128)(2,1)S(1)}, u32[]{:S(2)}, u32[]{:S(2)}) collective-permute-start(bf16[656,128]{1,0:T(8,128)(2,1)} %get-tuple-element.57), channel_id=1, source_target_pairs={{0,16},{4,20},{8,24},{12,28},{16,0},{20,4},{24,8},{28,12},{1,17},{... | collective-permute-start | bytes 503816 | tf_op jit(solution)/shard_map/ppermute | solution.py:498
  23.2 2.3 %collective-permute-start.4 = (bf16[656,128]{1,0:T(8,128)(2,1)}, bf16[656,128]{1,0:T(8,128)(2,1)S(1)}, u32[]{:S(2)}, u32[]{:S(2)}) collective-permute-start(bf16[656,128]{1,0:T(8,128)(2,1)} %get-tuple-element.58), channel_id=1, source_target_pairs={{0,12},{4,8},{8,4},{12,0},{16,28},{20,24},{24,20},{28,16},{1,13},{... | collective-permute-start | bytes 503816 | tf_op jit(solution)/shard_map/ppermute | solution.py:498
  25.5 0.0 collective-permute-done.refs_1_
  25.5 15.0 %collective-permute-start.5 = (bf16[656,128]{1,0:T(8,128)(2,1)}, bf16[656,128]{1,0:T(8,128)(2,1)S(1)}, u32[]{:S(2)}, u32[]{:S(2)}) collective-permute-start(bf16[656,128]{1,0:T(8,128)(2,1)} %get-tuple-element.59), channel_id=1, source_target_pairs={{0,8},{4,12},{8,0},{12,4},{16,24},{20,28},{24,16},{28,20},{1,9},{5... | collective-permute-start | bytes 503816 | tf_op jit(solution)/shard_map/ppermute | solution.py:498
  40.5 1.4 collective-permute-start.6
  41.9 5.2 %pack_values_grads.1 = (bf16[640,128]{1,0:T(8,128)(2,1)}, bf16[640,128]{1,0:T(8,128)(2,1)}, bf16[640,128]{1,0:T(8,128)(2,1)}, bf16[640,128]{1,0:T(8,128)(2,1)}, ...) custom-call(s32[16]{0:T(128)} %convert_reduce_fusion.hist, ...), custom_call_target="tpu_custom_call" | custom-call | flops 2000000000 | bytes 2621440 | tf_op jit(solution)/shard_map/pack_values_grads/pallas_call | solution.py:451
  47.1 0.0 copy-start.2
  47.1 2.1 %collective-permute-start.10 = (bf16[640,128]{1,0:T(8,128)(2,1)}, bf16[640,128]{1,0:T(8,128)(2,1)S(1)}, u32[]{:S(2)}, u32[]{:S(2)}) collective-permute-start(bf16[640,128]{1,0:T(8,128)(2,1)} %get-tuple-element.65), channel_id=1, source_target_pairs={{0,8},{4,12},{8,0},{12,4},{16,24},{20,28},{24,16},{28,20},{1,9},{5... | collective-permute-start | bytes 491528 | tf_op jit(solution)/shard_map/ppermute | solution.py:498
  49.2 0.0 collective-permute-done.3.refs_4_
  49.2 1.4 collective-permute-start.11
  50.7 0.0 all-gather.4.cloned.1.call-update
  50.7 0.0 all-gather.8.cloned.1.call-start
  50.7 0.0 collective-permute-done.4.refs_5_
  50.7 2.8 %collective-permute-start.12 = (bf16[640,128]{1,0:T(8,128)(2,1)}, bf16[640,128]{1,0:T(8,128)(2,1)S(1)}, u32[]{:S(2)}, u32[]{:S(2)}) collective-permute-start(bf16[640,128]{1,0:T(8,128)(2,1)} %get-tuple-element.67), channel_id=1, source_target_pairs={{0,28},{4,24},{8,20},{12,16},{16,12},{20,8},{24,4},{28,0},{1,29},{... | collective-permute-start | bytes 491528 | tf_op jit(solution)/shard_map/ppermute | solution.py:498
  53.5 0.0 collective-permute-done.5.refs_6_
  53.5 1.2 collective-permute-start.13
  54.7 0.4 collective-permute-start.7
  55.1 3.4 %collective-permute-start.8 = (bf16[640,128]{1,0:T(8,128)(2,1)}, bf16[640,128]{1,0:T(8,128)(2,1)S(1)}, u32[]{:S(2)}, u32[]{:S(2)}) collective-permute-start(bf16[640,128]{1,0:T(8,128)(2,1)} %get-tuple-element.63), channel_id=1, source_target_pairs={{0,16},{4,20},{8,24},{12,28},{16,0},{20,4},{24,8},{28,12},{1,17},{... | collective-permute-start | bytes 491528 | tf_op jit(solution)/shard_map/ppermute | solution.py:498
  58.5 0.4 collective-permute-start.9
  59.0 16.6 %weights.1 = (s32[8,128]{1,0:T(8,128)}, bf16[6,1024,128]{2,1,0:T(8,128)(2,1)}, bf16[6,64,1024]{2,1,0:T(8,128)(2,1)}, bf16[24,1024,256]{2,1,0:T(8,128)(2,1)}) custom-call(bf16[656,128]{1,0:T(8,128)(2,1)} %get-tuple-element.53.refs_0_, bf16[656,128]{1,0:T(8,128)(2,1)} %copy-done, bf16[656,128]{1,0:T(8,128)(2,1)} %copy-done.1, bf16[656,128]{1,0:T(8,128)(2,1)} %copy-done.2, ...), custom_call_target="tpu_custom_call" | custom-call | flops 10000000000 | bytes 29892608 | tf_op jit(solution)/shard_map/weights/pallas_call | solution.py:451
  75.6 0.0 copy-start.14
  75.6 2.5 %collective-permute-done.7.refs_1_ = bf16[640,128]{1,0:T(8,128)(2,1)S(1)} collective-permute-done((bf16[640,128]{1,0:T(8,128)(2,1)}, bf16[640,128]{1,0:T(8,128)(2,1)S(1)}, u32[]{:S(2)}, u32[]{:S(2)}) %collective-permute-start.7) | collective-permute-done | bytes 163872 | tf_op jit(solution)/shard_map/ppermute | solution.py:498
  78.1 1.4 collective-permute-done.8.refs_2_
  79.6 0.6 copy-done.29
  80.2 0.1 copy-done.32
  80.3 23.9 %attention_and_grad_queries.1 = (bf16[640,128]{1,0:T(8,128)(2,1)}, bf16[640,128]{1,0:T(8,128)(2,1)}, bf16[640,128]{1,0:T(8,128)(2,1)}, bf16[640,128]{1,0:T(8,128...) custom-call(s32[8,128]{1,0:T(8,128)} %get-tuple-element.61.table, ...), custom_call_target="tpu_custom_call" | custom-call | flops 10000000000 | bytes 30933040 | tf_op jit(solution)/shard_map/attention_and_grad_queries/pallas_call | solution.py:451
  104.2 0.1 collective-permute-start.14
  104.3 0.5 collective-permute-start.15
  104.8 0.1 collective-permute-start.16
  104.8 4.8 %collective-permute-start.17 = (bf16[640,128]{1,0:T(8,128)(2,1)}, bf16[640,128]{1,0:T(8,128)(2,1)S(1)}, u32[]{:S(2)}, u32[]{:S(2)}) collective-permute-start(bf16[640,128]{1,0:T(8,128)(2,1)} %get-tuple-element.81), channel_id=1, source_target_pairs={{0,24},{4,28},{8,16},{12,20},{16,8},{20,12},{24,0},{28,4},{1,25},{... | collective-permute-start | bytes 491528 | tf_op jit(solution)/shard_map/ppermute | solution.py:498
  109.6 6.3 %collective-permute-done.14.refs_1_ = bf16[640,128]{1,0:T(8,128)(2,1)S(1)} collective-permute-done((bf16[640,128]{1,0:T(8,128)(2,1)}, bf16[640,128]{1,0:T(8,128)(2,1)S(1)}, u32[]{:S(2)}, u32[]{:S(2)}) %collective-permute-start.14) | collective-permute-done | bytes 163872 | tf_op jit(solution)/shard_map/ppermute | solution.py:498
  115.9 0.0 copy-start.21
  116.0 0.1 collective-permute-start.20
  116.0 18.8 %grad_keys_and_grad_values.1 = (bf16[640,128]{1,0:T(8,128)(2,1)}, bf16[640,128]{1,0:T(8,128)(2,1)}, bf16[640,128]{1,0:T(8,128)(2,1)}, bf16[640,128]{1,0:T(8,128)...) custom-call(s32[8,128]{1,0:T(8,128)} %get-tuple-element.61.table, ...), custom_call_target="tpu_custom_call" | custom-call | flops 10000000000 | bytes 2621440 | tf_op jit(solution)/shard_map/grad_keys_and_grad_values/pallas_call | solution.py:451
  135.0 0.3 collective-permute-done.19.refs_6_
  135.4 0.3 copy-done.24
  135.6 0.1 copy-done.26
  135.7 0.1 copy-done.28
  135.8 0.2 copy-done.31
  136.0 0.7 copy-done.34
  136.7 4.4 %unpack_attention_grad_queries.1 = (bf16[192,1024]{1,0:T(8,128)(2,1)}, bf16[192,1024]{1,0:T(8,128)(2,1)}) custom-call(s32[16]{0:T(128)} %convert_reduce_fusion.hist, s32[1]{0:T(128)} %bitcast.me, s32[1,1024]{1,0:T(1,128)} %get-tuple-element.50.pos, bf16[640,128]{1,0:T(8,128)(2,1)} %get-tuple-element.77.refs_0_, bf16[640,128]{1,0:T(8,128)(2,1)} %copy-done.19, ...), custom_call_target="tpu_custom_call" | custom-call | flops 2000000000 | bytes 1572864 | tf_op jit(solution)/shard_map/unpack_attention_grad_queries/pallas_call | solution.py:451
  141.0 0.0 all-gather.8.cloned.1.call-update
  141.1 0.1 collective-permute-start.21
  141.2 0.9 collective-permute-start.22
  142.1 4.3 %collective-permute-start.23 = (bf16[640,128]{1,0:T(8,128)(2,1)S(1)}, bf16[640,128]{1,0:T(8,128)(2,1)S(1)}, u32[]{:S(2)}, u32[]{:S(2)}) collective-permute-start(bf16[640,128]{1,0:T(8,128)(2,1)S(1)} %copy-done.12), channel_id=1, source_target_pairs={{0,24},{4,28},{8,16},{12,20},{16,8},{20,12},{24,0},{28,4},{1,25},{... | collective-permute-start | bytes 491528 | tf_op jit(solution)/shard_map/ppermute | solution.py:498
  146.4 0.4 collective-permute-start.24
  146.9 2.0 %collective-permute-start.25 = (bf16[640,128]{1,0:T(8,128)(2,1)S(1)}, bf16[640,128]{1,0:T(8,128)(2,1)S(1)}, u32[]{:S(2)}, u32[]{:S(2)}) collective-permute-start(bf16[640,128]{1,0:T(8,128)(2,1)S(1)} %copy-done.9), channel_id=1, source_target_pairs={{0,16},{4,20},{8,24},{12,28},{16,0},{20,4},{24,8},{28,12},{1,17},{... | collective-permute-start | bytes 491528 | tf_op jit(solution)/shard_map/ppermute | solution.py:498
  148.9 1.0 collective-permute-start.26
  149.9 1.3 collective-permute-done.22.refs_2_
  151.2 12.6 %collective-permute-start.27 = (bf16[640,128]{1,0:T(8,128)(2,1)S(1)}, bf16[640,128]{1,0:T(8,128)(2,1)S(1)}, u32[]{:S(2)}, u32[]{:S(2)}) collective-permute-start(bf16[640,128]{1,0:T(8,128)(2,1)S(1)} %copy-done.7), channel_id=1, source_target_pairs={{0,8},{4,12},{8,0},{12,4},{16,24},{20,28},{24,16},{28,20},{1,9},{5... | collective-permute-start | bytes 491528 | tf_op jit(solution)/shard_map/ppermute | solution.py:498
  163.8 4.9 %collective-permute-done.24.refs_4_ = bf16[640,128]{1,0:T(8,128)(2,1)S(1)} collective-permute-done((bf16[640,128]{1,0:T(8,128)(2,1)S(1)}, bf16[640,128]{1,0:T(8,128)(2,1)S(1)}, u32[]{:S(2)}, u32[]{:S(2)}) %collective-permute-start.24) | collective-permute-done | bytes 163872 | tf_op jit(solution)/shard_map/ppermute | solution.py:498
  168.6 2.0 %collective-permute-done.25.refs_5_ = bf16[640,128]{1,0:T(8,128)(2,1)S(1)} collective-permute-done((bf16[640,128]{1,0:T(8,128)(2,1)S(1)}, bf16[640,128]{1,0:T(8,128)(2,1)S(1)}, u32[]{:S(2)}, u32[]{:S(2)}) %collective-permute-start.25) | collective-permute-done | bytes 163872 | tf_op jit(solution)/shard_map/ppermute | solution.py:498
  170.6 0.8 collective-permute-done.27.refs_7_
  171.5 0.7 copy-done.33
  172.2 4.2 %unpack_grad_keys_grad_values.1 = (bf16[192,1024]{1,0:T(8,128)(2,1)}, bf16[192,1024]{1,0:T(8,128)(2,1)}) custom-call(s32[16]{0:T(128)} %convert_reduce_fusion.hist, s32[1]{0:T(128)} %bitcast.me, s32[1,1024]{1,0:T(1,128)} %get-tuple-element.50.pos, bf16[640,128]{1,0:T(8,128)(2,1)} %get-tuple-element.76.refs_0_, bf16[640,128]{1,0:T(8,128)(2,1)} %copy-done.16, ...), custom_call_target="tpu_custom_call" | custom-call | flops 2000000000 | bytes 1572864 | tf_op jit(solution)/shard_map/unpack_grad_keys_grad_values/pallas_call | solution.py:451
  176.3 2.9 %convolution_convert_fusion = bf16[192,1024]{1,0:T(8,128)(2,1)} fusion(bf16[768,1024]{1,0:T(8,128)(2,1)} %all-gather.8.cloned.1.call-done, bf16[768,768]{1,0:T(8,128)(2,1)} %all-gather.4.cloned.1.call-done, s32[]{:T(128)S(6)} %select_n.3), kind=kOutput, calls=%fused_computation | convolution fusion | flops 302186496 | bytes 2359300 | tf_op jit(solution)/shard_map/dot_general | solution.py:564
  (80 shorter events, 0.2 us)
Async XLA Ops:
  7.2 34.8 %all-gather.6.cloned.1.call-start = ((), (), s32[]{:S(2)}) async-start(), calls=%async_computation.1 | async-start | bytes 1966080 | tf_op jit(solution)/shard_map/all_gather | solution.py:503
  7.9 168.4 %all-gather.4.cloned.1.call-start = ((), (), s32[]{:S(2)}) async-start(), calls=%async_computation | async-start | bytes 1474560 | tf_op jit(solution)/shard_map/all_gather | solution.py:504
  14.3 11.3 %collective-permute-start = (bf16[656,128]{1,0:T(8,128)(2,1)}, bf16[656,128]{1,0:T(8,128)(2,1)S(1)}, u32[]{:S(2)}, u32[]{:S(2)}) collective-permute-start(bf16[656,128]{1,0:T(8,128)(2,1)} %get-tuple-element.54), channel_id=1, source_target_pairs={{0,28},{4,24},{8,20},{12,16},{16,12},{20,8},{24,4},{28,0},{1,29},{... | collective-permute-start | bytes 503816 | tf_op jit(solution)/shard_map/ppermute | solution.py:498
  20.2 20.3 %collective-permute-start.1 = (bf16[656,128]{1,0:T(8,128)(2,1)}, bf16[656,128]{1,0:T(8,128)(2,1)S(1)}, u32[]{:S(2)}, u32[]{:S(2)}) collective-permute-start(bf16[656,128]{1,0:T(8,128)(2,1)} %get-tuple-element.55), channel_id=1, source_target_pairs={{0,24},{4,28},{8,16},{12,20},{16,8},{20,12},{24,0},{28,4},{1,25},{... | collective-permute-start | bytes 503816 | tf_op jit(solution)/shard_map/ppermute | solution.py:498
  20.5 26.6 %collective-permute-start.2 = (bf16[656,128]{1,0:T(8,128)(2,1)}, bf16[656,128]{1,0:T(8,128)(2,1)S(1)}, u32[]{:S(2)}, u32[]{:S(2)}) collective-permute-start(bf16[656,128]{1,0:T(8,128)(2,1)} %get-tuple-element.56), channel_id=1, source_target_pairs={{0,20},{4,16},{8,28},{12,24},{16,4},{20,0},{24,12},{28,8},{1,21},{... | collective-permute-start | bytes 503816 | tf_op jit(solution)/shard_map/ppermute | solution.py:498
  21.2 28.0 %collective-permute-start.3 = (bf16[656,128]{1,0:T(8,128)(2,1)}, bf16[656,128]{1,0:T(8,128)(2,1)S(1)}, u32[]{:S(2)}, u32[]{:S(2)}) collective-permute-start(bf16[656,128]{1,0:T(8,128)(2,1)} %get-tuple-element.57), channel_id=1, source_target_pairs={{0,16},{4,20},{8,24},{12,28},{16,0},{20,4},{24,8},{28,12},{1,17},{... | collective-permute-start | bytes 503816 | tf_op jit(solution)/shard_map/ppermute | solution.py:498
  23.2 27.5 %collective-permute-start.4 = (bf16[656,128]{1,0:T(8,128)(2,1)}, bf16[656,128]{1,0:T(8,128)(2,1)S(1)}, u32[]{:S(2)}, u32[]{:S(2)}) collective-permute-start(bf16[656,128]{1,0:T(8,128)(2,1)} %get-tuple-element.58), channel_id=1, source_target_pairs={{0,12},{4,8},{8,4},{12,0},{16,28},{20,24},{24,20},{28,16},{1,13},{... | collective-permute-start | bytes 503816 | tf_op jit(solution)/shard_map/ppermute | solution.py:498
  25.5 21.6 %copy-start = (bf16[656,128]{1,0:T(8,128)(2,1)}, bf16[656,128]{1,0:T(8,128)(2,1)S(1)}, u32[]{:S(2)}) copy-start(bf16[656,128]{1,0:T(8,128)(2,1)S(1)} %collective-permute-done.refs_1_) | copy-start | bytes 503812
  25.5 28.0 %collective-permute-start.5 = (bf16[656,128]{1,0:T(8,128)(2,1)}, bf16[656,128]{1,0:T(8,128)(2,1)S(1)}, u32[]{:S(2)}, u32[]{:S(2)}) collective-permute-start(bf16[656,128]{1,0:T(8,128)(2,1)} %get-tuple-element.59), channel_id=1, source_target_pairs={{0,8},{4,12},{8,0},{12,4},{16,24},{20,28},{24,16},{28,20},{1,9},{5... | collective-permute-start | bytes 503816 | tf_op jit(solution)/shard_map/ppermute | solution.py:498
  40.5 6.6 %copy-start.1 = (bf16[656,128]{1,0:T(8,128)(2,1)}, bf16[656,128]{1,0:T(8,128)(2,1)S(1)}, u32[]{:S(2)}) copy-start(bf16[656,128]{1,0:T(8,128)(2,1)S(1)} %collective-permute-done.1.refs_2_) | copy-start | bytes 503812
  40.5 14.2 %collective-permute-start.6 = (bf16[656,128]{1,0:T(8,128)(2,1)}, bf16[656,128]{1,0:T(8,128)(2,1)S(1)}, u32[]{:S(2)}, u32[]{:S(2)}) collective-permute-start(bf16[656,128]{1,0:T(8,128)(2,1)} %get-tuple-element.60), channel_id=1, source_target_pairs={{0,4},{4,0},{8,12},{12,8},{16,20},{20,16},{24,28},{28,24},{1,5},{5... | collective-permute-start | bytes 503816 | tf_op jit(solution)/shard_map/ppermute | solution.py:498
  47.1 11.8 %copy-start.2 = (bf16[656,128]{1,0:T(8,128)(2,1)}, bf16[656,128]{1,0:T(8,128)(2,1)S(1)}, u32[]{:S(2)}) copy-start(bf16[656,128]{1,0:T(8,128)(2,1)S(1)} %collective-permute-done.2.refs_3_) | copy-start | bytes 503812
  47.1 8.0 %collective-permute-start.10 = (bf16[640,128]{1,0:T(8,128)(2,1)}, bf16[640,128]{1,0:T(8,128)(2,1)S(1)}, u32[]{:S(2)}, u32[]{:S(2)}) collective-permute-start(bf16[640,128]{1,0:T(8,128)(2,1)} %get-tuple-element.65), channel_id=1, source_target_pairs={{0,8},{4,12},{8,0},{12,4},{16,24},{20,28},{24,16},{28,20},{1,9},{5... | collective-permute-start | bytes 491528 | tf_op jit(solution)/shard_map/ppermute | solution.py:498
  49.2 9.7 %copy-start.3 = (bf16[656,128]{1,0:T(8,128)(2,1)}, bf16[656,128]{1,0:T(8,128)(2,1)S(1)}, u32[]{:S(2)}) copy-start(bf16[656,128]{1,0:T(8,128)(2,1)S(1)} %collective-permute-done.3.refs_4_) | copy-start | bytes 503812
  49.2 9.2 %collective-permute-start.11 = (bf16[640,128]{1,0:T(8,128)(2,1)}, bf16[640,128]{1,0:T(8,128)(2,1)S(1)}, u32[]{:S(2)}, u32[]{:S(2)}) collective-permute-start(bf16[640,128]{1,0:T(8,128)(2,1)} %get-tuple-element.66), channel_id=1, source_target_pairs={{0,4},{4,0},{8,12},{12,8},{16,20},{20,16},{24,28},{28,24},{1,5},{5... | collective-permute-start | bytes 491528 | tf_op jit(solution)/shard_map/ppermute | solution.py:498
  50.7 125.7 %all-gather.8.cloned.1.call-start = ((), (), s32[]{:S(2)}) async-start(), calls=%async_computation.2 | async-start | bytes 1966080 | tf_op jit(solution)/shard_map/all_gather | solution.py:562
  50.7 8.2 %copy-start.4 = (bf16[656,128]{1,0:T(8,128)(2,1)}, bf16[656,128]{1,0:T(8,128)(2,1)S(1)}, u32[]{:S(2)}) copy-start(bf16[656,128]{1,0:T(8,128)(2,1)S(1)} %collective-permute-done.4.refs_5_) | copy-start | bytes 503812
  50.7 24.9 %collective-permute-start.12 = (bf16[640,128]{1,0:T(8,128)(2,1)}, bf16[640,128]{1,0:T(8,128)(2,1)S(1)}, u32[]{:S(2)}, u32[]{:S(2)}) collective-permute-start(bf16[640,128]{1,0:T(8,128)(2,1)} %get-tuple-element.67), channel_id=1, source_target_pairs={{0,28},{4,24},{8,20},{12,16},{16,12},{20,8},{24,4},{28,0},{1,29},{... | collective-permute-start | bytes 491528 | tf_op jit(solution)/shard_map/ppermute | solution.py:498
  53.5 5.4 %copy-start.5 = (bf16[656,128]{1,0:T(8,128)(2,1)}, bf16[656,128]{1,0:T(8,128)(2,1)S(1)}, u32[]{:S(2)}) copy-start(bf16[656,128]{1,0:T(8,128)(2,1)S(1)} %collective-permute-done.5.refs_6_) | copy-start | bytes 503812
  53.5 22.1 %collective-permute-start.13 = (bf16[640,128]{1,0:T(8,128)(2,1)}, bf16[640,128]{1,0:T(8,128)(2,1)S(1)}, u32[]{:S(2)}, u32[]{:S(2)}) collective-permute-start(bf16[640,128]{1,0:T(8,128)(2,1)} %get-tuple-element.68), channel_id=1, source_target_pairs={{0,24},{4,28},{8,16},{12,20},{16,8},{20,12},{24,0},{28,4},{1,25},{... | collective-permute-start | bytes 491528 | tf_op jit(solution)/shard_map/ppermute | solution.py:498
  54.7 4.2 %copy-start.6 = (bf16[656,128]{1,0:T(8,128)(2,1)}, bf16[656,128]{1,0:T(8,128)(2,1)S(1)}, u32[]{:S(2)}) copy-start(bf16[656,128]{1,0:T(8,128)(2,1)S(1)} %collective-permute-done.6.refs_7_) | copy-start | bytes 503812
  54.7 23.4 %collective-permute-start.7 = (bf16[640,128]{1,0:T(8,128)(2,1)}, bf16[640,128]{1,0:T(8,128)(2,1)S(1)}, u32[]{:S(2)}, u32[]{:S(2)}) collective-permute-start(bf16[640,128]{1,0:T(8,128)(2,1)} %get-tuple-element.62), channel_id=1, source_target_pairs={{0,20},{4,16},{8,28},{12,24},{16,4},{20,0},{24,12},{28,8},{1,21},{... | collective-permute-start | bytes 491528 | tf_op jit(solution)/shard_map/ppermute | solution.py:498
  55.1 20.5 %copy-start.11 = (bf16[640,128]{1,0:T(8,128)(2,1)}, bf16[640,128]{1,0:T(8,128)(2,1)S(1)}, u32[]{:S(2)}) copy-start(bf16[640,128]{1,0:T(8,128)(2,1)S(1)} %collective-permute-done.10.refs_4_) | copy-start | bytes 491524
  55.1 24.4 %collective-permute-start.8 = (bf16[640,128]{1,0:T(8,128)(2,1)}, bf16[640,128]{1,0:T(8,128)(2,1)S(1)}, u32[]{:S(2)}, u32[]{:S(2)}) collective-permute-start(bf16[640,128]{1,0:T(8,128)(2,1)} %get-tuple-element.63), channel_id=1, source_target_pairs={{0,16},{4,20},{8,24},{12,28},{16,0},{20,4},{24,8},{28,12},{1,17},{... | collective-permute-start | bytes 491528 | tf_op jit(solution)/shard_map/ppermute | solution.py:498
  58.5 17.1 %copy-start.13 = (bf16[640,128]{1,0:T(8,128)(2,1)}, bf16[640,128]{1,0:T(8,128)(2,1)S(1)}, u32[]{:S(2)}) copy-start(bf16[640,128]{1,0:T(8,128)(2,1)S(1)} %collective-permute-done.11.refs_5_) | copy-start | bytes 491524
  58.5 21.1 %collective-permute-start.9 = (bf16[640,128]{1,0:T(8,128)(2,1)}, bf16[640,128]{1,0:T(8,128)(2,1)S(1)}, u32[]{:S(2)}, u32[]{:S(2)}) collective-permute-start(bf16[640,128]{1,0:T(8,128)(2,1)} %get-tuple-element.64), channel_id=1, source_target_pairs={{0,12},{4,8},{8,4},{12,0},{16,28},{20,24},{24,20},{28,16},{1,13},{... | collective-permute-start | bytes 491528 | tf_op jit(solution)/shard_map/ppermute | solution.py:498
  75.6 3.9 %copy-start.14 = (bf16[640,128]{1,0:T(8,128)(2,1)}, bf16[640,128]{1,0:T(8,128)(2,1)S(1)}, u32[]{:S(2)}) copy-start(bf16[640,128]{1,0:T(8,128)(2,1)S(1)} %collective-permute-done.12.refs_6_) | copy-start | bytes 491524
  75.6 3.9 %copy-start.17 = (bf16[640,128]{1,0:T(8,128)(2,1)}, bf16[640,128]{1,0:T(8,128)(2,1)S(1)}, u32[]{:S(2)}) copy-start(bf16[640,128]{1,0:T(8,128)(2,1)S(1)} %collective-permute-done.13.refs_7_) | copy-start | bytes 491524
  78.1 1.4 copy-start.23
  79.5 0.7 copy-start.29
  79.5 0.7 copy-start.32
  104.2 11.7 %collective-permute-start.14 = (bf16[640,128]{1,0:T(8,128)(2,1)}, bf16[640,128]{1,0:T(8,128)(2,1)S(1)}, u32[]{:S(2)}, u32[]{:S(2)}) collective-permute-start(bf16[640,128]{1,0:T(8,128)(2,1)} %get-tuple-element.78), channel_id=1, source_target_pairs={{0,8},{4,12},{8,0},{12,4},{16,24},{20,28},{24,16},{28,20},{1,9},{5... | collective-permute-start | bytes 491528 | tf_op jit(solution)/shard_map/ppermute | solution.py:498
  104.3 11.7 %collective-permute-start.15 = (bf16[640,128]{1,0:T(8,128)(2,1)}, bf16[640,128]{1,0:T(8,128)(2,1)S(1)}, u32[]{:S(2)}, u32[]{:S(2)}) collective-permute-start(bf16[640,128]{1,0:T(8,128)(2,1)} %get-tuple-element.79), channel_id=1, source_target_pairs={{0,4},{4,0},{8,12},{12,8},{16,20},{20,16},{24,28},{28,24},{1,5},{5... | collective-permute-start | bytes 491528 | tf_op jit(solution)/shard_map/ppermute | solution.py:498
  104.8 30.2 %collective-permute-start.16 = (bf16[640,128]{1,0:T(8,128)(2,1)}, bf16[640,128]{1,0:T(8,128)(2,1)S(1)}, u32[]{:S(2)}, u32[]{:S(2)}) collective-permute-start(bf16[640,128]{1,0:T(8,128)(2,1)} %get-tuple-element.80), channel_id=1, source_target_pairs={{0,28},{4,24},{8,20},{12,16},{16,12},{20,8},{24,4},{28,0},{1,29},{... | collective-permute-start | bytes 491528 | tf_op jit(solution)/shard_map/ppermute | solution.py:498
  104.8 30.2 %collective-permute-start.17 = (bf16[640,128]{1,0:T(8,128)(2,1)}, bf16[640,128]{1,0:T(8,128)(2,1)S(1)}, u32[]{:S(2)}, u32[]{:S(2)}) collective-permute-start(bf16[640,128]{1,0:T(8,128)(2,1)} %get-tuple-element.81), channel_id=1, source_target_pairs={{0,24},{4,28},{8,16},{12,20},{16,8},{20,12},{24,0},{28,4},{1,25},{... | collective-permute-start | bytes 491528 | tf_op jit(solution)/shard_map/ppermute | solution.py:498
  109.6 25.4 %collective-permute-start.18 = (bf16[640,128]{1,0:T(8,128)(2,1)}, bf16[640,128]{1,0:T(8,128)(2,1)S(1)}, u32[]{:S(2)}, u32[]{:S(2)}) collective-permute-start(bf16[640,128]{1,0:T(8,128)(2,1)} %get-tuple-element.82), channel_id=1, source_target_pairs={{0,20},{4,16},{8,28},{12,24},{16,4},{20,0},{24,12},{28,8},{1,21},{... | collective-permute-start | bytes 491528 | tf_op jit(solution)/shard_map/ppermute | solution.py:498
  115.9 19.0 %copy-start.19 = (bf16[640,128]{1,0:T(8,128)(2,1)}, bf16[640,128]{1,0:T(8,128)(2,1)S(1)}, u32[]{:S(2)}) copy-start(bf16[640,128]{1,0:T(8,128)(2,1)S(1)} %collective-permute-done.14.refs_1_) | copy-start | bytes 491524
  115.9 19.4 %collective-permute-start.19 = (bf16[640,128]{1,0:T(8,128)(2,1)}, bf16[640,128]{1,0:T(8,128)(2,1)S(1)}, u32[]{:S(2)}, u32[]{:S(2)}) collective-permute-start(bf16[640,128]{1,0:T(8,128)(2,1)} %get-tuple-element.83), channel_id=1, source_target_pairs={{0,16},{4,20},{8,24},{12,28},{16,0},{20,4},{24,8},{28,12},{1,17},{... | collective-permute-start | bytes 491528 | tf_op jit(solution)/shard_map/ppermute | solution.py:498
  115.9 19.0 %copy-start.21 = (bf16[640,128]{1,0:T(8,128)(2,1)}, bf16[640,128]{1,0:T(8,128)(2,1)S(1)}, u32[]{:S(2)}) copy-start(bf16[640,128]{1,0:T(8,128)(2,1)S(1)} %collective-permute-done.15.refs_2_) | copy-start | bytes 491524
  116.0 19.4 %collective-permute-start.20 = (bf16[640,128]{1,0:T(8,128)(2,1)}, bf16[640,128]{1,0:T(8,128)(2,1)S(1)}, u32[]{:S(2)}, u32[]{:S(2)}) collective-permute-start(bf16[640,128]{1,0:T(8,128)(2,1)} %get-tuple-element.84), channel_id=1, source_target_pairs={{0,12},{4,8},{8,4},{12,0},{16,28},{20,24},{24,20},{28,16},{1,13},{... | collective-permute-start | bytes 491528 | tf_op jit(solution)/shard_map/ppermute | solution.py:498
  134.9 6.2 %copy-start.18 = (bf16[640,128]{1,0:T(8,128)(2,1)S(1)}, bf16[640,128]{1,0:T(8,128)(2,1)}, u32[]{:S(2)}) copy-start(bf16[640,128]{1,0:T(8,128)(2,1)} %get-tuple-element.87) | copy-start | bytes 491524
  134.9 6.2 %copy-start.15 = (bf16[640,128]{1,0:T(8,128)(2,1)S(1)}, bf16[640,128]{1,0:T(8,128)(2,1)}, u32[]{:S(2)}) copy-start(bf16[640,128]{1,0:T(8,128)(2,1)} %get-tuple-element.88) | copy-start | bytes 491524
  134.9 7.2 %copy-start.12 = (bf16[640,128]{1,0:T(8,128)(2,1)S(1)}, bf16[640,128]{1,0:T(8,128)(2,1)}, u32[]{:S(2)}) copy-start(bf16[640,128]{1,0:T(8,128)(2,1)} %get-tuple-element.89) | copy-start | bytes 491524
  134.9 11.5 %copy-start.10 = (bf16[640,128]{1,0:T(8,128)(2,1)S(1)}, bf16[640,128]{1,0:T(8,128)(2,1)}, u32[]{:S(2)}) copy-start(bf16[640,128]{1,0:T(8,128)(2,1)} %get-tuple-element.90) | copy-start | bytes 491524
  134.9 11.9 %copy-start.9 = (bf16[640,128]{1,0:T(8,128)(2,1)S(1)}, bf16[640,128]{1,0:T(8,128)(2,1)}, u32[]{:S(2)}) copy-start(bf16[640,128]{1,0:T(8,128)(2,1)} %get-tuple-element.91) | copy-start | bytes 491524
  134.9 13.9 %copy-start.8 = (bf16[640,128]{1,0:T(8,128)(2,1)S(1)}, bf16[640,128]{1,0:T(8,128)(2,1)}, u32[]{:S(2)}) copy-start(bf16[640,128]{1,0:T(8,128)(2,1)} %get-tuple-element.92) | copy-start | bytes 491524
  135.0 16.2 %copy-start.7 = (bf16[640,128]{1,0:T(8,128)(2,1)S(1)}, bf16[640,128]{1,0:T(8,128)(2,1)}, u32[]{:S(2)}) copy-start(bf16[640,128]{1,0:T(8,128)(2,1)} %get-tuple-element.93) | copy-start | bytes 491524
  135.0 0.7 copy-start.24
  135.0 0.7 copy-start.26
  135.0 0.8 copy-start.28
  136.0 0.7 copy-start.34
  141.1 7.8 %collective-permute-start.21 = (bf16[640,128]{1,0:T(8,128)(2,1)S(1)}, bf16[640,128]{1,0:T(8,128)(2,1)S(1)}, u32[]{:S(2)}, u32[]{:S(2)}) collective-permute-start(bf16[640,128]{1,0:T(8,128)(2,1)S(1)} %copy-done.18), channel_id=1, source_target_pairs={{0,4},{4,0},{8,12},{12,8},{16,20},{20,16},{24,28},{28,24},{1,5},{5... | collective-permute-start | bytes 491528 | tf_op jit(solution)/shard_map/ppermute | solution.py:498
  141.2 10.0 %collective-permute-start.22 = (bf16[640,128]{1,0:T(8,128)(2,1)S(1)}, bf16[640,128]{1,0:T(8,128)(2,1)S(1)}, u32[]{:S(2)}, u32[]{:S(2)}) collective-permute-start(bf16[640,128]{1,0:T(8,128)(2,1)S(1)} %copy-done.15), channel_id=1, source_target_pairs={{0,28},{4,24},{8,20},{12,16},{16,12},{20,8},{24,4},{28,0},{1,29},{... | collective-permute-start | bytes 491528 | tf_op jit(solution)/shard_map/ppermute | solution.py:498
  142.1 21.7 %collective-permute-start.23 = (bf16[640,128]{1,0:T(8,128)(2,1)S(1)}, bf16[640,128]{1,0:T(8,128)(2,1)S(1)}, u32[]{:S(2)}, u32[]{:S(2)}) collective-permute-start(bf16[640,128]{1,0:T(8,128)(2,1)S(1)} %copy-done.12), channel_id=1, source_target_pairs={{0,24},{4,28},{8,16},{12,20},{16,8},{20,12},{24,0},{28,4},{1,25},{... | collective-permute-start | bytes 491528 | tf_op jit(solution)/shard_map/ppermute | solution.py:498
  146.4 22.2 %collective-permute-start.24 = (bf16[640,128]{1,0:T(8,128)(2,1)S(1)}, bf16[640,128]{1,0:T(8,128)(2,1)S(1)}, u32[]{:S(2)}, u32[]{:S(2)}) collective-permute-start(bf16[640,128]{1,0:T(8,128)(2,1)S(1)} %copy-done.10), channel_id=1, source_target_pairs={{0,20},{4,16},{8,28},{12,24},{16,4},{20,0},{24,12},{28,8},{1,21},{... | collective-permute-start | bytes 491528 | tf_op jit(solution)/shard_map/ppermute | solution.py:498
  146.9 23.7 %collective-permute-start.25 = (bf16[640,128]{1,0:T(8,128)(2,1)S(1)}, bf16[640,128]{1,0:T(8,128)(2,1)S(1)}, u32[]{:S(2)}, u32[]{:S(2)}) collective-permute-start(bf16[640,128]{1,0:T(8,128)(2,1)S(1)} %copy-done.9), channel_id=1, source_target_pairs={{0,16},{4,20},{8,24},{12,28},{16,0},{20,4},{24,8},{28,12},{1,17},{... | collective-permute-start | bytes 491528 | tf_op jit(solution)/shard_map/ppermute | solution.py:498
  148.9 22.6 %copy-start.16 = (bf16[640,128]{1,0:T(8,128)(2,1)}, bf16[640,128]{1,0:T(8,128)(2,1)S(1)}, u32[]{:S(2)}) copy-start(bf16[640,128]{1,0:T(8,128)(2,1)S(1)} %collective-permute-done.21.refs_1_) | copy-start | bytes 491524
  148.9 21.7 %collective-permute-start.26 = (bf16[640,128]{1,0:T(8,128)(2,1)S(1)}, bf16[640,128]{1,0:T(8,128)(2,1)S(1)}, u32[]{:S(2)}, u32[]{:S(2)}) collective-permute-start(bf16[640,128]{1,0:T(8,128)(2,1)S(1)} %copy-done.8), channel_id=1, source_target_pairs={{0,12},{4,8},{8,4},{12,0},{16,28},{20,24},{24,20},{28,16},{1,13},{... | collective-permute-start | bytes 491528 | tf_op jit(solution)/shard_map/ppermute | solution.py:498
  151.2 20.3 %copy-start.20 = (bf16[640,128]{1,0:T(8,128)(2,1)}, bf16[640,128]{1,0:T(8,128)(2,1)S(1)}, u32[]{:S(2)}) copy-start(bf16[640,128]{1,0:T(8,128)(2,1)S(1)} %collective-permute-done.22.refs_2_) | copy-start | bytes 491524
  151.2 20.3 %collective-permute-start.27 = (bf16[640,128]{1,0:T(8,128)(2,1)S(1)}, bf16[640,128]{1,0:T(8,128)(2,1)S(1)}, u32[]{:S(2)}, u32[]{:S(2)}) collective-permute-start(bf16[640,128]{1,0:T(8,128)(2,1)S(1)} %copy-done.7), channel_id=1, source_target_pairs={{0,8},{4,12},{8,0},{12,4},{16,24},{20,28},{24,16},{28,20},{1,9},{5... | collective-permute-start | bytes 491528 | tf_op jit(solution)/shard_map/ppermute | solution.py:498
  163.8 7.7 %copy-start.22 = (bf16[640,128]{1,0:T(8,128)(2,1)}, bf16[640,128]{1,0:T(8,128)(2,1)S(1)}, u32[]{:S(2)}) copy-start(bf16[640,128]{1,0:T(8,128)(2,1)S(1)} %collective-permute-done.23.refs_3_) | copy-start | bytes 491524
  168.6 2.8 %copy-start.25 = (bf16[640,128]{1,0:T(8,128)(2,1)}, bf16[640,128]{1,0:T(8,128)(2,1)S(1)}, u32[]{:S(2)}) copy-start(bf16[640,128]{1,0:T(8,128)(2,1)S(1)} %collective-permute-done.24.refs_4_) | copy-start | bytes 491524
  170.6 0.9 copy-start.27
  170.6 0.9 copy-start.30
  (2 other events, 1.3 us)
Sparse Core Ops, SparseCore 0:
  9.6 22.3 all-gather.5
  50.8 16.8 all-gather.3
  141.2 19.0 all-gather.7

commit v4 on v3

--- a/solution.py
+++ b/solution.py
@@ -14,13 +14,16 @@
 TILE = 256
 SPARE = 32
 NOTE = 16
+HEAD_DEVICES = 4
 MASKS = (
     (7, 6, 5, 4, 3, 2, 1),
-    (5, 4, 3, 2, 1, 7, 6),
-    (2, 1, 7, 6, 5, 4, 3),
-    (1, 7, 6, 5, 4, 3, 2),
+    (1, 2, 7, 6, 5, 4, 3),
+    (),
+    (),
 )
-VMEM_LIMIT = 56 * 1024 * 1024
+PAIRED_NODES = 8
+UNIT_LIMIT = 52
+SLOTS = 4
 masked_score = -1e30
 
 NT = (((1,), (1,)), ((), ()))
@@ -46,7 +49,8 @@
         self.shift = tuple(3 * head % nodes for head in range(self.heads))
         self.units = self.heads * clusters
         self.tiles = self.units * (CLUSTER // TILE)
-        self.split = nodes == len(masks) + 1
+        self.paired = nodes == PAIRED_NODES
+        self.split = self.paired and len(masks) > 0
         self.masks = (0,) + masks
         self.blocks = nodes if self.split else 1
 
@@ -60,7 +64,7 @@
         for index in range(plan.nodes):
             visit(index)
     else:
-        lax.fori_loop(0, plan.nodes, lambda index, carry: visit(index) or carry, 0)
+        lax.fori_loop(0, plan.nodes, lambda index, carry: (visit(index), carry)[1], 0)
 
 
 def block_of(plan, blocks, index):
@@ -156,10 +160,32 @@
     each_block(plan, note)
 
 
-def pack_second_kernel(plan, hist, me, pos, values, weight, cotangent, *refs):
-    wires, (starts, ordered) = refs[: plan.blocks], refs[plan.blocks :]
-    grad_in = dot(weight[...], cotangent[...]).astype(jnp.bfloat16)
+def pack_second_kernel(plan, hist, me, column, pos, values, weight, *refs):
+    cotangents, refs = refs[:HEAD_DEVICES], refs[HEAD_DEVICES:]
+    wires, (starts, ordered, gathered) = refs[: plan.blocks], refs[plan.blocks :]
+    for mask in range(HEAD_DEVICES):
+        place = jnp.bitwise_xor(column[0], mask) * plan.width
+        span = pl.ds(pl.multiple_of(place, plan.width), plan.width)
+        gathered[span, :] = cotangents[mask][...]
+    grad_in = dot(weight[...], gathered[...]).astype(jnp.bfloat16)
     spread(plan, pos[...], values[...], grad_in, hist, me[0], starts, ordered, wires)
+
+
+def project_kernel(plan, column, *refs):
+    weights, refs = refs[:HEAD_DEVICES], refs[HEAD_DEVICES:]
+    attentions, (out, piece) = refs[:HEAD_DEVICES], refs[HEAD_DEVICES:]
+    for index in range(HEAD_DEVICES):
+
+        @pl.when(column[0] == index)
+        def _(index=index):
+            start = index * plan.width
+            for mask in range(HEAD_DEVICES):
+                piece[mask] = weights[mask][:, start : start + plan.width]
+
+    total = jnp.zeros((plan.width, plan.rows), jnp.float32)
+    for mask in range(HEAD_DEVICES):
+        total = total + dot(piece[mask], attentions[mask][...], (((0,), (0,)), ((), ())))
+    out[...] = total.astype(jnp.bfloat16)
 
 
 def unpack_kernel(plan, hist, me, pos, *refs):
@@ -185,7 +211,7 @@
             second[span, at : at + TILE] = out[head * PAIR + HEAD_DIM : (head + 1) * PAIR, :]
 
 
-def each_group(plan, table, visit):
+def each_group(plan, table, me, visit):
     def source(line, block, places):
         at = block * (plan.cap + SPARE)
         after = []
@@ -197,19 +223,20 @@
         return tuple(after)
 
     places = (jnp.int32(0),) * plan.units
-    if not plan.split:
+    if not plan.paired:
         return lax.fori_loop(0, plan.nodes, lambda at, places: source(at, at, places), places)
     for mask in range(plan.nodes):
-        places = source(mask, plan.masks.index(mask), places)
+        block = plan.masks.index(mask) if plan.split else jnp.bitwise_xor(me, mask)
+        places = source(mask, block, places)
     return places
 
 
 def stage_rows(plan, index):
     start = index * (plan.cap + SPARE)
-    return pl.ds(start if plan.split else pl.multiple_of(start, plan.half), plan.cap)
-
-
-def gather_units(plan, table, wires, stage, held, counts):
+    return pl.ds(start if plan.split else pl.multiple_of(start, NOTE), plan.cap)
+
+
+def gather_units(plan, table, me, wires, stage, held, counts):
     def widen(index):
         block = block_of(plan, wires, index)
         stage[stage_rows(plan, index), :] = block[0 : plan.cap, :].astype(jnp.float32)
@@ -225,12 +252,12 @@
 
         lax.fori_loop(0, pl.cdiv(count, SPARE), step, 0)
 
-    totals = each_group(plan, table, visit)
+    totals = each_group(plan, table, me, visit)
     for unit in range(plan.units):
         counts[unit] = totals[unit]
 
 
-def scatter_units(plan, table, held, stage, wires):
+def scatter_units(plan, table, me, held, stage, wires):
     def visit(unit, place, at, count):
         def step(index, carry):
             stage[pl.ds(at + index * SPARE, SPARE), :] = held[
@@ -240,11 +267,11 @@
 
         lax.fori_loop(0, pl.cdiv(count, SPARE), step, 0)
 
-    each_group(plan, table, visit)
+    each_group(plan, table, me, visit)
 
     def narrow(index):
-        block = block_of(plan, wires, index)
-        block[...] = stage[stage_rows(plan, index), :].astype(jnp.bfloat16)
+        rows = stage[stage_rows(plan, index), :].astype(jnp.bfloat16)
+        block_of(plan, wires, index)[...] = rows
 
     each_block(plan, narrow)
 
@@ -254,10 +281,68 @@
     return jnp.where(row < count, held[unit, 0:CLUSTER, :], 0.0)
 
 
+def tile_steps(plan, counts):
+    return sum(pl.cdiv(counts[unit], TILE) for unit in range(plan.units))
+
+
+class Tiles:
+    def __init__(self, array, slots, sems):
+        self.array, self.slots, self.sems = array, slots, sems
+
+    def slot(self, step):
+        return lax.rem(step, SLOTS)
+
+    def fetch(self, step):
+        at = self.slot(step)
+        return pltpu.make_async_copy(self.array.at[step], self.slots.at[at], self.sems.at[at])
+
+    def begin(self, steps):
+        for step in range(SLOTS - 1):
+
+            @pl.when(step < steps)
+            def _(step=step):
+                self.fetch(step).start()
+
+    def read(self, step, steps):
+        @pl.when(step + SLOTS - 1 < steps)
+        def _():
+            self.fetch(step + SLOTS - 1).start()
+
+        self.fetch(step).wait()
+        return self.slots[self.slot(step)]
+
+    def store(self, step):
+        at = self.slot(step)
+        return pltpu.make_async_copy(self.slots.at[at], self.array.at[step], self.sems.at[at])
+
+    def write(self, step, value):
+        @pl.when(step >= SLOTS)
+        def _():
+            self.store(step - SLOTS).wait()
+
+        self.slots[self.slot(step)] = value
+        self.store(step).start()
+
+    def finish(self, steps):
+        for back in range(SLOTS, 0, -1):
+
+            @pl.when(steps >= back)
+            def _(back=back):
+                self.store(steps - back).wait()
+
+
+def each_unit(plan, counts, visit):
+    def one(unit, step):
+        return lax.cond(counts[unit] > 0, lambda: visit(unit, step), lambda: step)
+
+    lax.fori_loop(0, plan.units, one, jnp.int32(0))
+
+
 def weights_kernel(plan, *refs):
     wires, refs = refs[: plan.blocks], refs[plan.blocks :]
-    (table, queries, keys_t, weights, noted, stage, held, counts, query_aug, key_aug, out, sems,
-     table_sem) = refs
+    (table, queries, keys_t, weights, noted, stage, held, counts, query_aug, key_aug, table_sem,
+     slots, sems) = refs
+    out = Tiles(weights, slots, sems)
 
     def note(index):
         row = block_of(plan, wires, index)[plan.cap :, :].astype(jnp.float32)
@@ -268,14 +353,10 @@
     table_copy = pltpu.make_async_copy(noted, table, table_sem)
     table_copy.start()
     table_copy.wait()
-    gather_units(plan, table, wires, stage, held, counts)
+    gather_units(plan, table, None, wires, stage, held, counts)
     factor = math.log2(math.e) / math.sqrt(HEAD_DIM)
     lane = lax.broadcasted_iota(jnp.int32, (CLUSTER, PAIR), 1)
     row = lax.broadcasted_iota(jnp.int32, (CLUSTER, PAIR), 0)
-
-    def copy_out(step):
-        slot = lax.rem(step, 2)
-        return pltpu.make_async_copy(out.at[slot], weights.at[step], sems.at[slot])
 
     def one_unit(unit, step):
         count = counts[unit]
@@ -289,56 +370,34 @@
         key_aug[...] = jnp.where(lane < HEAD_DIM, turned, outside).astype(jnp.bfloat16)
 
         def one_tile(tile, step):
-            slot = lax.rem(step, 2)
             part = query_aug[pl.ds(pl.multiple_of(tile * TILE, TILE), TILE), :]
             scores = dot(key_aug[...], part, NT)
             raised = jnp.exp2((scores - jnp.max(scores, axis=0, keepdims=True)) * factor)
             share = 1.0 / jnp.sum(raised, axis=0, keepdims=True)
-
-            @pl.when(step >= 2)
-            def _():
-                copy_out(step - 2).wait()
-
-            out[slot] = (raised * share).astype(jnp.bfloat16)
-            copy_out(step).start()
+            out.write(step, (raised * share).astype(jnp.bfloat16))
             return step + 1
 
         return lax.fori_loop(0, pl.cdiv(count, TILE), one_tile, step)
 
-    steps = lax.fori_loop(0, plan.units, one_unit, jnp.int32(0))
-    for back in (2, 1):
-
-        @pl.when(steps >= back)
-        def _(back=back):
-            copy_out(steps - back).wait()
-
-
-def queries_kernel(plans, table, *refs):
+    each_unit(plan, counts, one_unit)
+    out.finish(tile_steps(plan, counts))
+
+
+def queries_kernel(plans, table, me, *refs):
     plan, plan_out = plans
     wires, refs = refs[: plan.blocks], refs[plan.blocks :]
     keys_t, weights = refs[:2]
-    wires_out, refs = refs[2 : 2 + plan.blocks], refs[2 + plan.blocks :]
-    (dscores_out, grads, counts_out, stage, held, counts, value_turned, both_t, held_out, tiles,
-     out, sems, out_sems) = refs
-    gather_units(plan, table, wires, stage, held, counts)
+    wires_out, refs = refs[2 : 2 + plan_out.blocks], refs[2 + plan_out.blocks :]
+    (dscores_out, grads, counts_out, stage, held, counts, value_turned, both_t, held_out,
+     slots, sems, slots_out, sems_out) = refs
+    tiles, out = Tiles(weights, slots, sems), Tiles(dscores_out, slots_out, sems_out)
+    gather_units(plan, table, me[0], wires, stage, held, counts)
     scale = 1.0 / math.sqrt(HEAD_DIM)
     lane = lax.broadcasted_iota(jnp.int32, (CLUSTER, PAIR), 1)
-    steps = jnp.int32(0)
     for unit in range(plan.units):
-        steps = steps + pl.cdiv(counts[unit], TILE)
         counts_out[unit] = counts[unit]
-
-    def copy_in(step):
-        slot = lax.rem(step, 2)
-        return pltpu.make_async_copy(weights.at[step], tiles.at[slot], sems.at[slot])
-
-    def copy_out(step):
-        slot = lax.rem(step, 2)
-        return pltpu.make_async_copy(out.at[slot], dscores_out.at[step], out_sems.at[slot])
-
-    @pl.when(steps > 0)
-    def _():
-        copy_in(0).start()
+    steps = tile_steps(plan, counts)
+    tiles.begin(steps)
 
     def one_unit(unit, step):
         count = counts[unit]
@@ -349,84 +408,42 @@
         both_t[...] = both.T.astype(jnp.bfloat16)
 
         def one_tile(tile, step):
-            slot = lax.rem(step, 2)
             span = pl.ds(pl.multiple_of(tile * TILE, TILE), TILE)
-
-            @pl.when(step + 1 < steps)
-            def _():
-                copy_in(step + 1).start()
-
-            copy_in(step).wait()
-            held_weights = tiles[slot]
+            held_weights = tiles.read(step, steps)
             mixed = dot(both_t[0:HEAD_DIM, :], held_weights).astype(jnp.bfloat16)
             mixed = mixed.astype(jnp.float32)
             grad_t = both_t[HEAD_DIM:PAIR, span].astype(jnp.float32)
             delta = jnp.sum(grad_t * mixed, axis=0, keepdims=True)
             dweights = dot(value_turned[...], grads[unit, span, :], NT)
             dscores = (held_weights.astype(jnp.float32) * (dweights - delta)).astype(jnp.bfloat16)
-
-            @pl.when(step >= 2)
-            def _():
-                copy_out(step - 2).wait()
-
-            out[slot] = dscores
-            copy_out(step).start()
+            out.write(step, dscores)
             grad_query = dot(keys_t[unit], dscores) * scale
             held_out[unit, span, :] = jnp.concatenate([mixed, grad_query], axis=0).T
             return step + 1
 
         return lax.fori_loop(0, pl.cdiv(count, TILE), one_tile, step)
 
-    lax.fori_loop(0, plan.units, one_unit, jnp.int32(0))
-    scatter_units(plan_out, table, held_out, stage, wires_out)
-    for back in (2, 1):
-
-        @pl.when(steps >= back)
-        def _(back=back):
-            copy_out(steps - back).wait()
-
-
-def keys_kernel(plan, table, counts, queries, grads, weights, dscores, *refs):
+    each_unit(plan, counts, one_unit)
+    scatter_units(plan_out, table, me[0], held_out, stage, wires_out)
+    out.finish(steps)
+
+
+def keys_kernel(plan, table, me, counts, queries, grads, weights, dscores, *refs):
     wires_out, refs = refs[: plan.blocks], refs[plan.blocks :]
-    stage, held_out, total, tiles, sems = refs
+    stage, held_out, total, *slots, first_sems, second_sems = refs
+    steps = tile_steps(plan, counts)
+    tiles = Tiles(dscores, slots[0], first_sems), Tiles(weights, slots[1], second_sems)
+    for source in tiles:
+        source.begin(steps)
     scale = 1.0 / math.sqrt(HEAD_DIM)
     lane = lax.broadcasted_iota(jnp.int32, (CLUSTER, PAIR), 1)
-    steps = jnp.int32(0)
-    for unit in range(plan.units):
-        steps = steps + pl.cdiv(counts[unit], TILE)
-
-    def copies_in(step):
-        slot = lax.rem(step, 2)
-        return [
-            pltpu.make_async_copy(
-                source.at[step],
-                tiles.at[slot, :, pl.ds(index * TILE, TILE)],
-                sems.at[slot, index],
-            )
-            for index, source in enumerate((dscores, weights))
-        ]
-
-    @pl.when(steps > 0)
-    def _():
-        for copy in copies_in(0):
-            copy.start()
-
     def one_unit(unit, step):
         total[...] = jnp.zeros_like(total)
 
         def one_tile(tile, step):
-            slot = lax.rem(step, 2)
             span = pl.ds(pl.multiple_of(tile * TILE, TILE), TILE)
-
-            @pl.when(step + 1 < steps)
-            def _():
-                for copy in copies_in(step + 1):
-                    copy.start()
-
-            for copy in copies_in(step):
-                copy.wait()
             total[...] += dot(
-                tiles[slot],
+                jnp.concatenate([source.read(step, steps) for source in tiles], axis=1),
                 jnp.concatenate([queries[unit, span, :], grads[unit, span, :]], axis=0),
             )
             return step + 1
@@ -436,16 +453,16 @@
         held_out[unit, 0:CLUSTER, :] = total[...] * factor
         return step
 
-    lax.fori_loop(0, plan.units, one_unit, jnp.int32(0))
-    scatter_units(plan, table, held_out, stage, wires_out)
+    each_unit(plan, counts, one_unit)
+    scatter_units(plan, table, me[0], held_out, stage, wires_out)
 
 
 SCALARS = pl.BlockSpec(memory_space=pltpu.SMEM)
 WHOLE = pl.BlockSpec(memory_space=pltpu.VMEM)
-APART = pl.BlockSpec(memory_space=pl.ANY)
-
-
-def call(kernel, plan, name, outs, out_specs, in_specs, scratch, flops, args):
+APART = pl.BlockSpec(memory_space=pltpu.HBM)
+
+
+def call(kernel, plan, name, outs, out_specs, in_specs, scratch, flops, args, limit=56):
     shapes = [jax.ShapeDtypeStruct(shape, dtype) for shape, dtype in outs]
     moved = sum(math.prod(shape) * jnp.dtype(dtype).itemsize for shape, dtype in outs)
     return pl.pallas_call(
@@ -454,7 +471,7 @@
         in_specs=in_specs,
         out_specs=out_specs,
         scratch_shapes=scratch,
-        compiler_params=pltpu.CompilerParams(vmem_limit_bytes=VMEM_LIMIT),
+        compiler_params=pltpu.CompilerParams(vmem_limit_bytes=limit * 1024 * 1024),
         cost_estimate=pl.CostEstimate(flops=flops, bytes_accessed=2 * moved, transcendentals=0),
         name=name,
     )(*args)
@@ -476,8 +493,8 @@
     held = pltpu.VMEM((plan.units, CLUSTER + SPARE, PAIR), jnp.float32)
     unit_counts = pltpu.SMEM((plan.units,), jnp.int32)
     unit_block = pltpu.VMEM((CLUSTER, PAIR), narrow)
-    tiles = pltpu.VMEM((2, CLUSTER, TILE), narrow)
-    sems = pltpu.SemaphoreType.DMA((2,))
+    slots = pltpu.VMEM((SLOTS, CLUSTER, TILE), narrow)
+    sems = pltpu.SemaphoreType.DMA((SLOTS,))
 
     def blocks(plan, extra=0):
         lead = () if plan.split else (plan.nodes,)
@@ -488,6 +505,15 @@
 
     def after(value, *others):
         return lax.optimization_barrier((value,) + others)[0]
+
+    def head_swap(value, mask):
+        pairs = [(index, index ^ mask) for index in range(HEAD_DEVICES)]
+        return lax.ppermute(value, "head", pairs)
+
+    def gather_heads(value, beside=None):
+        far = head_swap(value, 2)
+        turned = far if beside is None else after(far, beside)
+        return [value, head_swap(value, 1), far, head_swap(turned, 1)]
 
     def swap(plan, wires):
         if not plan.split:
@@ -500,9 +526,9 @@
 
     named = jnp.arange(plan.total, dtype=jnp.int32)[:, None] == cluster_ids[None, :]
     hist = jnp.sum(named, axis=1, dtype=jnp.int32)
-    all_cotangent = lax.all_gather(cotangent, "head", axis=0, tiled=True)
-    all_weight = lax.all_gather(out_weight, "head", axis=0, tiled=True)
-
+    column = lax.axis_index("head").astype(jnp.int32)
+
+    cotangents = [cotangent] + [head_swap(cotangent, mask) for mask in (1, 2, 3)]
     *wires, pos = call(
         pack_first_kernel, plan, "pack_queries_keys",
         blocks(plan, NOTE) + [((1, rows), jnp.int32)], specs(plan) + [WHOLE],
@@ -511,9 +537,10 @@
     )
     query_wires = swap(plan, wires)
     wires = call(
-        pack_second_kernel, value_plan, "pack_values_grads", blocks(plan), specs(plan),
-        [SCALARS, SCALARS, WHOLE, WHOLE, WHOLE, WHOLE], [starts, ordered], 2 * 10**9,
-        (hist, me, pos, value_rows, out_weight, all_cotangent),
+        pack_second_kernel, value_plan, "pack_values_grads", blocks(value_plan), specs(value_plan),
+        [SCALARS] * 3 + [WHOLE] * (3 + HEAD_DEVICES),
+        [starts, ordered, pltpu.VMEM((HEAD_DEVICES * width, rows), narrow)], 2 * 10**9,
+        [hist, me, column.reshape(1), pos, value_rows, out_weight] + cotangents,
     )
     value_wires = swap(value_plan, wires)
     query_wires = [after(query_wires[0], wires[0])] + query_wires[1:]
@@ -527,23 +554,27 @@
         [(table_shape, jnp.int32), unit_rows_shape, unit_keys_shape, tiles_shape],
         [SCALARS, WHOLE, WHOLE, APART], specs(plan),
         [pltpu.VMEM(table_shape, jnp.int32), stage, held, unit_counts, unit_block, unit_block,
-         tiles, sems, pltpu.SemaphoreType.DMA], 10 * 10**9,
-        query_wires,
-    )
+         pltpu.SemaphoreType.DMA, slots, sems], 10 * 10**9,
+        query_wires, UNIT_LIMIT,
+    )
+    all_weight = gather_heads(after(out_weight, kept_keys))
     *first_wires, dscores, kept_grads, counted = call(
         queries_kernel, (value_plan, first_plan), "attention_and_grad_queries",
-        blocks(plan) + [tiles_shape, unit_rows_shape, ((plan.units,), jnp.int32)],
-        specs(plan) + [APART, WHOLE, SCALARS], [SCALARS] + specs(plan) + [WHOLE, APART],
-        [stage, held, unit_counts, unit_block, pltpu.VMEM((PAIR, CLUSTER), narrow), held, tiles,
-         tiles, sems, sems], 10 * 10**9,
-        [table] + value_wires + [kept_keys, weights],
-    )
+        blocks(first_plan) + [tiles_shape, unit_rows_shape, ((plan.units,), jnp.int32)],
+        specs(first_plan) + [APART, WHOLE, SCALARS],
+        [SCALARS] * 2 + specs(value_plan) + [WHOLE, APART],
+        [stage, held, unit_counts, unit_block, pltpu.VMEM((PAIR, CLUSTER), narrow), held, slots,
+         sems, slots, sems], 10 * 10**9,
+        [table, me] + value_wires + [kept_keys, weights], UNIT_LIMIT,
+    )
+    counted = after(counted, *all_weight[1:3])
     second_wires = call(
-        keys_kernel, second_plan, "grad_keys_and_grad_values", blocks(plan), specs(plan),
-        [SCALARS, SCALARS, WHOLE, WHOLE, APART, APART],
-        [stage, held, pltpu.VMEM((CLUSTER, PAIR), jnp.float32),
-         pltpu.VMEM((2, CLUSTER, 2 * TILE), narrow), pltpu.SemaphoreType.DMA((2, 2))], 10 * 10**9,
-        [table, counted, kept_queries, kept_grads, weights, dscores],
+        keys_kernel, second_plan, "grad_keys_and_grad_values",
+        blocks(second_plan), specs(second_plan),
+        [SCALARS, SCALARS, SCALARS, WHOLE, WHOLE, APART, APART],
+        [stage, held, pltpu.VMEM((CLUSTER, PAIR), jnp.float32), slots, slots, sems, sems],
+        10 * 10**9,
+        [table, me, counted, kept_queries, kept_grads, weights, dscores], UNIT_LIMIT,
     )
 
     def unpack(plan, wires, name):
@@ -558,12 +589,14 @@
     second_back = swap(second_plan, second_wires)
     first_back = [after(first_back[0], second_wires[0])] + first_back[1:]
     attention, grad_queries = unpack(first_plan, first_back, "unpack_attention_grad_queries")
+    (output,) = call(
+        project_kernel, plan, "project", [home_shape], [WHOLE],
+        [SCALARS] + [WHOLE] * (2 * HEAD_DEVICES),
+        [pltpu.VMEM((HEAD_DEVICES, width, width), narrow)], 10**9,
+        [column.reshape(1)] + all_weight + gather_heads(attention),
+    )
+    second_back[0] = after(second_back[0], output)
     grad_keys, grad_values = unpack(second_plan, second_back, "unpack_grad_keys_grad_values")
-    all_attention = lax.all_gather(attention, "head", axis=0, tiled=True)
-    mine = lax.dynamic_slice_in_dim(all_weight, lax.axis_index("head") * width, width, 1)
-    output = lax.dot_general(
-        mine, all_attention, (((0,), (0,)), ((), ())), preferred_element_type=jnp.float32
-    ).astype(narrow)
     return (output, grad_queries, grad_keys, grad_values)
 
 

time: 186 us -> 173 us (0.930)
  waiting for transfers between devices: 20.2 us -> 48.6 us
  starting transfers between devices: 66.3 us -> 48.2 us
  between operations: 14.1 us -> 0.79 us
  Pallas kernels: 78.1 us -> 70.6 us
  matrix products: 2.94 us -> 0 us
    ppermute x28 -> x14, starting transfers between devices: 66.2 us -> 31.6 us  [swap(): arrived[index] = lax.ppermute(wires[index], 'node', pairs)]
    ppermute x0 -> x9, waiting for transfers between devices: none -> 18.5 us  [head_swap(): return lax.ppermute(value, 'head', pairs)]
    all_to_all x0 -> x2, waiting for transfers between devices: none -> 17.1 us  [swap(): lax.all_to_all(wires[0], 'node', split_axis=0, concat_axis=0, tiled=True)]
    all_to_all x0 -> x2, starting transfers between devices: none -> 9.75 us  [swap(): lax.all_to_all(wires[0], 'node', split_axis=0, concat_axis=0, tiled=True)]
    pallas_call x7 -> x8, Pallas kernels: 78.1 us -> 70.6 us  [call(): pl.pallas_call(functools.partial(kernel, plan), out_shape=shapes, in_spec...]
    ppermute x0 -> x9, starting transfers between devices: none -> 6.85 us  [head_swap(): return lax.ppermute(value, 'head', pairs)]
    ppermute x28 -> x14, waiting for transfers between devices: 19.5 us -> 12.9 us  [swap(): arrived[index] = lax.ppermute(wires[index], 'node', pairs)]
    dot_general x1 -> x0, matrix products: 2.94 us -> none  [body(): lax.dot_general(mine, all_attention, (((0,), (0,)), ((), ())), preferred_...]
  transfers between devices with their start and end apart: 31 -> 25, of which waited for: 8 -> 12; matrix products, arithmetic and copies ran while one was open for 1% -> 1% of each run, Pallas kernels for 42% -> 27%
where the time goes in v4:
time: 173 us; the launch traced here: 172 us
  Pallas kernels  70.6 us (41%)
  waiting for transfers between devices  48.6 us (28%)
  starting transfers between devices  48.2 us (28%)
  local copies, waits for them, and re-layouts  2.73 us (2%)
    pallas_call x8, Pallas kernels, call(): pl.pallas_call(functools.partial(kernel, plan), out_shape=shapes, in_spec...  70.6 us
    ppermute x14, starting transfers between devices, swap(): arrived[index] = lax.ppermute(wires[index], 'node', pairs)  31.6 us
    ppermute x9, waiting for transfers between devices, head_swap(): return lax.ppermute(value, 'head', pairs)  18.5 us
    all_to_all x2, waiting for transfers between devices, swap(): lax.all_to_all(wires[0], 'node', split_axis=0, concat_axis=0, tiled=True)  17.1 us
    ppermute x14, waiting for transfers between devices, swap(): arrived[index] = lax.ppermute(wires[index], 'node', pairs)  12.9 us
    all_to_all x2, starting transfers between devices, swap(): lax.all_to_all(wires[0], 'node', split_axis=0, concat_axis=0, tiled=True)  9.75 us
    ppermute x9, starting transfers between devices, head_swap(): return lax.ppermute(value, 'head', pairs)  6.85 us
  transfers between devices with their start and end apart: 25, of which 12 were waited for; matrix products, arithmetic and copies ran while one was open for 1% of the time, Pallas kernels for 27%

profile of v4, /device:TPU:0, one launch (start us, length us, event | category | flops | bytes accessed | tf_op | source)
XLA Modules:
  0.0 172.4 jit_solution(2011663788630259265)
XLA Ops:
  0.6 0.5 collective-permute-start
  1.1 2.6 %collective-permute-start.1 = (bf16[192,1024]{1,0:T(8,128)(2,1)}, bf16[192,1024]{1,0:T(8,128)(2,1)S(1)}, u32[]{:S(2)}, u32[]{:S(2)}) collective-permute-start(bf16[192,1024]{1,0:T(8,128)(2,1)} %refs_0_.1), channel_id=1, source_target_pairs={{0,2},{1,3},{2,0},{3,1},{4,6},{5,7},{6,4},{7,5},{8,10},{9,11},{10,... | collective-permute-start | bytes 1179656 | tf_op jit(solution)/shard_map/ppermute | solution.py:511
  3.7 0.1 collective-permute-start.2
  3.8 1.4 convert_reduce_fusion.hist
  5.2 5.0 %pack_queries_keys.1 = (bf16[656,128]{1,0:T(8,128)(2,1)}, bf16[656,128]{1,0:T(8,128)(2,1)}, bf16[656,128]{1,0:T(8,128)(2,1)}, bf16[656,128]{1,0:T(8,128)(2,1)}, ...) custom-call(s32[16]{0:T(128)} %convert_reduce_fusion.hist, ...), custom_call_target="tpu_custom_call" | custom-call | flops 2000000000 | bytes 2695168 | tf_op jit(solution)/shard_map/pack_queries_keys/pallas_call | solution.py:468
  10.2 4.7 %collective-permute-start.3 = (bf16[656,128]{1,0:T(8,128)(2,1)}, bf16[656,128]{1,0:T(8,128)(2,1)S(1)}, u32[]{:S(2)}, u32[]{:S(2)}) collective-permute-start(bf16[656,128]{1,0:T(8,128)(2,1)} %get-tuple-element.42), channel_id=1, source_target_pairs={{0,28},{4,24},{8,20},{12,16},{16,12},{20,8},{24,4},{28,0},{1,29},{... | collective-permute-start | bytes 503816 | tf_op jit(solution)/shard_map/ppermute | solution.py:524
  14.9 0.2 collective-permute-start.4
  15.1 5.2 %collective-permute-done.3.refs_1_ = bf16[656,128]{1,0:T(8,128)(2,1)S(1)} collective-permute-done((bf16[656,128]{1,0:T(8,128)(2,1)}, bf16[656,128]{1,0:T(8,128)(2,1)S(1)}, u32[]{:S(2)}, u32[]{:S(2)}) %collective-permute-start.3) | collective-permute-done | bytes 167968 | tf_op jit(solution)/shard_map/ppermute | solution.py:524
  20.4 9.0 %collective-permute-start.5 = (bf16[656,128]{1,0:T(8,128)(2,1)}, bf16[656,128]{1,0:T(8,128)(2,1)S(1)}, u32[]{:S(2)}, u32[]{:S(2)}) collective-permute-start(bf16[656,128]{1,0:T(8,128)(2,1)} %get-tuple-element.44), channel_id=1, source_target_pairs={{0,20},{4,16},{8,28},{12,24},{16,4},{20,0},{24,12},{28,8},{1,21},{... | collective-permute-start | bytes 503816 | tf_op jit(solution)/shard_map/ppermute | solution.py:524
  29.3 0.0 collective-permute-done.4.refs_2_
  29.3 2.7 %collective-permute-start.6 = (bf16[656,128]{1,0:T(8,128)(2,1)}, bf16[656,128]{1,0:T(8,128)(2,1)S(1)}, u32[]{:S(2)}, u32[]{:S(2)}) collective-permute-start(bf16[656,128]{1,0:T(8,128)(2,1)} %get-tuple-element.45), channel_id=1, source_target_pairs={{0,16},{4,20},{8,24},{12,28},{16,0},{20,4},{24,8},{28,12},{1,17},{... | collective-permute-start | bytes 503816 | tf_op jit(solution)/shard_map/ppermute | solution.py:524
  32.0 0.0 collective-permute-done.refs_1_
  32.0 0.0 collective-permute-start.7
  32.0 0.0 collective-permute-done.1.refs_2_
  32.0 2.0 %collective-permute-start.8 = (bf16[656,128]{1,0:T(8,128)(2,1)}, bf16[656,128]{1,0:T(8,128)(2,1)S(1)}, u32[]{:S(2)}, u32[]{:S(2)}) collective-permute-start(bf16[656,128]{1,0:T(8,128)(2,1)} %get-tuple-element.47), channel_id=1, source_target_pairs={{0,8},{4,12},{8,0},{12,4},{16,24},{20,28},{24,16},{28,20},{1,9},{5... | collective-permute-start | bytes 503816 | tf_op jit(solution)/shard_map/ppermute | solution.py:524
  34.0 0.0 collective-permute-done.2.refs_3_
  34.0 1.5 collective-permute-start.9
  35.5 5.3 %pack_values_grads.1 = (bf16[640,128]{1,0:T(8,128)(2,1)}, bf16[640,128]{1,0:T(8,128)(2,1)}, bf16[640,128]{1,0:T(8,128)(2,1)}, bf16[640,128]{1,0:T(8,128)(2,1)}, ...) custom-call(s32[16]{0:T(128)} %convert_reduce_fusion.hist, ...), custom_call_target="tpu_custom_call" | custom-call | flops 2000000000 | bytes 2621440 | tf_op jit(solution)/shard_map/pack_values_grads/pallas_call | solution.py:468
  40.8 0.6 collective-permute-done.5.refs_3_
  41.4 1.4 collective-permute-start.13
  42.8 1.6 collective-permute-done.6.refs_4_
  44.4 0.0 collective-permute-start.14
  44.4 2.0 %collective-permute-done.7.refs_5_ = bf16[656,128]{1,0:T(8,128)(2,1)S(1)} collective-permute-done((bf16[656,128]{1,0:T(8,128)(2,1)}, bf16[656,128]{1,0:T(8,128)(2,1)S(1)}, u32[]{:S(2)}, u32[]{:S(2)}) %collective-permute-start.7) | collective-permute-done | bytes 167968 | tf_op jit(solution)/shard_map/ppermute | solution.py:524
  46.4 0.4 collective-permute-start.15
  46.8 0.7 collective-permute-done.8.refs_6_
  47.5 2.6 %collective-permute-start.16 = (bf16[640,128]{1,0:T(8,128)(2,1)}, bf16[640,128]{1,0:T(8,128)(2,1)S(1)}, u32[]{:S(2)}, u32[]{:S(2)}) collective-permute-start(bf16[640,128]{1,0:T(8,128)(2,1)} %get-tuple-element.55), channel_id=1, source_target_pairs={{0,24},{4,28},{8,16},{12,20},{16,8},{20,12},{24,0},{28,4},{1,25},{... | collective-permute-start | bytes 491528 | tf_op jit(solution)/shard_map/ppermute | solution.py:524
  50.2 0.0 collective-permute-done.9.refs_7_
  50.2 0.5 collective-permute-start.17
  50.7 0.0 collective-permute-done.13.refs_1_
  50.7 3.3 %collective-permute-start.18 = (bf16[640,128]{1,0:T(8,128)(2,1)}, bf16[640,128]{1,0:T(8,128)(2,1)S(1)}, u32[]{:S(2)}, u32[]{:S(2)}) collective-permute-start(bf16[640,128]{1,0:T(8,128)(2,1)} %get-tuple-element.57), channel_id=1, source_target_pairs={{0,16},{4,20},{8,24},{12,28},{16,0},{20,4},{24,8},{28,12},{1,17},{... | collective-permute-start | bytes 491528 | tf_op jit(solution)/shard_map/ppermute | solution.py:524
  54.0 0.0 collective-permute-done.14.refs_2_
  54.0 3.3 %collective-permute-start.19 = (bf16[640,128]{1,0:T(8,128)(2,1)}, bf16[640,128]{1,0:T(8,128)(2,1)S(1)}, u32[]{:S(2)}, u32[]{:S(2)}) collective-permute-start(bf16[640,128]{1,0:T(8,128)(2,1)} %get-tuple-element.58), channel_id=1, source_target_pairs={{0,12},{4,8},{8,4},{12,0},{16,28},{20,24},{24,20},{28,16},{1,13},{... | collective-permute-start | bytes 491528 | tf_op jit(solution)/shard_map/ppermute | solution.py:524
  57.3 15.7 %weights.1 = (s32[8,128]{1,0:T(8,128)S(1)}, bf16[6,1024,128]{2,1,0:T(8,128)(2,1)}, bf16[6,64,1024]{2,1,0:T(8,128)(2,1)}, bf16[24,1024,256]{2,1,0:T(8,128)(2,1)}) custom-call(bf16[656,128]{1,0:T(8,128)(2,1)S(1)} %copy-done.1, bf16[656,128]{1,0:T(8,128)(2,1)S(1)} %collective-permute-done.3.refs_1_, bf16[656,128]{1,0:T(8,128)(2,1)S(1)} %collective-permute-done.4.refs_2_, ...), custom_call_target="tpu_custom_call" | custom-call | flops 10000000000 | bytes 29892608 | tf_op jit(solution)/shard_map/weights/pallas_call | solution.py:468
  73.0 0.0 collective-permute-done.15.refs_3_
  73.0 0.0 collective-permute-done.16.refs_4_
  73.0 1.7 collective-permute-done.17.refs_5_
  74.7 1.0 collective-permute-done.18.refs_6_
  75.8 0.0 collective-permute-done.19.refs_7_
  75.8 19.7 %attention_and_grad_queries.1 = (bf16[8,640,128]{2,1,0:T(8,128)(2,1)}, bf16[24,1024,256]{2,1,0:T(8,128)(2,1)}, bf16[6,1024,128]{2,1,0:T(8,128)(2,1)}, s32[6]{0:T(128)S(1)}) custom-call(s32[8,128]{1,0:T(8,128)S(1)} %get-tuple-element.51.table, s32[1]{0:T(128)} %bitcast.1.me, bf16[640,128]{1,0:T(8,128)(2,1)S(1)} %copy-done, ...), custom_call_target="tpu_custom_call" | custom-call | flops 10000000000 | bytes 30933040 | tf_op jit(solution)/shard_map/attention_and_grad_queries/pallas_call | solution.py:468
  95.5 0.0 copy-start.10
  95.5 6.0 %all-to-all-start = ((bf16[8,640,128]{2,1,0:T(8,128)(2,1)}), bf16[8,640,128]{2,1,0:T(8,128)(2,1)S(1)}, u32[]{:S(2)}, u32[]{:S(2)}) async-start(bf16[8,640,128]{2,1,0:T(8,128)(2,1)} %get-tuple-element.60), calls=%async_computation | async-start | bytes 2621440 | tf_op jit(solution)/shard_map/all_to_all | solution.py:520
  101.5 0.1 collective-permute-start.10
  101.6 1.6 collective-permute-start.11
  103.2 0.0 collective-permute-done.10.refs_1_
  103.2 7.8 %collective-permute-done.11.refs_2_ = bf16[192,768]{1,0:T(8,128)(2,1)S(1)} collective-permute-done((bf16[192,768]{1,0:T(8,128)(2,1)S(1)}, bf16[192,768]{1,0:T(8,128)(2,1)S(1)}, u32[]{:S(2)}, u32[]{:S(2)}) %collective-permute-start.11) | collective-permute-done | bytes 294944 | tf_op jit(solution)/shard_map/ppermute | solution.py:511
  111.0 13.6 %grad_keys_and_grad_values.1 = bf16[8,640,128]{2,1,0:T(8,128)(2,1)} custom-call(s32[8,128]{1,0:T(8,128)S(1)} %get-tuple-element.51.table, s32[1]{0:T(128)} %bitcast.1.me, s32[6]{0:T(128)S(1)} %get-tuple-element.62.counts, bf16[6,1024,128]{2,1,0:T(8,128)(2,1)} %get-tuple-element.63.queries, bf16[6,1024,128]{2,1,0:T(8,128)(2,1)} %get-tuple-element.64.grads, ...), custom_call_target="tpu_custom_call" | custom-call | flops 10000000000 | bytes 2621440 | tf_op jit(solution)/shard_map/grad_keys_and_grad_values/pallas_call | solution.py:468
  124.6 7.5 %all-to-all-done.refs_0_ = bf16[8,640,128]{2,1,0:T(8,128)(2,1)S(1)} async-done(((bf16[8,640,128]{2,1,0:T(8,128)(2,1)}), bf16[8,640,128]{2,1,0:T(8,128)(2,1)S(1)}, u32[]{:S(2)}, u32[]{:S(2)}) %all-to-all-start) | async-done | bytes 1310752 | tf_op jit(solution)/shard_map/all_to_all | solution.py:520
  132.1 3.8 %all-to-all-start.1 = ((bf16[8,640,128]{2,1,0:T(8,128)(2,1)}), bf16[8,640,128]{2,1,0:T(8,128)(2,1)S(1)}, u32[]{:S(2)}, u32[]{:S(2)}) async-start(bf16[8,640,128]{2,1,0:T(8,128)(2,1)} %grad_keys_and_grad_values.1), calls=%async_computation.1 | async-start | bytes 2621440 | tf_op jit(solution)/shard_map/all_to_all | solution.py:520
  135.8 4.2 %unpack_attention_grad_queries.1 = (bf16[192,1024]{1,0:T(8,128)(2,1)}, bf16[192,1024]{1,0:T(8,128)(2,1)}) custom-call(s32[16]{0:T(128)} %convert_reduce_fusion.hist, s32[1]{0:T(128)} %bitcast.1.me, s32[1,1024]{1,0:T(1,128)} %get-tuple-element.39.pos, bf16[8,640,128]{2,1,0:T(8,128)(2,1)} %copy-done.3), custom_call_target="tpu_custom_call" | custom-call | flops 2000000000 | bytes 1572864 | tf_op jit(solution)/shard_map/unpack_attention_grad_queries/pallas_call | solution.py:468
  140.0 1.5 collective-permute-start.21
  141.5 0.0 collective-permute-start.20
  141.5 9.1 %collective-permute-done.21.refs_6_ = bf16[192,1024]{1,0:T(8,128)(2,1)S(1)} collective-permute-done((bf16[192,1024]{1,0:T(8,128)(2,1)}, bf16[192,1024]{1,0:T(8,128)(2,1)S(1)}, u32[]{:S(2)}, u32[]{:S(2)}) %collective-permute-start.21) | collective-permute-done | bytes 393248 | tf_op jit(solution)/shard_map/ppermute | solution.py:511
  150.6 0.0 collective-permute-start.22
  150.6 0.5 collective-permute-start.12
  151.1 1.6 collective-permute-done.12.refs_3_
  152.7 0.0 collective-permute-done.20.refs_5_
  152.7 0.0 collective-permute-done.22.refs_7_
  152.7 0.7 copy-done.13
  153.4 0.1 copy-done.8
  153.6 0.8 copy-done.9
  154.3 3.1 %project.1 = bf16[192,1024]{1,0:T(8,128)(2,1)} custom-call(s32[1]{0:T(128)} %bitcast.column, bf16[192,768]{1,0:T(8,128)(2,1)} %refs_0_.2, bf16[192,768]{1,0:T(8,128)(2,1)} %copy-done.11, bf16[192,768]{1,0:T(8,128)(2,1)} %copy-done.12, bf16[192,768]{1,0:T(8,128)(2,1)} %copy-done.13, bf16[192,1024]{1,0:T(8,128)(2,1)} %get-tuple-element.67.refs_4_, ...), custom_call_target="tpu_custom_call" | custom-call | flops 1000000000 | bytes 786432 | tf_op jit(solution)/shard_map/project/pallas_call | solution.py:468
  157.4 9.7 %all-to-all-done.1.refs_0_ = bf16[8,640,128]{2,1,0:T(8,128)(2,1)S(1)} async-done(((bf16[8,640,128]{2,1,0:T(8,128)(2,1)}), bf16[8,640,128]{2,1,0:T(8,128)(2,1)S(1)}, u32[]{:S(2)}, u32[]{:S(2)}) %all-to-all-start.1) | async-done | bytes 1310752 | tf_op jit(solution)/shard_map/all_to_all | solution.py:520
  167.1 1.1 copy-done.2
  168.2 4.2 %unpack_grad_keys_grad_values.1 = (bf16[192,1024]{1,0:T(8,128)(2,1)}, bf16[192,1024]{1,0:T(8,128)(2,1)}) custom-call(s32[16]{0:T(128)} %convert_reduce_fusion.hist, s32[1]{0:T(128)} %bitcast.1.me, s32[1,1024]{1,0:T(1,128)} %get-tuple-element.39.pos, bf16[8,640,128]{2,1,0:T(8,128)(2,1)} %copy-done.2), custom_call_target="tpu_custom_call" | custom-call | flops 2000000000 | bytes 1572864 | tf_op jit(solution)/shard_map/unpack_grad_keys_grad_values/pallas_call | solution.py:468
  (23 shorter events, 0.0 us)
Async XLA Ops:
  0.6 31.4 %collective-permute-start = (bf16[192,1024]{1,0:T(8,128)(2,1)}, bf16[192,1024]{1,0:T(8,128)(2,1)S(1)}, u32[]{:S(2)}, u32[]{:S(2)}) collective-permute-start(bf16[192,1024]{1,0:T(8,128)(2,1)} %refs_0_.1), channel_id=1, source_target_pairs={{0,1},{1,0},{2,3},{3,2},{4,5},{5,4},{6,7},{7,6},{8,9},{9,8},{10,11... | collective-permute-start | bytes 1179656 | tf_op jit(solution)/shard_map/ppermute | solution.py:511
  1.1 30.9 %collective-permute-start.1 = (bf16[192,1024]{1,0:T(8,128)(2,1)}, bf16[192,1024]{1,0:T(8,128)(2,1)S(1)}, u32[]{:S(2)}, u32[]{:S(2)}) collective-permute-start(bf16[192,1024]{1,0:T(8,128)(2,1)} %refs_0_.1), channel_id=1, source_target_pairs={{0,2},{1,3},{2,0},{3,1},{4,6},{5,7},{6,4},{7,5},{8,10},{9,11},{10,... | collective-permute-start | bytes 1179656 | tf_op jit(solution)/shard_map/ppermute | solution.py:511
  3.7 30.3 %collective-permute-start.2 = (bf16[192,1024]{1,0:T(8,128)(2,1)}, bf16[192,1024]{1,0:T(8,128)(2,1)S(1)}, u32[]{:S(2)}, u32[]{:S(2)}) collective-permute-start(bf16[192,1024]{1,0:T(8,128)(2,1)} %refs_0_.1), channel_id=1, source_target_pairs={{0,3},{1,2},{2,1},{3,0},{4,7},{5,6},{6,5},{7,4},{8,11},{9,10},{10,... | collective-permute-start | bytes 1179656 | tf_op jit(solution)/shard_map/ppermute | solution.py:511
  10.2 10.2 %collective-permute-start.3 = (bf16[656,128]{1,0:T(8,128)(2,1)}, bf16[656,128]{1,0:T(8,128)(2,1)S(1)}, u32[]{:S(2)}, u32[]{:S(2)}) collective-permute-start(bf16[656,128]{1,0:T(8,128)(2,1)} %get-tuple-element.42), channel_id=1, source_target_pairs={{0,28},{4,24},{8,20},{12,16},{16,12},{20,8},{24,4},{28,0},{1,29},{... | collective-permute-start | bytes 503816 | tf_op jit(solution)/shard_map/ppermute | solution.py:524
  14.9 14.4 %collective-permute-start.4 = (bf16[656,128]{1,0:T(8,128)(2,1)}, bf16[656,128]{1,0:T(8,128)(2,1)S(1)}, u32[]{:S(2)}, u32[]{:S(2)}) collective-permute-start(bf16[656,128]{1,0:T(8,128)(2,1)} %get-tuple-element.43), channel_id=1, source_target_pairs={{0,24},{4,28},{8,16},{12,20},{16,8},{20,12},{24,0},{28,4},{1,25},{... | collective-permute-start | bytes 503816 | tf_op jit(solution)/shard_map/ppermute | solution.py:524
  20.4 21.1 %collective-permute-start.5 = (bf16[656,128]{1,0:T(8,128)(2,1)}, bf16[656,128]{1,0:T(8,128)(2,1)S(1)}, u32[]{:S(2)}, u32[]{:S(2)}) collective-permute-start(bf16[656,128]{1,0:T(8,128)(2,1)} %get-tuple-element.44), channel_id=1, source_target_pairs={{0,20},{4,16},{8,28},{12,24},{16,4},{20,0},{24,12},{28,8},{1,21},{... | collective-permute-start | bytes 503816 | tf_op jit(solution)/shard_map/ppermute | solution.py:524
  29.3 15.1 %collective-permute-start.6 = (bf16[656,128]{1,0:T(8,128)(2,1)}, bf16[656,128]{1,0:T(8,128)(2,1)S(1)}, u32[]{:S(2)}, u32[]{:S(2)}) collective-permute-start(bf16[656,128]{1,0:T(8,128)(2,1)} %get-tuple-element.45), channel_id=1, source_target_pairs={{0,16},{4,20},{8,24},{12,28},{16,0},{20,4},{24,8},{28,12},{1,17},{... | collective-permute-start | bytes 503816 | tf_op jit(solution)/shard_map/ppermute | solution.py:524
  32.0 3.5 %copy-start.4 = (bf16[192,1024]{1,0:T(8,128)(2,1)}, bf16[192,1024]{1,0:T(8,128)(2,1)S(1)}, u32[]{:S(2)}) copy-start(bf16[192,1024]{1,0:T(8,128)(2,1)S(1)} %collective-permute-done.refs_1_) | copy-start | bytes 1179652
  32.0 14.4 %collective-permute-start.7 = (bf16[656,128]{1,0:T(8,128)(2,1)}, bf16[656,128]{1,0:T(8,128)(2,1)S(1)}, u32[]{:S(2)}, u32[]{:S(2)}) collective-permute-start(bf16[656,128]{1,0:T(8,128)(2,1)} %get-tuple-element.46), channel_id=1, source_target_pairs={{0,12},{4,8},{8,4},{12,0},{16,28},{20,24},{24,20},{28,16},{1,13},{... | collective-permute-start | bytes 503816 | tf_op jit(solution)/shard_map/ppermute | solution.py:524
  32.0 3.5 %copy-start.5 = (bf16[192,1024]{1,0:T(8,128)(2,1)}, bf16[192,1024]{1,0:T(8,128)(2,1)S(1)}, u32[]{:S(2)}) copy-start(bf16[192,1024]{1,0:T(8,128)(2,1)S(1)} %collective-permute-done.1.refs_2_) | copy-start | bytes 1179652
  32.0 15.5 %collective-permute-start.8 = (bf16[656,128]{1,0:T(8,128)(2,1)}, bf16[656,128]{1,0:T(8,128)(2,1)S(1)}, u32[]{:S(2)}, u32[]{:S(2)}) collective-permute-start(bf16[656,128]{1,0:T(8,128)(2,1)} %get-tuple-element.47), channel_id=1, source_target_pairs={{0,8},{4,12},{8,0},{12,4},{16,24},{20,28},{24,16},{28,20},{1,9},{5... | collective-permute-start | bytes 503816 | tf_op jit(solution)/shard_map/ppermute | solution.py:524
  34.0 1.5 copy-start.6
  34.0 16.1 %collective-permute-start.9 = (bf16[656,128]{1,0:T(8,128)(2,1)}, bf16[656,128]{1,0:T(8,128)(2,1)S(1)}, u32[]{:S(2)}, u32[]{:S(2)}) collective-permute-start(bf16[656,128]{1,0:T(8,128)(2,1)} %get-tuple-element.48), channel_id=1, source_target_pairs={{0,4},{4,0},{8,12},{12,8},{16,20},{20,16},{24,28},{28,24},{1,5},{5... | collective-permute-start | bytes 503816 | tf_op jit(solution)/shard_map/ppermute | solution.py:524
  35.5 21.8 %copy-start.1 = (bf16[656,128]{1,0:T(8,128)(2,1)S(1)}, bf16[656,128]{1,0:T(8,128)(2,1)}, u32[]{:S(2)}) copy-start(bf16[656,128]{1,0:T(8,128)(2,1)} %get-tuple-element.41.refs_0_) | copy-start | bytes 503812
  41.4 9.3 %collective-permute-start.13 = (bf16[640,128]{1,0:T(8,128)(2,1)}, bf16[640,128]{1,0:T(8,128)(2,1)S(1)}, u32[]{:S(2)}, u32[]{:S(2)}) collective-permute-start(bf16[640,128]{1,0:T(8,128)(2,1)} %get-tuple-element.52), channel_id=1, source_target_pairs={{0,4},{4,0},{8,12},{12,8},{16,20},{20,16},{24,28},{28,24},{1,5},{5... | collective-permute-start | bytes 491528 | tf_op jit(solution)/shard_map/ppermute | solution.py:524
  44.4 9.7 %collective-permute-start.14 = (bf16[640,128]{1,0:T(8,128)(2,1)}, bf16[640,128]{1,0:T(8,128)(2,1)S(1)}, u32[]{:S(2)}, u32[]{:S(2)}) collective-permute-start(bf16[640,128]{1,0:T(8,128)(2,1)} %get-tuple-element.53), channel_id=1, source_target_pairs={{0,8},{4,12},{8,0},{12,4},{16,24},{20,28},{24,16},{28,20},{1,9},{5... | collective-permute-start | bytes 491528 | tf_op jit(solution)/shard_map/ppermute | solution.py:524
  46.4 26.6 %collective-permute-start.15 = (bf16[640,128]{1,0:T(8,128)(2,1)}, bf16[640,128]{1,0:T(8,128)(2,1)S(1)}, u32[]{:S(2)}, u32[]{:S(2)}) collective-permute-start(bf16[640,128]{1,0:T(8,128)(2,1)} %get-tuple-element.54), channel_id=1, source_target_pairs={{0,28},{4,24},{8,20},{12,16},{16,12},{20,8},{24,4},{28,0},{1,29},{... | collective-permute-start | bytes 491528 | tf_op jit(solution)/shard_map/ppermute | solution.py:524
  47.5 25.4 %collective-permute-start.16 = (bf16[640,128]{1,0:T(8,128)(2,1)}, bf16[640,128]{1,0:T(8,128)(2,1)S(1)}, u32[]{:S(2)}, u32[]{:S(2)}) collective-permute-start(bf16[640,128]{1,0:T(8,128)(2,1)} %get-tuple-element.55), channel_id=1, source_target_pairs={{0,24},{4,28},{8,16},{12,20},{16,8},{20,12},{24,0},{28,4},{1,25},{... | collective-permute-start | bytes 491528 | tf_op jit(solution)/shard_map/ppermute | solution.py:524
  50.2 24.5 %collective-permute-start.17 = (bf16[640,128]{1,0:T(8,128)(2,1)}, bf16[640,128]{1,0:T(8,128)(2,1)S(1)}, u32[]{:S(2)}, u32[]{:S(2)}) collective-permute-start(bf16[640,128]{1,0:T(8,128)(2,1)} %get-tuple-element.56), channel_id=1, source_target_pairs={{0,20},{4,16},{8,28},{12,24},{16,4},{20,0},{24,12},{28,8},{1,21},{... | collective-permute-start | bytes 491528 | tf_op jit(solution)/shard_map/ppermute | solution.py:524
  50.7 25.1 %collective-permute-start.18 = (bf16[640,128]{1,0:T(8,128)(2,1)}, bf16[640,128]{1,0:T(8,128)(2,1)S(1)}, u32[]{:S(2)}, u32[]{:S(2)}) collective-permute-start(bf16[640,128]{1,0:T(8,128)(2,1)} %get-tuple-element.57), channel_id=1, source_target_pairs={{0,16},{4,20},{8,24},{12,28},{16,0},{20,4},{24,8},{28,12},{1,17},{... | collective-permute-start | bytes 491528 | tf_op jit(solution)/shard_map/ppermute | solution.py:524
  54.0 21.7 %copy-start = (bf16[640,128]{1,0:T(8,128)(2,1)S(1)}, bf16[640,128]{1,0:T(8,128)(2,1)}, u32[]{:S(2)}) copy-start(bf16[640,128]{1,0:T(8,128)(2,1)} %get-tuple-element.40.refs_0_) | copy-start | bytes 491524
  54.0 21.7 %collective-permute-start.19 = (bf16[640,128]{1,0:T(8,128)(2,1)}, bf16[640,128]{1,0:T(8,128)(2,1)S(1)}, u32[]{:S(2)}, u32[]{:S(2)}) collective-permute-start(bf16[640,128]{1,0:T(8,128)(2,1)} %get-tuple-element.58), channel_id=1, source_target_pairs={{0,12},{4,8},{8,4},{12,0},{16,28},{20,24},{24,20},{28,16},{1,13},{... | collective-permute-start | bytes 491528 | tf_op jit(solution)/shard_map/ppermute | solution.py:524
  95.5 6.0 %copy-start.10 = (bf16[192,768]{1,0:T(8,128)(2,1)S(1)}, bf16[192,768]{1,0:T(8,128)(2,1)}, u32[]{:S(2)}) copy-start(bf16[192,768]{1,0:T(8,128)(2,1)} %refs_0_.2) | copy-start | bytes 884740
  95.5 36.6 %all-to-all-start = ((bf16[8,640,128]{2,1,0:T(8,128)(2,1)}), bf16[8,640,128]{2,1,0:T(8,128)(2,1)S(1)}, u32[]{:S(2)}, u32[]{:S(2)}) async-start(bf16[8,640,128]{2,1,0:T(8,128)(2,1)} %get-tuple-element.60), calls=%async_computation | async-start | bytes 2621440 | tf_op jit(solution)/shard_map/all_to_all | solution.py:520
  101.5 1.7 collective-permute-start.10
  101.6 9.4 %collective-permute-start.11 = (bf16[192,768]{1,0:T(8,128)(2,1)S(1)}, bf16[192,768]{1,0:T(8,128)(2,1)S(1)}, u32[]{:S(2)}, u32[]{:S(2)}) collective-permute-start(bf16[192,768]{1,0:T(8,128)(2,1)S(1)} %copy-done.10), channel_id=1, source_target_pairs={{0,2},{1,3},{2,0},{3,1},{4,6},{5,7},{6,4},{7,5},{8,10},{9,11},{10,... | collective-permute-start | bytes 884744 | tf_op jit(solution)/shard_map/ppermute | solution.py:511
  103.2 21.4 %copy-start.11 = (bf16[192,768]{1,0:T(8,128)(2,1)}, bf16[192,768]{1,0:T(8,128)(2,1)S(1)}, u32[]{:S(2)}) copy-start(bf16[192,768]{1,0:T(8,128)(2,1)S(1)} %collective-permute-done.10.refs_1_) | copy-start | bytes 884740
  111.0 39.6 %copy-start.12 = (bf16[192,768]{1,0:T(8,128)(2,1)}, bf16[192,768]{1,0:T(8,128)(2,1)S(1)}, u32[]{:S(2)}) copy-start(bf16[192,768]{1,0:T(8,128)(2,1)S(1)} %collective-permute-done.11.refs_2_) | copy-start | bytes 884740
  132.1 3.8 %copy-start.3 = (bf16[8,640,128]{2,1,0:T(8,128)(2,1)}, bf16[8,640,128]{2,1,0:T(8,128)(2,1)S(1)}, u32[]{:S(2)}) copy-start(bf16[8,640,128]{2,1,0:T(8,128)(2,1)S(1)} %all-to-all-done.refs_0_) | copy-start | bytes 3932164
  132.1 35.0 %all-to-all-start.1 = ((bf16[8,640,128]{2,1,0:T(8,128)(2,1)}), bf16[8,640,128]{2,1,0:T(8,128)(2,1)S(1)}, u32[]{:S(2)}, u32[]{:S(2)}) async-start(bf16[8,640,128]{2,1,0:T(8,128)(2,1)} %grad_keys_and_grad_values.1), calls=%async_computation.1 | async-start | bytes 2621440 | tf_op jit(solution)/shard_map/all_to_all | solution.py:520
  140.0 10.6 %collective-permute-start.21 = (bf16[192,1024]{1,0:T(8,128)(2,1)}, bf16[192,1024]{1,0:T(8,128)(2,1)S(1)}, u32[]{:S(2)}, u32[]{:S(2)}) collective-permute-start(bf16[192,1024]{1,0:T(8,128)(2,1)} %get-tuple-element.67.refs_4_), channel_id=1, source_target_pairs={{0,2},{1,3},{2,0},{3,1},{4,6},{5,7},{6,4},{7,5},{8,10},{9,11},{10,... | collective-permute-start | bytes 1179656 | tf_op jit(solution)/shard_map/ppermute | solution.py:511
  141.5 11.2 %collective-permute-start.20 = (bf16[192,1024]{1,0:T(8,128)(2,1)}, bf16[192,1024]{1,0:T(8,128)(2,1)S(1)}, u32[]{:S(2)}, u32[]{:S(2)}) collective-permute-start(bf16[192,1024]{1,0:T(8,128)(2,1)} %get-tuple-element.67.refs_4_), channel_id=1, source_target_pairs={{0,1},{1,0},{2,3},{3,2},{4,5},{5,4},{6,7},{7,6},{8,9},{9,8},{10,11... | collective-permute-start | bytes 1179656 | tf_op jit(solution)/shard_map/ppermute | solution.py:511
  150.6 2.2 %copy-start.7 = (bf16[192,1024]{1,0:T(8,128)(2,1)}, bf16[192,1024]{1,0:T(8,128)(2,1)S(1)}, u32[]{:S(2)}) copy-start(bf16[192,1024]{1,0:T(8,128)(2,1)S(1)} %collective-permute-done.21.refs_6_) | copy-start | bytes 1179652
  150.6 2.2 %collective-permute-start.22 = (bf16[192,1024]{1,0:T(8,128)(2,1)S(1)}, bf16[192,1024]{1,0:T(8,128)(2,1)S(1)}, u32[]{:S(2)}, u32[]{:S(2)}) collective-permute-start(bf16[192,1024]{1,0:T(8,128)(2,1)S(1)} %collective-permute-done.21.refs_6_), channel_id=1, source_target_pairs={{0,1},{1,0},{2,3},{3,2},{4,5},{5,4},{6,7},{7,6},{8,9},{9,8},{10,11... | collective-permute-start | bytes 1179656 | tf_op jit(solution)/shard_map/ppermute | solution.py:511
  150.6 2.1 %collective-permute-start.12 = (bf16[192,768]{1,0:T(8,128)(2,1)S(1)}, bf16[192,768]{1,0:T(8,128)(2,1)S(1)}, u32[]{:S(2)}, u32[]{:S(2)}) collective-permute-start(bf16[192,768]{1,0:T(8,128)(2,1)S(1)} %collective-permute-done.11.refs_2_), channel_id=1, source_target_pairs={{0,1},{1,0},{2,3},{3,2},{4,5},{5,4},{6,7},{7,6},{8,9},{9,8},{10,11... | collective-permute-start | bytes 884744 | tf_op jit(solution)/shard_map/ppermute | solution.py:511
  152.7 0.7 copy-start.13
  152.7 0.8 copy-start.8
  153.6 0.8 copy-start.9
  167.1 1.1 copy-start.2

commit v5 on v4

--- a/solution.py
+++ b/solution.py
@@ -16,18 +16,20 @@
 NOTE = 16
 HEAD_DEVICES = 4
 MASKS = (
-    (7, 6, 5, 4, 3, 2, 1),
+    (1, 7, 6, 5, 4, 2, 3),
     (1, 2, 7, 6, 5, 4, 3),
     (),
     (),
 )
 PAIRED_NODES = 8
-UNIT_LIMIT = 52
+UNIT_LIMIT = 46
+SPACE = 16
 SLOTS = 4
 masked_score = -1e30
 
 NT = (((1,), (1,)), ((), ()))
 NN = (((1,), (0,)), ((), ()))
+TN = (((0,), (0,)), ((), ()))
 
 
 def dot(left, right, dims=NN):
@@ -197,14 +199,11 @@
         ]
 
     each_chunk(plan, hist, me[0], starts, visit)
-    source = jnp.concatenate(
-        [ordered[head].astype(jnp.float32).T.astype(jnp.bfloat16) for head in range(plan.heads)],
-        axis=0,
-    )
+    source = jnp.concatenate([ordered[head] for head in range(plan.heads)], axis=1)
     for at in range(0, plan.rows, TILE):
         row = lax.broadcasted_iota(jnp.int32, (plan.rows, TILE), 0)
         pick = (row == pos[:, at : at + TILE]).astype(jnp.bfloat16)
-        out = dot(source, pick).astype(jnp.bfloat16)
+        out = dot(source, pick, TN).astype(jnp.bfloat16)
         for head in range(plan.heads):
             span = slice(head * HEAD_DIM, (head + 1) * HEAD_DIM)
             first[span, at : at + TILE] = out[head * PAIR : head * PAIR + HEAD_DIM, :]
@@ -547,7 +546,7 @@
 
     unit_rows_shape = ((plan.units, CLUSTER, PAIR), narrow)
     unit_keys_shape = ((plan.units, HEAD_DIM, CLUSTER), narrow)
-    tiles_shape = ((plan.tiles, CLUSTER, TILE), narrow)
+    tiles_shape = ((plan.tiles + SPACE, CLUSTER, TILE), narrow)
     table_shape = (plan.nodes, PAIR)
     table, kept_queries, kept_keys, weights = call(
         weights_kernel, plan, "weights",

time: 173 us -> 168 us (0.971)
  Pallas kernels: 70.6 us -> 59.7 us
  waiting for transfers between devices: 48.6 us -> 56.7 us
  starting transfers between devices: 48.2 us -> 43.6 us
  local copies, waits for them, and re-layouts: 2.73 us -> 5.22 us
    pallas_call x8, Pallas kernels: 70.6 us -> 59.7 us  [call(): pl.pallas_call(functools.partial(kernel, plan), out_shape=shapes, in_spec...]
    ppermute x14, waiting for transfers between devices: 12.9 us -> 19.5 us  [swap(): arrived[index] = lax.ppermute(wires[index], 'node', pairs)]
    ppermute x14, starting transfers between devices: 31.6 us -> 26.9 us  [swap(): arrived[index] = lax.ppermute(wires[index], 'node', pairs)]
    unnamed x28 -> x30, local copies, waits for them, and re-layouts: 2.73 us -> 5.22 us
    all_to_all x2, waiting for transfers between devices: 17.1 us -> 19.1 us  [swap(): lax.all_to_all(wires[0], 'node', split_axis=0, concat_axis=0, tiled=True)]
  transfers between devices with their start and end apart: 25 -> 25, of which waited for: 12 -> 10; matrix products, arithmetic and copies ran while one was open for 1% -> 1% of each run, Pallas kernels for 27% -> 24%
where the time goes in v5:
time: 168 us; the launch traced here: 167 us
  Pallas kernels  59.7 us (36%)
  waiting for transfers between devices  56.7 us (34%)
  starting transfers between devices  43.6 us (26%)
  local copies, waits for them, and re-layouts  5.22 us (3%)
    pallas_call x8, Pallas kernels, call(): pl.pallas_call(functools.partial(kernel, plan), out_shape=shapes, in_spec...  59.7 us
    ppermute x14, starting transfers between devices, swap(): arrived[index] = lax.ppermute(wires[index], 'node', pairs)  26.9 us
    ppermute x14, waiting for transfers between devices, swap(): arrived[index] = lax.ppermute(wires[index], 'node', pairs)  19.5 us
    all_to_all x2, waiting for transfers between devices, swap(): lax.all_to_all(wires[0], 'node', split_axis=0, concat_axis=0, tiled=True)  19.1 us
    ppermute x9, waiting for transfers between devices, head_swap(): return lax.ppermute(value, 'head', pairs)  18.1 us
    all_to_all x2, starting transfers between devices, swap(): lax.all_to_all(wires[0], 'node', split_axis=0, concat_axis=0, tiled=True)  9.86 us
    ppermute x9, starting transfers between devices, head_swap(): return lax.ppermute(value, 'head', pairs)  6.87 us
    unnamed x30, local copies, waits for them, and re-layouts  5.22 us
  transfers between devices with their start and end apart: 25, of which 10 were waited for; matrix products, arithmetic and copies ran while one was open for 1% of the time, Pallas kernels for 24%

profile of v5, /device:TPU:0, one launch (start us, length us, event | category | flops | bytes accessed | tf_op | source)
XLA Modules:
  0.0 167.5 jit_solution(2704679150710301670)
XLA Ops:
  0.6 0.5 collective-permute-start
  1.1 2.6 %collective-permute-start.1 = (bf16[192,1024]{1,0:T(8,128)(2,1)}, bf16[192,1024]{1,0:T(8,128)(2,1)S(1)}, u32[]{:S(2)}, u32[]{:S(2)}) collective-permute-start(bf16[192,1024]{1,0:T(8,128)(2,1)} %refs_0_.1), channel_id=1, source_target_pairs={{0,2},{1,3},{2,0},{3,1},{4,6},{5,7},{6,4},{7,5},{8,10},{9,11},{10,... | collective-permute-start | bytes 1179656 | tf_op jit(solution)/shard_map/ppermute | solution.py:510
  3.7 0.1 collective-permute-start.2
  3.8 1.4 convert_reduce_fusion.hist
  5.2 5.0 %pack_queries_keys.1 = (bf16[656,128]{1,0:T(8,128)(2,1)}, bf16[656,128]{1,0:T(8,128)(2,1)}, bf16[656,128]{1,0:T(8,128)(2,1)}, bf16[656,128]{1,0:T(8,128)(2,1)}, ...) custom-call(s32[16]{0:T(128)} %convert_reduce_fusion.hist, ...), custom_call_target="tpu_custom_call" | custom-call | flops 2000000000 | bytes 2695168 | tf_op jit(solution)/shard_map/pack_queries_keys/pallas_call | solution.py:467
  10.2 1.7 %collective-permute-start.3 = (bf16[656,128]{1,0:T(8,128)(2,1)}, bf16[656,128]{1,0:T(8,128)(2,1)S(1)}, u32[]{:S(2)}, u32[]{:S(2)}) collective-permute-start(bf16[656,128]{1,0:T(8,128)(2,1)} %get-tuple-element.42), channel_id=1, source_target_pairs={{0,4},{4,0},{8,12},{12,8},{16,20},{20,16},{24,28},{28,24},{1,5},{5... | collective-permute-start | bytes 503816 | tf_op jit(solution)/shard_map/ppermute | solution.py:523
  11.9 3.6 %collective-permute-start.4 = (bf16[656,128]{1,0:T(8,128)(2,1)}, bf16[656,128]{1,0:T(8,128)(2,1)S(1)}, u32[]{:S(2)}, u32[]{:S(2)}) collective-permute-start(bf16[656,128]{1,0:T(8,128)(2,1)} %get-tuple-element.43), channel_id=1, source_target_pairs={{0,28},{4,24},{8,20},{12,16},{16,12},{20,8},{24,4},{28,0},{1,29},{... | collective-permute-start | bytes 503816 | tf_op jit(solution)/shard_map/ppermute | solution.py:523
  15.5 4.4 %collective-permute-done.3.refs_1_ = bf16[656,128]{1,0:T(8,128)(2,1)S(1)} collective-permute-done((bf16[656,128]{1,0:T(8,128)(2,1)}, bf16[656,128]{1,0:T(8,128)(2,1)S(1)}, u32[]{:S(2)}, u32[]{:S(2)}) %collective-permute-start.3) | collective-permute-done | bytes 167968 | tf_op jit(solution)/shard_map/ppermute | solution.py:523
  19.9 3.6 %collective-permute-start.5 = (bf16[656,128]{1,0:T(8,128)(2,1)}, bf16[656,128]{1,0:T(8,128)(2,1)S(1)}, u32[]{:S(2)}, u32[]{:S(2)}) collective-permute-start(bf16[656,128]{1,0:T(8,128)(2,1)} %get-tuple-element.44), channel_id=1, source_target_pairs={{0,24},{4,28},{8,16},{12,20},{16,8},{20,12},{24,0},{28,4},{1,25},{... | collective-permute-start | bytes 503816 | tf_op jit(solution)/shard_map/ppermute | solution.py:523
  23.5 0.0 collective-permute-done.4.refs_2_
  23.5 4.2 %collective-permute-start.6 = (bf16[656,128]{1,0:T(8,128)(2,1)}, bf16[656,128]{1,0:T(8,128)(2,1)S(1)}, u32[]{:S(2)}, u32[]{:S(2)}) collective-permute-start(bf16[656,128]{1,0:T(8,128)(2,1)} %get-tuple-element.45), channel_id=1, source_target_pairs={{0,20},{4,16},{8,28},{12,24},{16,4},{20,0},{24,12},{28,8},{1,21},{... | collective-permute-start | bytes 503816 | tf_op jit(solution)/shard_map/ppermute | solution.py:523
  27.7 0.0 collective-permute-done.refs_1_
  27.7 0.5 collective-permute-start.7
  28.2 0.0 collective-permute-done.1.refs_2_
  28.2 3.6 %collective-permute-start.8 = (bf16[656,128]{1,0:T(8,128)(2,1)}, bf16[656,128]{1,0:T(8,128)(2,1)S(1)}, u32[]{:S(2)}, u32[]{:S(2)}) collective-permute-start(bf16[656,128]{1,0:T(8,128)(2,1)} %get-tuple-element.47), channel_id=1, source_target_pairs={{0,8},{4,12},{8,0},{12,4},{16,24},{20,28},{24,16},{28,20},{1,9},{5... | collective-permute-start | bytes 503816 | tf_op jit(solution)/shard_map/ppermute | solution.py:523
  31.8 0.0 collective-permute-done.2.refs_3_
  31.8 0.0 collective-permute-start.9
  31.8 0.7 copy-done.6
  32.6 5.3 %pack_values_grads.1 = (bf16[640,128]{1,0:T(8,128)(2,1)}, bf16[640,128]{1,0:T(8,128)(2,1)}, bf16[640,128]{1,0:T(8,128)(2,1)}, bf16[640,128]{1,0:T(8,128)(2,1)}, ...) custom-call(s32[16]{0:T(128)} %convert_reduce_fusion.hist, ...), custom_call_target="tpu_custom_call" | custom-call | flops 2000000000 | bytes 2621440 | tf_op jit(solution)/shard_map/pack_values_grads/pallas_call | solution.py:467
  37.8 0.0 collective-permute-done.5.refs_3_
  37.8 0.9 collective-permute-start.13
  38.7 4.0 %collective-permute-done.6.refs_4_ = bf16[656,128]{1,0:T(8,128)(2,1)S(1)} collective-permute-done((bf16[656,128]{1,0:T(8,128)(2,1)}, bf16[656,128]{1,0:T(8,128)(2,1)S(1)}, u32[]{:S(2)}, u32[]{:S(2)}) %collective-permute-start.6) | collective-permute-done | bytes 167968 | tf_op jit(solution)/shard_map/ppermute | solution.py:523
  42.7 0.0 collective-permute-start.14
  42.7 1.9 %collective-permute-done.7.refs_5_ = bf16[656,128]{1,0:T(8,128)(2,1)S(1)} collective-permute-done((bf16[656,128]{1,0:T(8,128)(2,1)}, bf16[656,128]{1,0:T(8,128)(2,1)S(1)}, u32[]{:S(2)}, u32[]{:S(2)}) %collective-permute-start.7) | collective-permute-done | bytes 167968 | tf_op jit(solution)/shard_map/ppermute | solution.py:523
  44.6 3.4 %collective-permute-start.15 = (bf16[640,128]{1,0:T(8,128)(2,1)}, bf16[640,128]{1,0:T(8,128)(2,1)S(1)}, u32[]{:S(2)}, u32[]{:S(2)}) collective-permute-start(bf16[640,128]{1,0:T(8,128)(2,1)} %get-tuple-element.54), channel_id=1, source_target_pairs={{0,28},{4,24},{8,20},{12,16},{16,12},{20,8},{24,4},{28,0},{1,29},{... | collective-permute-start | bytes 491528 | tf_op jit(solution)/shard_map/ppermute | solution.py:523
  48.0 0.0 collective-permute-done.8.refs_6_
  48.0 1.3 collective-permute-start.16
  49.4 0.0 collective-permute-done.9.refs_7_
  49.4 0.0 collective-permute-start.17
  49.4 0.0 collective-permute-done.13.refs_1_
  49.4 2.9 %collective-permute-start.18 = (bf16[640,128]{1,0:T(8,128)(2,1)}, bf16[640,128]{1,0:T(8,128)(2,1)S(1)}, u32[]{:S(2)}, u32[]{:S(2)}) collective-permute-start(bf16[640,128]{1,0:T(8,128)(2,1)} %get-tuple-element.57), channel_id=1, source_target_pairs={{0,16},{4,20},{8,24},{12,28},{16,0},{20,4},{24,8},{28,12},{1,17},{... | collective-permute-start | bytes 491528 | tf_op jit(solution)/shard_map/ppermute | solution.py:523
  52.3 0.0 collective-permute-done.14.refs_2_
  52.3 1.2 collective-permute-start.19
  53.4 12.6 %weights.1 = (s32[8,128]{1,0:T(8,128)S(1)}, bf16[6,1024,128]{2,1,0:T(8,128)(2,1)S(1)}, bf16[6,64,1024]{2,1,0:T(8,128)(2,1)S(1)}, bf16[40,1024,256]{2,1,0:T(8,128)(2,1)}) custom-call(bf16[656,128]{1,0:T(8,128)(2,1)S(1)} %copy-done.2, bf16[656,128]{1,0:T(8,128)(2,1)S(1)} %collective-permute-done.3.refs_1_, ...), custom_call_target="tpu_custom_call" | custom-call | flops 10000000000 | bytes 46669824 | tf_op jit(solution)/shard_map/weights/pallas_call | solution.py:467
  66.0 0.0 collective-permute-done.15.refs_3_
  66.1 0.0 collective-permute-done.16.refs_4_
  66.1 7.4 %collective-permute-done.17.refs_5_ = bf16[640,128]{1,0:T(8,128)(2,1)S(1)} collective-permute-done((bf16[640,128]{1,0:T(8,128)(2,1)}, bf16[640,128]{1,0:T(8,128)(2,1)S(1)}, u32[]{:S(2)}, u32[]{:S(2)}) %collective-permute-start.17) | collective-permute-done | bytes 163872 | tf_op jit(solution)/shard_map/ppermute | solution.py:523
  73.5 1.8 %collective-permute-done.18.refs_6_ = bf16[640,128]{1,0:T(8,128)(2,1)S(1)} collective-permute-done((bf16[640,128]{1,0:T(8,128)(2,1)}, bf16[640,128]{1,0:T(8,128)(2,1)S(1)}, u32[]{:S(2)}, u32[]{:S(2)}) %collective-permute-start.18) | collective-permute-done | bytes 163872 | tf_op jit(solution)/shard_map/ppermute | solution.py:523
  75.3 0.0 collective-permute-done.19.refs_7_
  75.3 15.3 %attention_and_grad_queries.1 = (bf16[8,640,128]{2,1,0:T(8,128)(2,1)S(1)}, bf16[40,1024,256]{2,1,0:T(8,128)(2,1)}, bf16[6,1024,128]{2,1,0:T(8,128)(2,1)S(1)}, s32[6]{0:T(128)S(1)}) custom-call(s32[8,128]{1,0:T(8,128)S(1)} %get-tuple-element.51.table, s32[1]{0:T(128)} %bitcast.1.me, bf16[640,128]{1,0:T(8,128)(2,1)S(1)} %copy-done.1, ...), custom_call_target="tpu_custom_call" | custom-call | flops 10000000000 | bytes 47710256 | tf_op jit(solution)/shard_map/attention_and_grad_queries/pallas_call | solution.py:467
  90.6 1.1 copy-done
  91.6 6.1 %all-to-all-start = ((bf16[8,640,128]{2,1,0:T(8,128)(2,1)}), bf16[8,640,128]{2,1,0:T(8,128)(2,1)}, u32[]{:S(2)}, u32[]{:S(2)}) async-start(bf16[8,640,128]{2,1,0:T(8,128)(2,1)} %copy-done), calls=%async_computation | async-start | bytes 2621440 | tf_op jit(solution)/shard_map/all_to_all | solution.py:519
  97.8 0.1 collective-permute-start.10
  97.8 1.6 collective-permute-start.11
  99.4 7.8 %collective-permute-done.11.refs_2_ = bf16[192,768]{1,0:T(8,128)(2,1)S(1)} collective-permute-done((bf16[192,768]{1,0:T(8,128)(2,1)S(1)}, bf16[192,768]{1,0:T(8,128)(2,1)S(1)}, u32[]{:S(2)}, u32[]{:S(2)}) %collective-permute-start.11) | collective-permute-done | bytes 294944 | tf_op jit(solution)/shard_map/ppermute | solution.py:510
  107.3 0.7 copy-done.12
  108.0 10.5 %grad_keys_and_grad_values.1 = bf16[8,640,128]{2,1,0:T(8,128)(2,1)} custom-call(s32[8,128]{1,0:T(8,128)S(1)} %get-tuple-element.51.table, s32[1]{0:T(128)} %bitcast.1.me, s32[6]{0:T(128)S(1)} %get-tuple-element.62.counts, bf16[6,1024,128]{2,1,0:T(8,128)(2,1)S(1)} %get-tuple-element.63.queries, bf16[6,1024,128]{2,1,0:T(8,128)(2,1)S(1)} %get-tuple-element.64.grads, ...), custom_call_target="tpu_custom_call" | custom-call | flops 10000000000 | bytes 2621440 | tf_op jit(solution)/shard_map/grad_keys_and_grad_values/pallas_call | solution.py:467
  118.5 9.2 %all-to-all-done.refs_0_ = bf16[8,640,128]{2,1,0:T(8,128)(2,1)} async-done(((bf16[8,640,128]{2,1,0:T(8,128)(2,1)}), bf16[8,640,128]{2,1,0:T(8,128)(2,1)}, u32[]{:S(2)}, u32[]{:S(2)}) %all-to-all-start) | async-done | bytes 1310752 | tf_op jit(solution)/shard_map/all_to_all | solution.py:519
  127.7 3.8 %all-to-all-start.1 = ((bf16[8,640,128]{2,1,0:T(8,128)(2,1)}), bf16[8,640,128]{2,1,0:T(8,128)(2,1)S(1)}, u32[]{:S(2)}, u32[]{:S(2)}) async-start(bf16[8,640,128]{2,1,0:T(8,128)(2,1)} %grad_keys_and_grad_values.1), calls=%async_computation.1 | async-start | bytes 2621440 | tf_op jit(solution)/shard_map/all_to_all | solution.py:519
  131.5 4.0 %unpack_attention_grad_queries.1 = (bf16[192,1024]{1,0:T(8,128)(2,1)}, bf16[192,1024]{1,0:T(8,128)(2,1)}) custom-call(s32[16]{0:T(128)} %convert_reduce_fusion.hist, s32[1]{0:T(128)} %bitcast.1.me, s32[1,1024]{1,0:T(1,128)} %get-tuple-element.39.pos, bf16[8,640,128]{2,1,0:T(8,128)(2,1)} %all-to-all-done.refs_0_), custom_call_target="tpu_custom_call" | custom-call | flops 2000000000 | bytes 1572864 | tf_op jit(solution)/shard_map/unpack_attention_grad_queries/pallas_call | solution.py:467
  135.5 1.5 collective-permute-start.21
  137.0 0.0 collective-permute-start.20
  137.0 8.7 %collective-permute-done.21.refs_6_ = bf16[192,1024]{1,0:T(8,128)(2,1)S(1)} collective-permute-done((bf16[192,1024]{1,0:T(8,128)(2,1)}, bf16[192,1024]{1,0:T(8,128)(2,1)S(1)}, u32[]{:S(2)}, u32[]{:S(2)}) %collective-permute-start.21) | collective-permute-done | bytes 393248 | tf_op jit(solution)/shard_map/ppermute | solution.py:510
  145.7 0.0 collective-permute-start.22
  145.7 0.5 collective-permute-start.12
  146.2 1.6 collective-permute-done.12.refs_3_
  147.9 0.0 collective-permute-done.20.refs_5_
  147.9 0.7 copy-done.14
  148.6 0.1 copy-done.8
  148.7 0.8 copy-done.9
  149.5 3.1 %project.1 = bf16[192,1024]{1,0:T(8,128)(2,1)} custom-call(s32[1]{0:T(128)} %bitcast.column, bf16[192,768]{1,0:T(8,128)(2,1)} %refs_0_.2, bf16[192,768]{1,0:T(8,128)(2,1)} %copy-done.11, bf16[192,768]{1,0:T(8,128)(2,1)} %copy-done.12, bf16[192,768]{1,0:T(8,128)(2,1)} %copy-done.14, bf16[192,1024]{1,0:T(8,128)(2,1)} %get-tuple-element.67.refs_4_, ...), custom_call_target="tpu_custom_call" | custom-call | flops 1000000000 | bytes 786432 | tf_op jit(solution)/shard_map/project/pallas_call | solution.py:467
  152.6 9.9 %all-to-all-done.1.refs_0_ = bf16[8,640,128]{2,1,0:T(8,128)(2,1)S(1)} async-done(((bf16[8,640,128]{2,1,0:T(8,128)(2,1)}), bf16[8,640,128]{2,1,0:T(8,128)(2,1)S(1)}, u32[]{:S(2)}, u32[]{:S(2)}) %all-to-all-start.1) | async-done | bytes 1310752 | tf_op jit(solution)/shard_map/all_to_all | solution.py:519
  162.4 1.1 copy-done.3
  163.5 4.0 %unpack_grad_keys_grad_values.1 = (bf16[192,1024]{1,0:T(8,128)(2,1)}, bf16[192,1024]{1,0:T(8,128)(2,1)}) custom-call(s32[16]{0:T(128)} %convert_reduce_fusion.hist, s32[1]{0:T(128)} %bitcast.1.me, s32[1,1024]{1,0:T(1,128)} %get-tuple-element.39.pos, bf16[8,640,128]{2,1,0:T(8,128)(2,1)} %copy-done.3), custom_call_target="tpu_custom_call" | custom-call | flops 2000000000 | bytes 1572864 | tf_op jit(solution)/shard_map/unpack_grad_keys_grad_values/pallas_call | solution.py:467
  (25 shorter events, 0.0 us)
Async XLA Ops:
  0.6 27.1 %collective-permute-start = (bf16[192,1024]{1,0:T(8,128)(2,1)}, bf16[192,1024]{1,0:T(8,128)(2,1)S(1)}, u32[]{:S(2)}, u32[]{:S(2)}) collective-permute-start(bf16[192,1024]{1,0:T(8,128)(2,1)} %refs_0_.1), channel_id=1, source_target_pairs={{0,1},{1,0},{2,3},{3,2},{4,5},{5,4},{6,7},{7,6},{8,9},{9,8},{10,11... | collective-permute-start | bytes 1179656 | tf_op jit(solution)/shard_map/ppermute | solution.py:510
  1.1 27.1 %collective-permute-start.1 = (bf16[192,1024]{1,0:T(8,128)(2,1)}, bf16[192,1024]{1,0:T(8,128)(2,1)S(1)}, u32[]{:S(2)}, u32[]{:S(2)}) collective-permute-start(bf16[192,1024]{1,0:T(8,128)(2,1)} %refs_0_.1), channel_id=1, source_target_pairs={{0,2},{1,3},{2,0},{3,1},{4,6},{5,7},{6,4},{7,5},{8,10},{9,11},{10,... | collective-permute-start | bytes 1179656 | tf_op jit(solution)/shard_map/ppermute | solution.py:510
  3.7 28.1 %collective-permute-start.2 = (bf16[192,1024]{1,0:T(8,128)(2,1)}, bf16[192,1024]{1,0:T(8,128)(2,1)S(1)}, u32[]{:S(2)}, u32[]{:S(2)}) collective-permute-start(bf16[192,1024]{1,0:T(8,128)(2,1)} %refs_0_.1), channel_id=1, source_target_pairs={{0,3},{1,2},{2,1},{3,0},{4,7},{5,6},{6,5},{7,4},{8,11},{9,10},{10,... | collective-permute-start | bytes 1179656 | tf_op jit(solution)/shard_map/ppermute | solution.py:510
  10.2 9.7 %collective-permute-start.3 = (bf16[656,128]{1,0:T(8,128)(2,1)}, bf16[656,128]{1,0:T(8,128)(2,1)S(1)}, u32[]{:S(2)}, u32[]{:S(2)}) collective-permute-start(bf16[656,128]{1,0:T(8,128)(2,1)} %get-tuple-element.42), channel_id=1, source_target_pairs={{0,4},{4,0},{8,12},{12,8},{16,20},{20,16},{24,28},{28,24},{1,5},{5... | collective-permute-start | bytes 503816 | tf_op jit(solution)/shard_map/ppermute | solution.py:523
  11.9 11.6 %collective-permute-start.4 = (bf16[656,128]{1,0:T(8,128)(2,1)}, bf16[656,128]{1,0:T(8,128)(2,1)S(1)}, u32[]{:S(2)}, u32[]{:S(2)}) collective-permute-start(bf16[656,128]{1,0:T(8,128)(2,1)} %get-tuple-element.43), channel_id=1, source_target_pairs={{0,28},{4,24},{8,20},{12,16},{16,12},{20,8},{24,4},{28,0},{1,29},{... | collective-permute-start | bytes 503816 | tf_op jit(solution)/shard_map/ppermute | solution.py:523
  19.9 17.9 %collective-permute-start.5 = (bf16[656,128]{1,0:T(8,128)(2,1)}, bf16[656,128]{1,0:T(8,128)(2,1)S(1)}, u32[]{:S(2)}, u32[]{:S(2)}) collective-permute-start(bf16[656,128]{1,0:T(8,128)(2,1)} %get-tuple-element.44), channel_id=1, source_target_pairs={{0,24},{4,28},{8,16},{12,20},{16,8},{20,12},{24,0},{28,4},{1,25},{... | collective-permute-start | bytes 503816 | tf_op jit(solution)/shard_map/ppermute | solution.py:523
  23.5 19.2 %collective-permute-start.6 = (bf16[656,128]{1,0:T(8,128)(2,1)}, bf16[656,128]{1,0:T(8,128)(2,1)S(1)}, u32[]{:S(2)}, u32[]{:S(2)}) collective-permute-start(bf16[656,128]{1,0:T(8,128)(2,1)} %get-tuple-element.45), channel_id=1, source_target_pairs={{0,20},{4,16},{8,28},{12,24},{16,4},{20,0},{24,12},{28,8},{1,21},{... | collective-permute-start | bytes 503816 | tf_op jit(solution)/shard_map/ppermute | solution.py:523
  27.7 4.1 %copy-start.4 = (bf16[192,1024]{1,0:T(8,128)(2,1)}, bf16[192,1024]{1,0:T(8,128)(2,1)S(1)}, u32[]{:S(2)}) copy-start(bf16[192,1024]{1,0:T(8,128)(2,1)S(1)} %collective-permute-done.refs_1_) | copy-start | bytes 1179652
  27.7 16.9 %collective-permute-start.7 = (bf16[656,128]{1,0:T(8,128)(2,1)}, bf16[656,128]{1,0:T(8,128)(2,1)S(1)}, u32[]{:S(2)}, u32[]{:S(2)}) collective-permute-start(bf16[656,128]{1,0:T(8,128)(2,1)} %get-tuple-element.46), channel_id=1, source_target_pairs={{0,16},{4,20},{8,24},{12,28},{16,0},{20,4},{24,8},{28,12},{1,17},{... | collective-permute-start | bytes 503816 | tf_op jit(solution)/shard_map/ppermute | solution.py:523
  28.2 3.6 %copy-start.5 = (bf16[192,1024]{1,0:T(8,128)(2,1)}, bf16[192,1024]{1,0:T(8,128)(2,1)S(1)}, u32[]{:S(2)}) copy-start(bf16[192,1024]{1,0:T(8,128)(2,1)S(1)} %collective-permute-done.1.refs_2_) | copy-start | bytes 1179652
  28.2 19.8 %collective-permute-start.8 = (bf16[656,128]{1,0:T(8,128)(2,1)}, bf16[656,128]{1,0:T(8,128)(2,1)S(1)}, u32[]{:S(2)}, u32[]{:S(2)}) collective-permute-start(bf16[656,128]{1,0:T(8,128)(2,1)} %get-tuple-element.47), channel_id=1, source_target_pairs={{0,8},{4,12},{8,0},{12,4},{16,24},{20,28},{24,16},{28,20},{1,9},{5... | collective-permute-start | bytes 503816 | tf_op jit(solution)/shard_map/ppermute | solution.py:523
  31.8 0.7 copy-start.6
  31.8 17.5 %collective-permute-start.9 = (bf16[656,128]{1,0:T(8,128)(2,1)}, bf16[656,128]{1,0:T(8,128)(2,1)S(1)}, u32[]{:S(2)}, u32[]{:S(2)}) collective-permute-start(bf16[656,128]{1,0:T(8,128)(2,1)} %get-tuple-element.48), channel_id=1, source_target_pairs={{0,12},{4,8},{8,4},{12,0},{16,28},{20,24},{24,20},{28,16},{1,13},{... | collective-permute-start | bytes 503816 | tf_op jit(solution)/shard_map/ppermute | solution.py:523
  32.6 20.9 %copy-start.2 = (bf16[656,128]{1,0:T(8,128)(2,1)S(1)}, bf16[656,128]{1,0:T(8,128)(2,1)}, u32[]{:S(2)}) copy-start(bf16[656,128]{1,0:T(8,128)(2,1)} %get-tuple-element.41.refs_0_) | copy-start | bytes 503812
  37.8 11.5 %collective-permute-start.13 = (bf16[640,128]{1,0:T(8,128)(2,1)}, bf16[640,128]{1,0:T(8,128)(2,1)S(1)}, u32[]{:S(2)}, u32[]{:S(2)}) collective-permute-start(bf16[640,128]{1,0:T(8,128)(2,1)} %get-tuple-element.52), channel_id=1, source_target_pairs={{0,4},{4,0},{8,12},{12,8},{16,20},{20,16},{24,28},{28,24},{1,5},{5... | collective-permute-start | bytes 491528 | tf_op jit(solution)/shard_map/ppermute | solution.py:523
  42.7 9.5 %collective-permute-start.14 = (bf16[640,128]{1,0:T(8,128)(2,1)}, bf16[640,128]{1,0:T(8,128)(2,1)S(1)}, u32[]{:S(2)}, u32[]{:S(2)}) collective-permute-start(bf16[640,128]{1,0:T(8,128)(2,1)} %get-tuple-element.53), channel_id=1, source_target_pairs={{0,8},{4,12},{8,0},{12,4},{16,24},{20,28},{24,16},{28,20},{1,9},{5... | collective-permute-start | bytes 491528 | tf_op jit(solution)/shard_map/ppermute | solution.py:523
  44.6 21.5 %collective-permute-start.15 = (bf16[640,128]{1,0:T(8,128)(2,1)}, bf16[640,128]{1,0:T(8,128)(2,1)S(1)}, u32[]{:S(2)}, u32[]{:S(2)}) collective-permute-start(bf16[640,128]{1,0:T(8,128)(2,1)} %get-tuple-element.54), channel_id=1, source_target_pairs={{0,28},{4,24},{8,20},{12,16},{16,12},{20,8},{24,4},{28,0},{1,29},{... | collective-permute-start | bytes 491528 | tf_op jit(solution)/shard_map/ppermute | solution.py:523
  48.0 18.0 %collective-permute-start.16 = (bf16[640,128]{1,0:T(8,128)(2,1)}, bf16[640,128]{1,0:T(8,128)(2,1)S(1)}, u32[]{:S(2)}, u32[]{:S(2)}) collective-permute-start(bf16[640,128]{1,0:T(8,128)(2,1)} %get-tuple-element.55), channel_id=1, source_target_pairs={{0,24},{4,28},{8,16},{12,20},{16,8},{20,12},{24,0},{28,4},{1,25},{... | collective-permute-start | bytes 491528 | tf_op jit(solution)/shard_map/ppermute | solution.py:523
  49.4 24.1 %collective-permute-start.17 = (bf16[640,128]{1,0:T(8,128)(2,1)}, bf16[640,128]{1,0:T(8,128)(2,1)S(1)}, u32[]{:S(2)}, u32[]{:S(2)}) collective-permute-start(bf16[640,128]{1,0:T(8,128)(2,1)} %get-tuple-element.56), channel_id=1, source_target_pairs={{0,20},{4,16},{8,28},{12,24},{16,4},{20,0},{24,12},{28,8},{1,21},{... | collective-permute-start | bytes 491528 | tf_op jit(solution)/shard_map/ppermute | solution.py:523
  49.4 25.9 %collective-permute-start.18 = (bf16[640,128]{1,0:T(8,128)(2,1)}, bf16[640,128]{1,0:T(8,128)(2,1)S(1)}, u32[]{:S(2)}, u32[]{:S(2)}) collective-permute-start(bf16[640,128]{1,0:T(8,128)(2,1)} %get-tuple-element.57), channel_id=1, source_target_pairs={{0,16},{4,20},{8,24},{12,28},{16,0},{20,4},{24,8},{28,12},{1,17},{... | collective-permute-start | bytes 491528 | tf_op jit(solution)/shard_map/ppermute | solution.py:523
  52.3 23.0 %copy-start.1 = (bf16[640,128]{1,0:T(8,128)(2,1)S(1)}, bf16[640,128]{1,0:T(8,128)(2,1)}, u32[]{:S(2)}) copy-start(bf16[640,128]{1,0:T(8,128)(2,1)} %get-tuple-element.40.refs_0_) | copy-start | bytes 491524
  52.3 23.0 %collective-permute-start.19 = (bf16[640,128]{1,0:T(8,128)(2,1)}, bf16[640,128]{1,0:T(8,128)(2,1)S(1)}, u32[]{:S(2)}, u32[]{:S(2)}) collective-permute-start(bf16[640,128]{1,0:T(8,128)(2,1)} %get-tuple-element.58), channel_id=1, source_target_pairs={{0,12},{4,8},{8,4},{12,0},{16,28},{20,24},{24,20},{28,16},{1,13},{... | collective-permute-start | bytes 491528 | tf_op jit(solution)/shard_map/ppermute | solution.py:523
  90.6 1.1 copy-start
  91.6 6.1 %copy-start.10 = (bf16[192,768]{1,0:T(8,128)(2,1)S(1)}, bf16[192,768]{1,0:T(8,128)(2,1)}, u32[]{:S(2)}) copy-start(bf16[192,768]{1,0:T(8,128)(2,1)} %refs_0_.2) | copy-start | bytes 884740
  91.6 36.1 %all-to-all-start = ((bf16[8,640,128]{2,1,0:T(8,128)(2,1)}), bf16[8,640,128]{2,1,0:T(8,128)(2,1)}, u32[]{:S(2)}, u32[]{:S(2)}) async-start(bf16[8,640,128]{2,1,0:T(8,128)(2,1)} %copy-done), calls=%async_computation | async-start | bytes 2621440 | tf_op jit(solution)/shard_map/all_to_all | solution.py:519
  97.8 1.7 collective-permute-start.10
  97.8 9.4 %collective-permute-start.11 = (bf16[192,768]{1,0:T(8,128)(2,1)S(1)}, bf16[192,768]{1,0:T(8,128)(2,1)S(1)}, u32[]{:S(2)}, u32[]{:S(2)}) collective-permute-start(bf16[192,768]{1,0:T(8,128)(2,1)S(1)} %copy-done.10), channel_id=1, source_target_pairs={{0,2},{1,3},{2,0},{3,1},{4,6},{5,7},{6,4},{7,5},{8,10},{9,11},{10,... | collective-permute-start | bytes 884744 | tf_op jit(solution)/shard_map/ppermute | solution.py:510
  99.4 7.8 %copy-start.11 = (bf16[192,768]{1,0:T(8,128)(2,1)}, bf16[192,768]{1,0:T(8,128)(2,1)S(1)}, u32[]{:S(2)}) copy-start(bf16[192,768]{1,0:T(8,128)(2,1)S(1)} %collective-permute-done.10.refs_1_) | copy-start | bytes 884740
  107.3 0.7 copy-start.12
  127.7 34.7 %all-to-all-start.1 = ((bf16[8,640,128]{2,1,0:T(8,128)(2,1)}), bf16[8,640,128]{2,1,0:T(8,128)(2,1)S(1)}, u32[]{:S(2)}, u32[]{:S(2)}) async-start(bf16[8,640,128]{2,1,0:T(8,128)(2,1)} %grad_keys_and_grad_values.1), calls=%async_computation.1 | async-start | bytes 2621440 | tf_op jit(solution)/shard_map/all_to_all | solution.py:519
  131.5 14.2 %copy-start.13 = (bf16[192,768]{1,0:T(8,128)(2,1)S(1)}, bf16[192,768]{1,0:T(8,128)(2,1)}, u32[]{:S(2)}) copy-start(bf16[192,768]{1,0:T(8,128)(2,1)} %copy-done.12) | copy-start | bytes 884740
  135.5 10.2 %collective-permute-start.21 = (bf16[192,1024]{1,0:T(8,128)(2,1)}, bf16[192,1024]{1,0:T(8,128)(2,1)S(1)}, u32[]{:S(2)}, u32[]{:S(2)}) collective-permute-start(bf16[192,1024]{1,0:T(8,128)(2,1)} %get-tuple-element.67.refs_4_), channel_id=1, source_target_pairs={{0,2},{1,3},{2,0},{3,1},{4,6},{5,7},{6,4},{7,5},{8,10},{9,11},{10,... | collective-permute-start | bytes 1179656 | tf_op jit(solution)/shard_map/ppermute | solution.py:510
  137.0 10.8 %collective-permute-start.20 = (bf16[192,1024]{1,0:T(8,128)(2,1)}, bf16[192,1024]{1,0:T(8,128)(2,1)S(1)}, u32[]{:S(2)}, u32[]{:S(2)}) collective-permute-start(bf16[192,1024]{1,0:T(8,128)(2,1)} %get-tuple-element.67.refs_4_), channel_id=1, source_target_pairs={{0,1},{1,0},{2,3},{3,2},{4,5},{5,4},{6,7},{7,6},{8,9},{9,8},{10,11... | collective-permute-start | bytes 1179656 | tf_op jit(solution)/shard_map/ppermute | solution.py:510
  145.7 2.2 %copy-start.7 = (bf16[192,1024]{1,0:T(8,128)(2,1)}, bf16[192,1024]{1,0:T(8,128)(2,1)S(1)}, u32[]{:S(2)}) copy-start(bf16[192,1024]{1,0:T(8,128)(2,1)S(1)} %collective-permute-done.21.refs_6_) | copy-start | bytes 1179652
  145.7 2.2 %collective-permute-start.22 = (bf16[192,1024]{1,0:T(8,128)(2,1)S(1)}, bf16[192,1024]{1,0:T(8,128)(2,1)S(1)}, u32[]{:S(2)}, u32[]{:S(2)}) collective-permute-start(bf16[192,1024]{1,0:T(8,128)(2,1)S(1)} %collective-permute-done.21.refs_6_), channel_id=1, source_target_pairs={{0,1},{1,0},{2,3},{3,2},{4,5},{5,4},{6,7},{7,6},{8,9},{9,8},{10,11... | collective-permute-start | bytes 1179656 | tf_op jit(solution)/shard_map/ppermute | solution.py:510
  145.7 2.1 %collective-permute-start.12 = (bf16[192,768]{1,0:T(8,128)(2,1)S(1)}, bf16[192,768]{1,0:T(8,128)(2,1)S(1)}, u32[]{:S(2)}, u32[]{:S(2)}) collective-permute-start(bf16[192,768]{1,0:T(8,128)(2,1)S(1)} %copy-done.13), channel_id=1, source_target_pairs={{0,1},{1,0},{2,3},{3,2},{4,5},{5,4},{6,7},{7,6},{8,9},{9,8},{10,11... | collective-permute-start | bytes 884744 | tf_op jit(solution)/shard_map/ppermute | solution.py:510
  147.9 0.7 copy-start.14
  147.9 0.8 copy-start.8
  148.7 0.8 copy-start.9
  162.4 1.1 copy-start.3

commit v6 on v5

--- a/solution.py
+++ b/solution.py
@@ -58,7 +58,7 @@
 
 
 def owner_rows(plan, hist, owner):
-    return sum(hist[owner * plan.clusters + index] for index in range(plan.clusters))
+    return sum(hist[owner * plan.clusters + index, 0] for index in range(plan.clusters))
 
 
 def each_block(plan, visit):
@@ -131,9 +131,16 @@
     each_chunk(plan, hist, me, starts, visit)
 
 
-def pack_first_kernel(plan, hist, me, ids, queries, keys, *refs):
-    wires, (pos_out, starts, ordered) = refs[: plan.blocks], refs[plan.blocks :]
+def pack_first_kernel(plan, me, ids, queries, keys, *refs):
+    wires, refs = refs[: plan.blocks], refs[plan.blocks :]
+    pos_out, hist, starts, ordered, counted, hist_sem = refs
     rows = plan.rows
+    cluster = lax.broadcasted_iota(jnp.int32, (plan.total, rows), 0)
+    named = (cluster == ids[...]).astype(jnp.float32)
+    count = jnp.sum(named, axis=1, keepdims=True).astype(jnp.int32)
+    counted[...] = jnp.broadcast_to(count, (plan.total, PAIR))
+    hist_copy = pltpu.make_async_copy(counted, hist, hist_sem)
+    hist_copy.start()
     rank = ids[...] * rows + lax.broadcasted_iota(jnp.int32, (1, rows), 1)
     rank = rank.astype(jnp.float32)
     column = jnp.broadcast_to(rank, (128, rows)).T
@@ -143,6 +150,7 @@
         parts.append(jnp.sum(below, axis=0, keepdims=True))
     pos = jnp.concatenate(parts, axis=1).astype(jnp.int32)
     pos_out[...] = pos
+    hist_copy.wait()
     spread(plan, pos, queries[...], keys[...], hist, me[0], starts, ordered, wires)
     lane = lax.broadcasted_iota(jnp.int32, (NOTE, PAIR), 1)
 
@@ -153,7 +161,7 @@
             owner = lax.rem(dest + plan.shift[head], plan.nodes)
             for cluster in range(plan.clusters):
                 unit = head * plan.clusters + cluster
-                count = hist[owner * plan.clusters + cluster]
+                count = hist[owner * plan.clusters + cluster, 0]
                 counts = jnp.where(lane == unit, count, counts)
         block_of(plan, wires, number)[plan.cap :, :] = counts.astype(jnp.float32).astype(
             jnp.bfloat16
@@ -382,16 +390,15 @@
     out.finish(tile_steps(plan, counts))
 
 
-def queries_kernel(plans, table, me, *refs):
+def attention_kernel(plans, table, me, *refs):
     plan, plan_out = plans
     wires, refs = refs[: plan.blocks], refs[plan.blocks :]
-    keys_t, weights = refs[:2]
-    wires_out, refs = refs[2 : 2 + plan_out.blocks], refs[2 + plan_out.blocks :]
-    (dscores_out, grads, counts_out, stage, held, counts, value_turned, both_t, held_out,
-     slots, sems, slots_out, sems_out) = refs
-    tiles, out = Tiles(weights, slots, sems), Tiles(dscores_out, slots_out, sems_out)
+    weights = refs[0]
+    wires_out, refs = refs[1 : 1 + plan_out.blocks], refs[1 + plan_out.blocks :]
+    (kept, deltas, counts_out, stage, held, counts, grad_rows, both_t, held_out, total, slots,
+     sems) = refs
+    tiles = Tiles(weights, slots, sems)
     gather_units(plan, table, me[0], wires, stage, held, counts)
-    scale = 1.0 / math.sqrt(HEAD_DIM)
     lane = lax.broadcasted_iota(jnp.int32, (CLUSTER, PAIR), 1)
     for unit in range(plan.units):
         counts_out[unit] = counts[unit]
@@ -401,10 +408,10 @@
     def one_unit(unit, step):
         count = counts[unit]
         both = unit_rows(held, unit, count)
-        turned = pltpu.roll(both, HEAD_DIM, 1)
-        value_turned[...] = jnp.where(lane >= HEAD_DIM, turned, 0.0).astype(jnp.bfloat16)
-        grads[unit] = jnp.where(lane >= HEAD_DIM, both, 0.0).astype(jnp.bfloat16)
+        kept[unit] = both.astype(jnp.bfloat16)
+        grad_rows[...] = jnp.where(lane >= HEAD_DIM, both, 0.0).astype(jnp.bfloat16)
         both_t[...] = both.T.astype(jnp.bfloat16)
+        total[...] = jnp.zeros_like(total)
 
         def one_tile(tile, step):
             span = pl.ds(pl.multiple_of(tile * TILE, TILE), TILE)
@@ -412,44 +419,52 @@
             mixed = dot(both_t[0:HEAD_DIM, :], held_weights).astype(jnp.bfloat16)
             mixed = mixed.astype(jnp.float32)
             grad_t = both_t[HEAD_DIM:PAIR, span].astype(jnp.float32)
-            delta = jnp.sum(grad_t * mixed, axis=0, keepdims=True)
-            dweights = dot(value_turned[...], grads[unit, span, :], NT)
-            dscores = (held_weights.astype(jnp.float32) * (dweights - delta)).astype(jnp.bfloat16)
-            out.write(step, dscores)
-            grad_query = dot(keys_t[unit], dscores) * scale
-            held_out[unit, span, :] = jnp.concatenate([mixed, grad_query], axis=0).T
+            deltas[pl.ds(step, 1), :] = jnp.sum(grad_t * mixed, axis=0, keepdims=True)
+            held_out[unit, span, :] = jnp.concatenate([mixed, jnp.zeros_like(mixed)], axis=0).T
+            total[...] += dot(held_weights, grad_rows[span, :])
             return step + 1
 
-        return lax.fori_loop(0, pl.cdiv(count, TILE), one_tile, step)
+        step = lax.fori_loop(0, pl.cdiv(count, TILE), one_tile, step)
+        held_out[unit, 0:CLUSTER, :] = jnp.where(
+            lane < HEAD_DIM, held_out[unit, 0:CLUSTER, :], total[...]
+        )
+        return step
 
     each_unit(plan, counts, one_unit)
     scatter_units(plan_out, table, me[0], held_out, stage, wires_out)
-    out.finish(steps)
-
-
-def keys_kernel(plan, table, me, counts, queries, grads, weights, dscores, *refs):
+
+
+def scores_kernel(plan, table, me, counts, queries, keys_t, kept, deltas, weights, *refs):
     wires_out, refs = refs[: plan.blocks], refs[plan.blocks :]
-    stage, held_out, total, *slots, first_sems, second_sems = refs
+    stage, held_out, total, grad_rows, slots, sems = refs
     steps = tile_steps(plan, counts)
-    tiles = Tiles(dscores, slots[0], first_sems), Tiles(weights, slots[1], second_sems)
-    for source in tiles:
-        source.begin(steps)
+    tiles = Tiles(weights, slots, sems)
+    tiles.begin(steps)
     scale = 1.0 / math.sqrt(HEAD_DIM)
     lane = lax.broadcasted_iota(jnp.int32, (CLUSTER, PAIR), 1)
+
     def one_unit(unit, step):
+        turned = pltpu.roll(kept[unit].astype(jnp.float32), HEAD_DIM, 1)
+        grad_rows[...] = jnp.where(lane < HEAD_DIM, turned, 0.0).astype(jnp.bfloat16)
         total[...] = jnp.zeros_like(total)
 
         def one_tile(tile, step):
             span = pl.ds(pl.multiple_of(tile * TILE, TILE), TILE)
-            total[...] += dot(
-                jnp.concatenate([source.read(step, steps) for source in tiles], axis=1),
-                jnp.concatenate([queries[unit, span, :], grads[unit, span, :]], axis=0),
-            )
+            held_weights = tiles.read(step, steps).astype(jnp.float32)
+            dweights = dot(kept[unit], grad_rows[span, :], NT)
+            delta = deltas[pl.ds(step, 1), :]
+            dscores = (held_weights * (dweights - delta)).astype(jnp.bfloat16)
+            grad_query = dot(keys_t[unit], dscores) * scale
+            held_out[unit, span, :] = jnp.concatenate(
+                [jnp.zeros_like(grad_query), grad_query], axis=0
+            ).T
+            total[...] += dot(dscores, queries[unit, span, :])
             return step + 1
 
         step = lax.fori_loop(0, pl.cdiv(counts[unit], TILE), one_tile, step)
-        factor = jnp.where(lane < HEAD_DIM, scale, 1.0)
-        held_out[unit, 0:CLUSTER, :] = total[...] * factor
+        held_out[unit, 0:CLUSTER, :] = jnp.where(
+            lane < HEAD_DIM, total[...] * scale, held_out[unit, 0:CLUSTER, :]
+        )
         return step
 
     each_unit(plan, counts, one_unit)
@@ -523,16 +538,16 @@
             arrived[index] = lax.ppermute(wires[index], "node", pairs)
         return arrived
 
-    named = jnp.arange(plan.total, dtype=jnp.int32)[:, None] == cluster_ids[None, :]
-    hist = jnp.sum(named, axis=1, dtype=jnp.int32)
     column = lax.axis_index("head").astype(jnp.int32)
 
     cotangents = [cotangent] + [head_swap(cotangent, mask) for mask in (1, 2, 3)]
-    *wires, pos = call(
+    *wires, pos, hist = call(
         pack_first_kernel, plan, "pack_queries_keys",
-        blocks(plan, NOTE) + [((1, rows), jnp.int32)], specs(plan) + [WHOLE],
-        [SCALARS, SCALARS, WHOLE, WHOLE, WHOLE], [starts, ordered], 2 * 10**9,
-        (hist, me, cluster_ids.reshape(1, rows), queries, key_rows),
+        blocks(plan, NOTE) + [((1, rows), jnp.int32), ((plan.total, PAIR), jnp.int32)], specs(plan) + [WHOLE, SCALARS],
+        [SCALARS, WHOLE, WHOLE, WHOLE],
+        [starts, ordered, pltpu.VMEM((plan.total, PAIR), jnp.int32), pltpu.SemaphoreType.DMA],
+        2 * 10**9,
+        (me, cluster_ids.reshape(1, rows), queries, key_rows),
     )
     query_wires = swap(plan, wires)
     wires = call(
@@ -557,23 +572,23 @@
         query_wires, UNIT_LIMIT,
     )
     all_weight = gather_heads(after(out_weight, kept_keys))
-    *first_wires, dscores, kept_grads, counted = call(
-        queries_kernel, (value_plan, first_plan), "attention_and_grad_queries",
-        blocks(first_plan) + [tiles_shape, unit_rows_shape, ((plan.units,), jnp.int32)],
-        specs(first_plan) + [APART, WHOLE, SCALARS],
-        [SCALARS] * 2 + specs(value_plan) + [WHOLE, APART],
-        [stage, held, unit_counts, unit_block, pltpu.VMEM((PAIR, CLUSTER), narrow), held, slots,
-         sems, slots, sems], 10 * 10**9,
-        [table, me] + value_wires + [kept_keys, weights], UNIT_LIMIT,
+    unit_total = pltpu.VMEM((CLUSTER, PAIR), jnp.float32)
+    *first_wires, kept, deltas, counted = call(
+        attention_kernel, (value_plan, first_plan), "attention_and_grad_values",
+        blocks(first_plan)
+        + [unit_rows_shape, ((plan.tiles, TILE), jnp.float32), ((plan.units,), jnp.int32)],
+        specs(first_plan) + [WHOLE, WHOLE, SCALARS],
+        [SCALARS] * 2 + specs(value_plan) + [APART],
+        [stage, held, unit_counts, unit_block, pltpu.VMEM((PAIR, CLUSTER), narrow), held,
+         unit_total, slots, sems], 10 * 10**9,
+        [table, me] + value_wires + [weights], UNIT_LIMIT,
     )
     counted = after(counted, *all_weight[1:3])
     second_wires = call(
-        keys_kernel, second_plan, "grad_keys_and_grad_values",
-        blocks(second_plan), specs(second_plan),
-        [SCALARS, SCALARS, SCALARS, WHOLE, WHOLE, APART, APART],
-        [stage, held, pltpu.VMEM((CLUSTER, PAIR), jnp.float32), slots, slots, sems, sems],
-        10 * 10**9,
-        [table, me, counted, kept_queries, kept_grads, weights, dscores], UNIT_LIMIT,
+        scores_kernel, second_plan, "grad_keys_and_grad_queries",
+        blocks(second_plan), specs(second_plan), [SCALARS] * 3 + [WHOLE] * 4 + [APART],
+        [stage, held, unit_total, unit_block, slots, sems], 10 * 10**9,
+        [table, me, counted, kept_queries, kept_keys, kept, deltas, weights], UNIT_LIMIT,
     )
 
     def unpack(plan, wires, name):
@@ -587,7 +602,7 @@
     first_back = swap(first_plan, first_wires)
     second_back = swap(second_plan, second_wires)
     first_back = [after(first_back[0], second_wires[0])] + first_back[1:]
-    attention, grad_queries = unpack(first_plan, first_back, "unpack_attention_grad_queries")
+    attention, grad_values = unpack(first_plan, first_back, "unpack_attention_grad_values")
     (output,) = call(
         project_kernel, plan, "project", [home_shape], [WHOLE],
         [SCALARS] + [WHOLE] * (2 * HEAD_DEVICES),
@@ -595,7 +610,7 @@
         [column.reshape(1)] + all_weight + gather_heads(attention),
     )
     second_back[0] = after(second_back[0], output)
-    grad_keys, grad_values = unpack(second_plan, second_back, "unpack_grad_keys_grad_values")
+    grad_keys, grad_queries = unpack(second_plan, second_back, "unpack_grad_keys_grad_queries")
     return (output, grad_queries, grad_keys, grad_values)
 
 

time: 168 us -> 160 us (0.952)
  Pallas kernels: 59.7 us -> 54.7 us
    pallas_call x8, Pallas kernels: 59.7 us -> 54.7 us  [call(): pl.pallas_call(functools.partial(kernel, plan), out_shape=shapes, in_spec...]
    all_to_all x2, waiting for transfers between devices: 19.1 us -> 16.2 us  [swap(): lax.all_to_all(wires[0], 'node', split_axis=0, concat_axis=0, tiled=True)]
    ppermute x14, waiting for transfers between devices: 19.5 us -> 21.2 us  [swap(): arrived[index] = lax.ppermute(wires[index], 'node', pairs)]
    unnamed x30 -> x32, local copies, waits for them, and re-layouts: 5.22 us -> 5.31 us
  transfers between devices with their start and end apart: 25 -> 25, of which waited for: 10 -> 10; matrix products, arithmetic and copies ran while one was open for 1% -> 0% of each run, Pallas kernels for 24% -> 26%
where the time goes in v6:
time: 160 us; the launch traced here: 159 us
  waiting for transfers between devices  55.5 us (35%)
  Pallas kernels  54.7 us (34%)
  starting transfers between devices  42.7 us (27%)
  local copies, waits for them, and re-layouts  5.31 us (3%)
    pallas_call x8, Pallas kernels, call(): pl.pallas_call(functools.partial(kernel, plan), out_shape=shapes, in_spec...  54.7 us
    ppermute x14, starting transfers between devices, swap(): arrived[index] = lax.ppermute(wires[index], 'node', pairs)  26.9 us
    ppermute x14, waiting for transfers between devices, swap(): arrived[index] = lax.ppermute(wires[index], 'node', pairs)  21.2 us
    ppermute x9, waiting for transfers between devices, head_swap(): return lax.ppermute(value, 'head', pairs)  18.1 us
    all_to_all x2, waiting for transfers between devices, swap(): lax.all_to_all(wires[0], 'node', split_axis=0, concat_axis=0, tiled=True)  16.2 us
    all_to_all x2, starting transfers between devices, swap(): lax.all_to_all(wires[0], 'node', split_axis=0, concat_axis=0, tiled=True)  8.86 us
    ppermute x9, starting transfers between devices, head_swap(): return lax.ppermute(value, 'head', pairs)  6.86 us
    unnamed x32, local copies, waits for them, and re-layouts  5.31 us
  transfers between devices with their start and end apart: 25, of which 10 were waited for; matrix products, arithmetic and copies ran while one was open for 0% of the time, Pallas kernels for 26%

profile of v6, /device:TPU:0, one launch (start us, length us, event | category | flops | bytes accessed | tf_op | source)
XLA Modules:
  0.0 159.0 jit_solution(2548419232811001438)
XLA Ops:
  0.6 0.5 collective-permute-start
  1.1 2.6 %collective-permute-start.1 = (bf16[192,1024]{1,0:T(8,128)(2,1)}, bf16[192,1024]{1,0:T(8,128)(2,1)S(1)}, u32[]{:S(2)}, u32[]{:S(2)}) collective-permute-start(bf16[192,1024]{1,0:T(8,128)(2,1)} %refs_0_.1), channel_id=1, source_target_pairs={{0,2},{1,3},{2,0},{3,1},{4,6},{5,7},{6,4},{7,5},{8,10},{9,11},{10,... | collective-permute-start | bytes 1179656 | tf_op jit(solution)/shard_map/ppermute | solution.py:525
  3.7 0.1 collective-permute-start.2
  3.8 5.5 %pack_queries_keys.1 = (bf16[656,128]{1,0:T(8,128)(2,1)}, bf16[656,128]{1,0:T(8,128)(2,1)}, bf16[656,128]{1,0:T(8,128)(2,1)}, bf16[656,128]{1,0:T(8,128)(2,1)}, ...) custom-call(s32[1]{0:T(128)} %bitcast.1.me, ...), custom_call_target="tpu_custom_call" | custom-call | flops 2000000000 | bytes 2711552 | tf_op jit(solution)/shard_map/pack_queries_keys/pallas_call | solution.py:482
  9.3 1.8 %collective-permute-start.3 = (bf16[656,128]{1,0:T(8,128)(2,1)}, bf16[656,128]{1,0:T(8,128)(2,1)S(1)}, u32[]{:S(2)}, u32[]{:S(2)}) collective-permute-start(bf16[656,128]{1,0:T(8,128)(2,1)} %get-tuple-element.44), channel_id=1, source_target_pairs={{0,4},{4,0},{8,12},{12,8},{16,20},{20,16},{24,28},{28,24},{1,5},{5... | collective-permute-start | bytes 503816 | tf_op jit(solution)/shard_map/ppermute | solution.py:538
  11.1 3.6 %collective-permute-start.4 = (bf16[656,128]{1,0:T(8,128)(2,1)}, bf16[656,128]{1,0:T(8,128)(2,1)S(1)}, u32[]{:S(2)}, u32[]{:S(2)}) collective-permute-start(bf16[656,128]{1,0:T(8,128)(2,1)} %get-tuple-element.45), channel_id=1, source_target_pairs={{0,28},{4,24},{8,20},{12,16},{16,12},{20,8},{24,4},{28,0},{1,29},{... | collective-permute-start | bytes 503816 | tf_op jit(solution)/shard_map/ppermute | solution.py:538
  14.6 4.4 %collective-permute-done.3.refs_1_ = bf16[656,128]{1,0:T(8,128)(2,1)S(1)} collective-permute-done((bf16[656,128]{1,0:T(8,128)(2,1)}, bf16[656,128]{1,0:T(8,128)(2,1)S(1)}, u32[]{:S(2)}, u32[]{:S(2)}) %collective-permute-start.3) | collective-permute-done | bytes 167968 | tf_op jit(solution)/shard_map/ppermute | solution.py:538
  19.1 3.6 %collective-permute-start.5 = (bf16[656,128]{1,0:T(8,128)(2,1)}, bf16[656,128]{1,0:T(8,128)(2,1)S(1)}, u32[]{:S(2)}, u32[]{:S(2)}) collective-permute-start(bf16[656,128]{1,0:T(8,128)(2,1)} %get-tuple-element.46), channel_id=1, source_target_pairs={{0,24},{4,28},{8,16},{12,20},{16,8},{20,12},{24,0},{28,4},{1,25},{... | collective-permute-start | bytes 503816 | tf_op jit(solution)/shard_map/ppermute | solution.py:538
  22.7 0.0 collective-permute-done.4.refs_2_
  22.7 4.2 %collective-permute-start.6 = (bf16[656,128]{1,0:T(8,128)(2,1)}, bf16[656,128]{1,0:T(8,128)(2,1)S(1)}, u32[]{:S(2)}, u32[]{:S(2)}) collective-permute-start(bf16[656,128]{1,0:T(8,128)(2,1)} %get-tuple-element.47), channel_id=1, source_target_pairs={{0,20},{4,16},{8,28},{12,24},{16,4},{20,0},{24,12},{28,8},{1,21},{... | collective-permute-start | bytes 503816 | tf_op jit(solution)/shard_map/ppermute | solution.py:538
  26.9 0.0 collective-permute-done.refs_1_
  26.9 0.5 collective-permute-start.7
  27.4 0.0 collective-permute-done.1.refs_2_
  27.4 3.6 %collective-permute-start.8 = (bf16[656,128]{1,0:T(8,128)(2,1)}, bf16[656,128]{1,0:T(8,128)(2,1)S(1)}, u32[]{:S(2)}, u32[]{:S(2)}) collective-permute-start(bf16[656,128]{1,0:T(8,128)(2,1)} %get-tuple-element.49), channel_id=1, source_target_pairs={{0,8},{4,12},{8,0},{12,4},{16,24},{20,28},{24,16},{28,20},{1,9},{5... | collective-permute-start | bytes 503816 | tf_op jit(solution)/shard_map/ppermute | solution.py:538
  31.0 0.0 collective-permute-done.2.refs_3_
  31.0 0.0 collective-permute-start.9
  31.0 0.7 copy-done.7
  31.7 5.3 %pack_values_grads.1 = (bf16[640,128]{1,0:T(8,128)(2,1)}, bf16[640,128]{1,0:T(8,128)(2,1)}, bf16[640,128]{1,0:T(8,128)(2,1)}, bf16[640,128]{1,0:T(8,128)(2,1)}, ...) custom-call(s32[16,128]{1,0:T(8,128)} %get-tuple-element.40.hist, ...), custom_call_target="tpu_custom_call" | custom-call | flops 2000000000 | bytes 2621440 | tf_op jit(solution)/shard_map/pack_values_grads/pallas_call | solution.py:482
  37.0 0.0 collective-permute-done.5.refs_3_
  37.0 0.9 collective-permute-start.13
  37.9 4.0 %collective-permute-done.6.refs_4_ = bf16[656,128]{1,0:T(8,128)(2,1)S(1)} collective-permute-done((bf16[656,128]{1,0:T(8,128)(2,1)}, bf16[656,128]{1,0:T(8,128)(2,1)S(1)}, u32[]{:S(2)}, u32[]{:S(2)}) %collective-permute-start.6) | collective-permute-done | bytes 167968 | tf_op jit(solution)/shard_map/ppermute | solution.py:538
  41.9 0.0 collective-permute-start.14
  41.9 1.9 %collective-permute-done.7.refs_5_ = bf16[656,128]{1,0:T(8,128)(2,1)S(1)} collective-permute-done((bf16[656,128]{1,0:T(8,128)(2,1)}, bf16[656,128]{1,0:T(8,128)(2,1)S(1)}, u32[]{:S(2)}, u32[]{:S(2)}) %collective-permute-start.7) | collective-permute-done | bytes 167968 | tf_op jit(solution)/shard_map/ppermute | solution.py:538
  43.8 3.4 %collective-permute-start.15 = (bf16[640,128]{1,0:T(8,128)(2,1)}, bf16[640,128]{1,0:T(8,128)(2,1)S(1)}, u32[]{:S(2)}, u32[]{:S(2)}) collective-permute-start(bf16[640,128]{1,0:T(8,128)(2,1)} %get-tuple-element.56), channel_id=1, source_target_pairs={{0,28},{4,24},{8,20},{12,16},{16,12},{20,8},{24,4},{28,0},{1,29},{... | collective-permute-start | bytes 491528 | tf_op jit(solution)/shard_map/ppermute | solution.py:538
  47.2 0.0 collective-permute-done.8.refs_6_
  47.2 1.3 collective-permute-start.16
  48.5 0.0 collective-permute-done.9.refs_7_
  48.5 0.0 collective-permute-start.17
  48.5 0.0 collective-permute-done.13.refs_1_
  48.5 2.9 %collective-permute-start.18 = (bf16[640,128]{1,0:T(8,128)(2,1)}, bf16[640,128]{1,0:T(8,128)(2,1)S(1)}, u32[]{:S(2)}, u32[]{:S(2)}) collective-permute-start(bf16[640,128]{1,0:T(8,128)(2,1)} %get-tuple-element.59), channel_id=1, source_target_pairs={{0,16},{4,20},{8,24},{12,28},{16,0},{20,4},{24,8},{28,12},{1,17},{... | collective-permute-start | bytes 491528 | tf_op jit(solution)/shard_map/ppermute | solution.py:538
  51.4 0.0 collective-permute-done.14.refs_2_
  51.4 1.2 collective-permute-start.19
  52.6 10.9 %weights.1 = (s32[8,128]{1,0:T(8,128)S(1)}, bf16[6,1024,128]{2,1,0:T(8,128)(2,1)S(1)}, bf16[6,64,1024]{2,1,0:T(8,128)(2,1)S(1)}, bf16[40,1024,256]{2,1,0:T(8,128)(2,1)}) custom-call(bf16[656,128]{1,0:T(8,128)(2,1)S(1)} %copy-done.3, bf16[656,128]{1,0:T(8,128)(2,1)S(1)} %collective-permute-done.3.refs_1_, ...), custom_call_target="tpu_custom_call" | custom-call | flops 10000000000 | bytes 46669824 | tf_op jit(solution)/shard_map/weights/pallas_call | solution.py:482
  63.5 0.0 collective-permute-done.15.refs_3_
  63.5 0.0 collective-permute-done.16.refs_4_
  63.5 9.1 %collective-permute-done.17.refs_5_ = bf16[640,128]{1,0:T(8,128)(2,1)S(1)} collective-permute-done((bf16[640,128]{1,0:T(8,128)(2,1)}, bf16[640,128]{1,0:T(8,128)(2,1)S(1)}, u32[]{:S(2)}, u32[]{:S(2)}) %collective-permute-start.17) | collective-permute-done | bytes 163872 | tf_op jit(solution)/shard_map/ppermute | solution.py:538
  72.7 1.8 %collective-permute-done.18.refs_6_ = bf16[640,128]{1,0:T(8,128)(2,1)S(1)} collective-permute-done((bf16[640,128]{1,0:T(8,128)(2,1)}, bf16[640,128]{1,0:T(8,128)(2,1)S(1)}, u32[]{:S(2)}, u32[]{:S(2)}) %collective-permute-start.18) | collective-permute-done | bytes 163872 | tf_op jit(solution)/shard_map/ppermute | solution.py:538
  74.4 0.0 collective-permute-done.19.refs_7_
  74.4 9.6 %attention_and_grad_values.1 = (bf16[8,640,128]{2,1,0:T(8,128)(2,1)}, bf16[6,1024,128]{2,1,0:T(8,128)(2,1)S(1)}, f32[24,256]{1,0:T(8,128)S(1)}, s32[6]{0:T(128)S(1)}) custom-call(s32[8,128]{1,0:T(8,128)S(1)} %get-tuple-element.53.table, s32[1]{0:T(128)} %bitcast.1.me, bf16[640,128]{1,0:T(8,128)(2,1)S(1)} %copy-done.2, ...), custom_call_target="tpu_custom_call" | custom-call | flops 10000000000 | bytes 5816368 | tf_op jit(solution)/shard_map/attention_and_grad_values/pallas_call | solution.py:482
  84.1 0.0 copy-start.11
  84.1 5.1 %all-to-all-start = ((bf16[8,640,128]{2,1,0:T(8,128)(2,1)}), bf16[8,640,128]{2,1,0:T(8,128)(2,1)}, u32[]{:S(2)}, u32[]{:S(2)}) async-start(bf16[8,640,128]{2,1,0:T(8,128)(2,1)} %get-tuple-element.62), calls=%async_computation | async-start | bytes 2621440 | tf_op jit(solution)/shard_map/all_to_all | solution.py:534
  89.2 0.1 collective-permute-start.10
  89.3 1.6 collective-permute-start.11
  90.9 0.0 collective-permute-done.10.refs_1_
  90.9 7.8 %collective-permute-done.11.refs_2_ = bf16[192,768]{1,0:T(8,128)(2,1)S(1)} collective-permute-done((bf16[192,768]{1,0:T(8,128)(2,1)S(1)}, bf16[192,768]{1,0:T(8,128)(2,1)S(1)}, u32[]{:S(2)}, u32[]{:S(2)}) %collective-permute-start.11) | collective-permute-done | bytes 294944 | tf_op jit(solution)/shard_map/ppermute | solution.py:525
  98.7 0.7 copy-done.13
  99.4 1.1 copy-done.1
  100.6 12.4 %grad_keys_and_grad_queries.1 = bf16[8,640,128]{2,1,0:T(8,128)(2,1)} custom-call(s32[8,128]{1,0:T(8,128)S(1)} %get-tuple-element.53.table, s32[1]{0:T(128)} %bitcast.1.me, s32[6]{0:T(128)S(1)} %get-tuple-element.64.counts, bf16[6,1024,128]{2,1,0:T(8,128)(2,1)S(1)} %get-tuple-element.65.queries, bf16[6,64,1024]{2,1,0:T(8,128)(2,1)S(1)} %copy-done.1, ...), custom_call_target="tpu_custom_call" | custom-call | flops 10000000000 | bytes 2621440 | tf_op jit(solution)/shard_map/grad_keys_and_grad_queries/pallas_call | solution.py:482
  113.0 6.3 %all-to-all-done.refs_0_ = bf16[8,640,128]{2,1,0:T(8,128)(2,1)} async-done(((bf16[8,640,128]{2,1,0:T(8,128)(2,1)}), bf16[8,640,128]{2,1,0:T(8,128)(2,1)}, u32[]{:S(2)}, u32[]{:S(2)}) %all-to-all-start) | async-done | bytes 1310752 | tf_op jit(solution)/shard_map/all_to_all | solution.py:534
  119.3 3.8 %all-to-all-start.1 = ((bf16[8,640,128]{2,1,0:T(8,128)(2,1)}), bf16[8,640,128]{2,1,0:T(8,128)(2,1)S(1)}, u32[]{:S(2)}, u32[]{:S(2)}) async-start(bf16[8,640,128]{2,1,0:T(8,128)(2,1)} %grad_keys_and_grad_queries.1), calls=%async_computation.1 | async-start | bytes 2621440 | tf_op jit(solution)/shard_map/all_to_all | solution.py:534
  123.1 4.0 %unpack_attention_grad_values.1 = (bf16[192,1024]{1,0:T(8,128)(2,1)}, bf16[192,1024]{1,0:T(8,128)(2,1)}) custom-call(s32[16,128]{1,0:T(8,128)} %get-tuple-element.40.hist, s32[1]{0:T(128)} %bitcast.1.me, s32[1,1024]{1,0:T(1,128)} %get-tuple-element.41.pos, bf16[8,640,128]{2,1,0:T(8,128)(2,1)} %all-to-all-done.refs_0_), custom_call_target="tpu_custom_call" | custom-call | flops 2000000000 | bytes 1572864 | tf_op jit(solution)/shard_map/unpack_attention_grad_values/pallas_call | solution.py:482
  127.1 1.5 collective-permute-start.21
  128.6 0.0 collective-permute-start.20
  128.6 8.6 %collective-permute-done.21.refs_6_ = bf16[192,1024]{1,0:T(8,128)(2,1)S(1)} collective-permute-done((bf16[192,1024]{1,0:T(8,128)(2,1)}, bf16[192,1024]{1,0:T(8,128)(2,1)S(1)}, u32[]{:S(2)}, u32[]{:S(2)}) %collective-permute-start.21) | collective-permute-done | bytes 393248 | tf_op jit(solution)/shard_map/ppermute | solution.py:525
  137.2 0.0 collective-permute-start.22
  137.2 0.5 collective-permute-start.12
  137.7 1.6 %collective-permute-done.12.refs_3_ = bf16[192,768]{1,0:T(8,128)(2,1)S(1)} collective-permute-done((bf16[192,768]{1,0:T(8,128)(2,1)S(1)}, bf16[192,768]{1,0:T(8,128)(2,1)S(1)}, u32[]{:S(2)}, u32[]{:S(2)}) %collective-permute-start.12) | collective-permute-done | bytes 294944 | tf_op jit(solution)/shard_map/ppermute | solution.py:525
  139.4 0.7 copy-done.15
  140.1 0.1 copy-done.9
  140.2 0.8 copy-done.10
  141.0 3.1 %project.1 = bf16[192,1024]{1,0:T(8,128)(2,1)} custom-call(s32[1]{0:T(128)} %bitcast.column, bf16[192,768]{1,0:T(8,128)(2,1)} %refs_0_.2, bf16[192,768]{1,0:T(8,128)(2,1)} %copy-done.12, bf16[192,768]{1,0:T(8,128)(2,1)} %copy-done.13, bf16[192,768]{1,0:T(8,128)(2,1)} %copy-done.15, bf16[192,1024]{1,0:T(8,128)(2,1)} %get-tuple-element.69.refs_4_, ...), custom_call_target="tpu_custom_call" | custom-call | flops 1000000000 | bytes 786432 | tf_op jit(solution)/shard_map/project/pallas_call | solution.py:482
  144.1 9.9 %all-to-all-done.1.refs_0_ = bf16[8,640,128]{2,1,0:T(8,128)(2,1)S(1)} async-done(((bf16[8,640,128]{2,1,0:T(8,128)(2,1)}), bf16[8,640,128]{2,1,0:T(8,128)(2,1)S(1)}, u32[]{:S(2)}, u32[]{:S(2)}) %all-to-all-start.1) | async-done | bytes 1310752 | tf_op jit(solution)/shard_map/all_to_all | solution.py:534
  153.9 1.1 copy-done.4
  155.0 4.0 %unpack_grad_keys_grad_queries.1 = (bf16[192,1024]{1,0:T(8,128)(2,1)}, bf16[192,1024]{1,0:T(8,128)(2,1)}) custom-call(s32[16,128]{1,0:T(8,128)} %get-tuple-element.40.hist, s32[1]{0:T(128)} %bitcast.1.me, s32[1,1024]{1,0:T(1,128)} %get-tuple-element.41.pos, bf16[8,640,128]{2,1,0:T(8,128)(2,1)} %copy-done.4), custom_call_target="tpu_custom_call" | custom-call | flops 2000000000 | bytes 1572864 | tf_op jit(solution)/shard_map/unpack_grad_keys_grad_queries/pallas_call | solution.py:482
  (26 shorter events, 0.0 us)
Async XLA Ops:
  0.6 26.3 %collective-permute-start = (bf16[192,1024]{1,0:T(8,128)(2,1)}, bf16[192,1024]{1,0:T(8,128)(2,1)S(1)}, u32[]{:S(2)}, u32[]{:S(2)}) collective-permute-start(bf16[192,1024]{1,0:T(8,128)(2,1)} %refs_0_.1), channel_id=1, source_target_pairs={{0,1},{1,0},{2,3},{3,2},{4,5},{5,4},{6,7},{7,6},{8,9},{9,8},{10,11... | collective-permute-start | bytes 1179656 | tf_op jit(solution)/shard_map/ppermute | solution.py:525
  1.1 26.2 %collective-permute-start.1 = (bf16[192,1024]{1,0:T(8,128)(2,1)}, bf16[192,1024]{1,0:T(8,128)(2,1)S(1)}, u32[]{:S(2)}, u32[]{:S(2)}) collective-permute-start(bf16[192,1024]{1,0:T(8,128)(2,1)} %refs_0_.1), channel_id=1, source_target_pairs={{0,2},{1,3},{2,0},{3,1},{4,6},{5,7},{6,4},{7,5},{8,10},{9,11},{10,... | collective-permute-start | bytes 1179656 | tf_op jit(solution)/shard_map/ppermute | solution.py:525
  3.7 27.3 %collective-permute-start.2 = (bf16[192,1024]{1,0:T(8,128)(2,1)}, bf16[192,1024]{1,0:T(8,128)(2,1)S(1)}, u32[]{:S(2)}, u32[]{:S(2)}) collective-permute-start(bf16[192,1024]{1,0:T(8,128)(2,1)} %refs_0_.1), channel_id=1, source_target_pairs={{0,3},{1,2},{2,1},{3,0},{4,7},{5,6},{6,5},{7,4},{8,11},{9,10},{10,... | collective-permute-start | bytes 1179656 | tf_op jit(solution)/shard_map/ppermute | solution.py:525
  9.3 9.8 %collective-permute-start.3 = (bf16[656,128]{1,0:T(8,128)(2,1)}, bf16[656,128]{1,0:T(8,128)(2,1)S(1)}, u32[]{:S(2)}, u32[]{:S(2)}) collective-permute-start(bf16[656,128]{1,0:T(8,128)(2,1)} %get-tuple-element.44), channel_id=1, source_target_pairs={{0,4},{4,0},{8,12},{12,8},{16,20},{20,16},{24,28},{28,24},{1,5},{5... | collective-permute-start | bytes 503816 | tf_op jit(solution)/shard_map/ppermute | solution.py:538
  11.1 11.6 %collective-permute-start.4 = (bf16[656,128]{1,0:T(8,128)(2,1)}, bf16[656,128]{1,0:T(8,128)(2,1)S(1)}, u32[]{:S(2)}, u32[]{:S(2)}) collective-permute-start(bf16[656,128]{1,0:T(8,128)(2,1)} %get-tuple-element.45), channel_id=1, source_target_pairs={{0,28},{4,24},{8,20},{12,16},{16,12},{20,8},{24,4},{28,0},{1,29},{... | collective-permute-start | bytes 503816 | tf_op jit(solution)/shard_map/ppermute | solution.py:538
  19.1 17.9 %collective-permute-start.5 = (bf16[656,128]{1,0:T(8,128)(2,1)}, bf16[656,128]{1,0:T(8,128)(2,1)S(1)}, u32[]{:S(2)}, u32[]{:S(2)}) collective-permute-start(bf16[656,128]{1,0:T(8,128)(2,1)} %get-tuple-element.46), channel_id=1, source_target_pairs={{0,24},{4,28},{8,16},{12,20},{16,8},{20,12},{24,0},{28,4},{1,25},{... | collective-permute-start | bytes 503816 | tf_op jit(solution)/shard_map/ppermute | solution.py:538
  22.7 19.2 %collective-permute-start.6 = (bf16[656,128]{1,0:T(8,128)(2,1)}, bf16[656,128]{1,0:T(8,128)(2,1)S(1)}, u32[]{:S(2)}, u32[]{:S(2)}) collective-permute-start(bf16[656,128]{1,0:T(8,128)(2,1)} %get-tuple-element.47), channel_id=1, source_target_pairs={{0,20},{4,16},{8,28},{12,24},{16,4},{20,0},{24,12},{28,8},{1,21},{... | collective-permute-start | bytes 503816 | tf_op jit(solution)/shard_map/ppermute | solution.py:538
  26.9 4.1 %copy-start.5 = (bf16[192,1024]{1,0:T(8,128)(2,1)}, bf16[192,1024]{1,0:T(8,128)(2,1)S(1)}, u32[]{:S(2)}) copy-start(bf16[192,1024]{1,0:T(8,128)(2,1)S(1)} %collective-permute-done.refs_1_) | copy-start | bytes 1179652
  26.9 16.9 %collective-permute-start.7 = (bf16[656,128]{1,0:T(8,128)(2,1)}, bf16[656,128]{1,0:T(8,128)(2,1)S(1)}, u32[]{:S(2)}, u32[]{:S(2)}) collective-permute-start(bf16[656,128]{1,0:T(8,128)(2,1)} %get-tuple-element.48), channel_id=1, source_target_pairs={{0,16},{4,20},{8,24},{12,28},{16,0},{20,4},{24,8},{28,12},{1,17},{... | collective-permute-start | bytes 503816 | tf_op jit(solution)/shard_map/ppermute | solution.py:538
  27.4 3.6 %copy-start.6 = (bf16[192,1024]{1,0:T(8,128)(2,1)}, bf16[192,1024]{1,0:T(8,128)(2,1)S(1)}, u32[]{:S(2)}) copy-start(bf16[192,1024]{1,0:T(8,128)(2,1)S(1)} %collective-permute-done.1.refs_2_) | copy-start | bytes 1179652
  27.4 19.8 %collective-permute-start.8 = (bf16[656,128]{1,0:T(8,128)(2,1)}, bf16[656,128]{1,0:T(8,128)(2,1)S(1)}, u32[]{:S(2)}, u32[]{:S(2)}) collective-permute-start(bf16[656,128]{1,0:T(8,128)(2,1)} %get-tuple-element.49), channel_id=1, source_target_pairs={{0,8},{4,12},{8,0},{12,4},{16,24},{20,28},{24,16},{28,20},{1,9},{5... | collective-permute-start | bytes 503816 | tf_op jit(solution)/shard_map/ppermute | solution.py:538
  31.0 0.7 copy-start.7
  31.0 17.5 %collective-permute-start.9 = (bf16[656,128]{1,0:T(8,128)(2,1)}, bf16[656,128]{1,0:T(8,128)(2,1)S(1)}, u32[]{:S(2)}, u32[]{:S(2)}) collective-permute-start(bf16[656,128]{1,0:T(8,128)(2,1)} %get-tuple-element.50), channel_id=1, source_target_pairs={{0,12},{4,8},{8,4},{12,0},{16,28},{20,24},{24,20},{28,16},{1,13},{... | collective-permute-start | bytes 503816 | tf_op jit(solution)/shard_map/ppermute | solution.py:538
  31.7 20.9 %copy-start.3 = (bf16[656,128]{1,0:T(8,128)(2,1)S(1)}, bf16[656,128]{1,0:T(8,128)(2,1)}, u32[]{:S(2)}) copy-start(bf16[656,128]{1,0:T(8,128)(2,1)} %get-tuple-element.43.refs_0_) | copy-start | bytes 503812
  37.0 11.5 %collective-permute-start.13 = (bf16[640,128]{1,0:T(8,128)(2,1)}, bf16[640,128]{1,0:T(8,128)(2,1)S(1)}, u32[]{:S(2)}, u32[]{:S(2)}) collective-permute-start(bf16[640,128]{1,0:T(8,128)(2,1)} %get-tuple-element.54), channel_id=1, source_target_pairs={{0,4},{4,0},{8,12},{12,8},{16,20},{20,16},{24,28},{28,24},{1,5},{5... | collective-permute-start | bytes 491528 | tf_op jit(solution)/shard_map/ppermute | solution.py:538
  41.9 9.5 %collective-permute-start.14 = (bf16[640,128]{1,0:T(8,128)(2,1)}, bf16[640,128]{1,0:T(8,128)(2,1)S(1)}, u32[]{:S(2)}, u32[]{:S(2)}) collective-permute-start(bf16[640,128]{1,0:T(8,128)(2,1)} %get-tuple-element.55), channel_id=1, source_target_pairs={{0,8},{4,12},{8,0},{12,4},{16,24},{20,28},{24,16},{28,20},{1,9},{5... | collective-permute-start | bytes 491528 | tf_op jit(solution)/shard_map/ppermute | solution.py:538
  43.8 19.7 %collective-permute-start.15 = (bf16[640,128]{1,0:T(8,128)(2,1)}, bf16[640,128]{1,0:T(8,128)(2,1)S(1)}, u32[]{:S(2)}, u32[]{:S(2)}) collective-permute-start(bf16[640,128]{1,0:T(8,128)(2,1)} %get-tuple-element.56), channel_id=1, source_target_pairs={{0,28},{4,24},{8,20},{12,16},{16,12},{20,8},{24,4},{28,0},{1,29},{... | collective-permute-start | bytes 491528 | tf_op jit(solution)/shard_map/ppermute | solution.py:538
  47.2 16.3 %collective-permute-start.16 = (bf16[640,128]{1,0:T(8,128)(2,1)}, bf16[640,128]{1,0:T(8,128)(2,1)S(1)}, u32[]{:S(2)}, u32[]{:S(2)}) collective-permute-start(bf16[640,128]{1,0:T(8,128)(2,1)} %get-tuple-element.57), channel_id=1, source_target_pairs={{0,24},{4,28},{8,16},{12,20},{16,8},{20,12},{24,0},{28,4},{1,25},{... | collective-permute-start | bytes 491528 | tf_op jit(solution)/shard_map/ppermute | solution.py:538
  48.5 24.1 %collective-permute-start.17 = (bf16[640,128]{1,0:T(8,128)(2,1)}, bf16[640,128]{1,0:T(8,128)(2,1)S(1)}, u32[]{:S(2)}, u32[]{:S(2)}) collective-permute-start(bf16[640,128]{1,0:T(8,128)(2,1)} %get-tuple-element.58), channel_id=1, source_target_pairs={{0,20},{4,16},{8,28},{12,24},{16,4},{20,0},{24,12},{28,8},{1,21},{... | collective-permute-start | bytes 491528 | tf_op jit(solution)/shard_map/ppermute | solution.py:538
  48.5 25.9 %collective-permute-start.18 = (bf16[640,128]{1,0:T(8,128)(2,1)}, bf16[640,128]{1,0:T(8,128)(2,1)S(1)}, u32[]{:S(2)}, u32[]{:S(2)}) collective-permute-start(bf16[640,128]{1,0:T(8,128)(2,1)} %get-tuple-element.59), channel_id=1, source_target_pairs={{0,16},{4,20},{8,24},{12,28},{16,0},{20,4},{24,8},{28,12},{1,17},{... | collective-permute-start | bytes 491528 | tf_op jit(solution)/shard_map/ppermute | solution.py:538
  51.4 23.0 %copy-start.2 = (bf16[640,128]{1,0:T(8,128)(2,1)S(1)}, bf16[640,128]{1,0:T(8,128)(2,1)}, u32[]{:S(2)}) copy-start(bf16[640,128]{1,0:T(8,128)(2,1)} %get-tuple-element.42.refs_0_) | copy-start | bytes 491524
  51.4 23.0 %collective-permute-start.19 = (bf16[640,128]{1,0:T(8,128)(2,1)}, bf16[640,128]{1,0:T(8,128)(2,1)S(1)}, u32[]{:S(2)}, u32[]{:S(2)}) collective-permute-start(bf16[640,128]{1,0:T(8,128)(2,1)} %get-tuple-element.60), channel_id=1, source_target_pairs={{0,12},{4,8},{8,4},{12,0},{16,28},{20,24},{24,20},{28,16},{1,13},{... | collective-permute-start | bytes 491528 | tf_op jit(solution)/shard_map/ppermute | solution.py:538
  63.5 20.6 %copy-start = (bf16[6,64,1024]{2,1,0:T(8,128)(2,1)}, bf16[6,64,1024]{2,1,0:T(8,128)(2,1)S(1)}, u32[]{:S(2)}) copy-start(bf16[6,64,1024]{2,1,0:T(8,128)(2,1)S(1)} %get-tuple-element.51.keys_t) | copy-start | bytes 2359300
  84.1 5.1 %copy-start.11 = (bf16[192,768]{1,0:T(8,128)(2,1)S(1)}, bf16[192,768]{1,0:T(8,128)(2,1)}, u32[]{:S(2)}) copy-start(bf16[192,768]{1,0:T(8,128)(2,1)} %refs_0_.2) | copy-start | bytes 884740
  84.1 35.2 %all-to-all-start = ((bf16[8,640,128]{2,1,0:T(8,128)(2,1)}), bf16[8,640,128]{2,1,0:T(8,128)(2,1)}, u32[]{:S(2)}, u32[]{:S(2)}) async-start(bf16[8,640,128]{2,1,0:T(8,128)(2,1)} %get-tuple-element.62), calls=%async_computation | async-start | bytes 2621440 | tf_op jit(solution)/shard_map/all_to_all | solution.py:534
  89.2 1.7 %collective-permute-start.10 = (bf16[192,768]{1,0:T(8,128)(2,1)S(1)}, bf16[192,768]{1,0:T(8,128)(2,1)S(1)}, u32[]{:S(2)}, u32[]{:S(2)}) collective-permute-start(bf16[192,768]{1,0:T(8,128)(2,1)S(1)} %copy-done.11), channel_id=1, source_target_pairs={{0,1},{1,0},{2,3},{3,2},{4,5},{5,4},{6,7},{7,6},{8,9},{9,8},{10,11... | collective-permute-start | bytes 884744 | tf_op jit(solution)/shard_map/ppermute | solution.py:525
  89.3 9.4 %collective-permute-start.11 = (bf16[192,768]{1,0:T(8,128)(2,1)S(1)}, bf16[192,768]{1,0:T(8,128)(2,1)S(1)}, u32[]{:S(2)}, u32[]{:S(2)}) collective-permute-start(bf16[192,768]{1,0:T(8,128)(2,1)S(1)} %copy-done.11), channel_id=1, source_target_pairs={{0,2},{1,3},{2,0},{3,1},{4,6},{5,7},{6,4},{7,5},{8,10},{9,11},{10,... | collective-permute-start | bytes 884744 | tf_op jit(solution)/shard_map/ppermute | solution.py:525
  90.9 7.8 %copy-start.12 = (bf16[192,768]{1,0:T(8,128)(2,1)}, bf16[192,768]{1,0:T(8,128)(2,1)S(1)}, u32[]{:S(2)}) copy-start(bf16[192,768]{1,0:T(8,128)(2,1)S(1)} %collective-permute-done.10.refs_1_) | copy-start | bytes 884740
  98.7 0.7 copy-start.13
  99.4 1.1 copy-start.1
  119.3 34.6 %all-to-all-start.1 = ((bf16[8,640,128]{2,1,0:T(8,128)(2,1)}), bf16[8,640,128]{2,1,0:T(8,128)(2,1)S(1)}, u32[]{:S(2)}, u32[]{:S(2)}) async-start(bf16[8,640,128]{2,1,0:T(8,128)(2,1)} %grad_keys_and_grad_queries.1), calls=%async_computation.1 | async-start | bytes 2621440 | tf_op jit(solution)/shard_map/all_to_all | solution.py:534
  123.0 14.2 %copy-start.14 = (bf16[192,768]{1,0:T(8,128)(2,1)S(1)}, bf16[192,768]{1,0:T(8,128)(2,1)}, u32[]{:S(2)}) copy-start(bf16[192,768]{1,0:T(8,128)(2,1)} %copy-done.13) | copy-start | bytes 884740
  127.1 10.1 %collective-permute-start.21 = (bf16[192,1024]{1,0:T(8,128)(2,1)}, bf16[192,1024]{1,0:T(8,128)(2,1)S(1)}, u32[]{:S(2)}, u32[]{:S(2)}) collective-permute-start(bf16[192,1024]{1,0:T(8,128)(2,1)} %get-tuple-element.69.refs_4_), channel_id=1, source_target_pairs={{0,2},{1,3},{2,0},{3,1},{4,6},{5,7},{6,4},{7,5},{8,10},{9,11},{10,... | collective-permute-start | bytes 1179656 | tf_op jit(solution)/shard_map/ppermute | solution.py:525
  128.6 10.8 %collective-permute-start.20 = (bf16[192,1024]{1,0:T(8,128)(2,1)}, bf16[192,1024]{1,0:T(8,128)(2,1)S(1)}, u32[]{:S(2)}, u32[]{:S(2)}) collective-permute-start(bf16[192,1024]{1,0:T(8,128)(2,1)} %get-tuple-element.69.refs_4_), channel_id=1, source_target_pairs={{0,1},{1,0},{2,3},{3,2},{4,5},{5,4},{6,7},{7,6},{8,9},{9,8},{10,11... | collective-permute-start | bytes 1179656 | tf_op jit(solution)/shard_map/ppermute | solution.py:525
  137.2 2.2 %copy-start.8 = (bf16[192,1024]{1,0:T(8,128)(2,1)}, bf16[192,1024]{1,0:T(8,128)(2,1)S(1)}, u32[]{:S(2)}) copy-start(bf16[192,1024]{1,0:T(8,128)(2,1)S(1)} %collective-permute-done.21.refs_6_) | copy-start | bytes 1179652
  137.2 2.2 %collective-permute-start.22 = (bf16[192,1024]{1,0:T(8,128)(2,1)S(1)}, bf16[192,1024]{1,0:T(8,128)(2,1)S(1)}, u32[]{:S(2)}, u32[]{:S(2)}) collective-permute-start(bf16[192,1024]{1,0:T(8,128)(2,1)S(1)} %collective-permute-done.21.refs_6_), channel_id=1, source_target_pairs={{0,1},{1,0},{2,3},{3,2},{4,5},{5,4},{6,7},{7,6},{8,9},{9,8},{10,11... | collective-permute-start | bytes 1179656 | tf_op jit(solution)/shard_map/ppermute | solution.py:525
  137.2 2.1 %collective-permute-start.12 = (bf16[192,768]{1,0:T(8,128)(2,1)S(1)}, bf16[192,768]{1,0:T(8,128)(2,1)S(1)}, u32[]{:S(2)}, u32[]{:S(2)}) collective-permute-start(bf16[192,768]{1,0:T(8,128)(2,1)S(1)} %copy-done.14), channel_id=1, source_target_pairs={{0,1},{1,0},{2,3},{3,2},{4,5},{5,4},{6,7},{7,6},{8,9},{9,8},{10,11... | collective-permute-start | bytes 884744 | tf_op jit(solution)/shard_map/ppermute | solution.py:525
  139.4 0.7 copy-start.15
  139.4 0.8 copy-start.9
  140.2 0.8 copy-start.10
  153.9 1.1 copy-start.4
